TPU v7x, 32 devices: a whole 2x2x4 slice. The times are simulated.
32 devices in a mesh: tm: 16 (over z, y, x), panel: 2 (over core).
Axes of the slice: x: 2, y: 2, z: 4, core: 2. Of those that a mesh axis runs over, the one named last changes fastest.
Arguments:
- factor_inverse: float32 [16, 768, 768], P('tm', None, 'panel'), may hold values from -1 to 1, as said below
- coupling: float32 [16, 768, 768], P('tm', None, 'panel'), may hold values from -1 to 1
- sigma_after: float32 [768, 768], replicated, may hold values from -1 to 3, as said below
Outputs:
- marginal_cov: float32 [16, 768, 768], P('tm', None, 'panel')
- propagator: bfloat16 [16, 768, 768], P('tm', None, 'panel')
Inputs may be any that keep to these rules, and one draw needn't show every extreme that they name: `factor_inverse`: factor_inverse_t is lower triangular with a positive diagonal. sigma_after is symmetric.
All inputs are finite; a program needn't handle non-finite values.
Results may differ from a plain program's by a relative error of at most 0.007.
The roundings to bfloat16 on the way count: a program that leaves them out, or rounds other values in their place, can miss the bound.
Values may be sent and summed in bfloat16 or wider, within the bound.
No kernel may reach another device: no remote copies, remote signals or barrier semaphores. Data moves between devices by JAX's collectives and lax.ppermute only.
A program may use at most 64 MiB of HBM per device.

v0:
```python
import functools

import jax
import jax.numpy as jnp
from jax import lax
from jax.experimental import pallas as pl
from jax.experimental.pallas import tpu as pltpu
from jax.sharding import PartitionSpec as P

BF = jnp.bfloat16
F32 = jnp.float32
GROUP = 4
BLOCK = 128
ANY = pl.BlockSpec(memory_space=pl.ANY)
VMEM = pl.BlockSpec(memory_space=pltpu.VMEM)
MIB = 1 << 20


def mm(a, b):
    return jnp.dot(a, b, preferred_element_type=F32)


def mm_t(a, b):
    return lax.dot_general(a, b, (((0,), (0,)), ((), ())), preferred_element_type=F32)


def whole(ref):
    return jnp.concatenate([ref[p] for p in range(ref.shape[0])], axis=1)


def put(ref, value):
    width = ref.shape[2]
    for p in range(ref.shape[0]):
        ref[p] = value[:, p * width : (p + 1) * width].astype(ref.dtype)


def where_am_i():
    t = lax.axis_index("tm")
    return t // GROUP, lax.rem(t, GROUP), lax.axis_index("panel")


def run(copies):
    for c in copies:
        c.start()
    for c in copies:
        c.wait()


def copy_all(pairs, sems):
    return [pltpu.make_async_copy(s, d, sems.at[i]) for i, (s, d) in enumerate(pairs)]


def panel_pairs(pieces, dst, q):
    n = len(pieces)
    return [(piece, dst.at[lax.rem(q + r, n)]) for r, piece in enumerate(pieces)]


def group_start(blocks, dst, sems, lo, q):
    own, first, second, diag = blocks
    n = len(own)
    for r in range(n):
        p = lax.rem(q + r, n)
        even = 1 - lax.rem(p, 2)
        for mask, piece in ((3, diag[r]), (1 + even, first[r]), (2 - even, second[r]), (0, own[r])):
            slot = jnp.bitwise_xor(lo, mask)
            pltpu.make_async_copy(piece, dst.at[slot, p], sems.at[slot, p]).start()


def group_wait(own, dst, sems, *slots):
    for slot in slots:
        for p in range(len(own)):
            pltpu.make_async_copy(own[p], dst.at[slot, p], sems.at[slot, p]).wait()


def packs(n, w):
    return n == 2 and w % BLOCK == 0


def packed_shape(n, nb, w):
    if not packs(n, w):
        return nb, w
    k = w // BLOCK
    return (k * (k + 1) // 2 + (k * k + 1) // 2) * BLOCK, BLOCK


def triangle(k):
    return [(i, j) for i in range(k) for j in range(i + 1)]


def halves(k):
    every = [(a, b) for a in range(k) for b in range(k)]
    half = (k * k + 1) // 2
    return every[:half], every[k * k - half :]


def pack(panel, out, q, n):
    nb, w = panel.shape
    if not packs(n, w):
        out[...] = panel[...].astype(BF)
        return
    k = w // BLOCK
    at = 0
    for i, j in triangle(k):
        rows = pl.ds(pl.multiple_of(q * w + i * BLOCK, BLOCK), BLOCK)
        out[at : at + BLOCK, :] = panel[rows, j * BLOCK : (j + 1) * BLOCK].astype(BF)
        at += BLOCK
    for side, blocks in enumerate(halves(k)):

        @pl.when(q == side)
        def _():
            to = at
            for a, b in blocks:
                i, j = (b, a) if side else (w // BLOCK + a, b)
                value = panel[i * BLOCK : (i + 1) * BLOCK, j * BLOCK : (j + 1) * BLOCK]
                out[to : to + BLOCK, :] = value.astype(BF)
                to += BLOCK


def unpack(src, dst, n):
    nb = dst.shape[0]
    w = nb // n
    if not packs(n, w):
        dst[...] = whole(src)
        return
    k = w // BLOCK

    def both(block, i, j):
        dst[i * BLOCK : (i + 1) * BLOCK, j * BLOCK : (j + 1) * BLOCK] = block
        if i != j:
            dst[j * BLOCK : (j + 1) * BLOCK, i * BLOCK : (i + 1) * BLOCK] = block.T

    seen = set()
    for p in range(n):
        at = 0
        for i, j in triangle(k):
            both(src[p, at : at + BLOCK, :], p * k + i, p * k + j)
            at += BLOCK
        for a, b in halves(k)[p]:
            if (a, b) not in seen:
                i, j = (b, k + a) if p else (k + a, b)
                both(src[p, at : at + BLOCK, :], i, j)
            seen.add((a, b))
            at += BLOCK


def panel_of(matrix, q, n, use):
    w = matrix.shape[1] // n
    for p in range(n):

        @pl.when(q == p)
        def _():
            use(matrix[:, p * w : (p + 1) * w])


def split(refs, *counts):
    out, at = [], 0
    for c in counts:
        out.append(refs[at : at + c])
        at += c
    return out


def call(kernel, ins, in_specs, outs, scratch, flops, aliases=None):
    size = sum(a.size * a.dtype.itemsize for a in ins) + sum(
        o.size * o.dtype.itemsize for o in outs
    )
    return pl.pallas_call(
        kernel,
        in_specs=in_specs,
        out_specs=[VMEM] * len(outs),
        out_shape=outs,
        scratch_shapes=scratch,
        input_output_aliases=aliases or {},
        compiler_params=pltpu.CompilerParams(vmem_limit_bytes=24 * MIB),
        cost_estimate=pl.CostEstimate(flops=flops, bytes_accessed=size, transcendentals=0),
    )(*ins)


def base_kernel(n, *refs):
    factor, sigma, f_parts, c_parts, (base, base_bf), (f_all, c_all, sig, sems) = split(
        refs, 1, 1, n, n, 2, 4
    )
    factor, sigma = factor[0], sigma[0]
    hi, lo, q = where_am_i()
    width = factor.shape[1]
    run(copy_all(panel_pairs(f_parts, f_all, q), sems))
    own = factor[...]
    high = own.astype(BF)
    low = (own - high.astype(F32)).astype(BF)
    for p in range(n):
        part = f_all[p]
        base[p * width : (p + 1) * width, :] = mm_t(part, high) + mm_t(part, low)

    @pl.when(lax.axis_index("tm") == lax.axis_size("tm") - 1)
    def _():
        run(copy_all(panel_pairs(c_parts, c_all, q) + [(sigma, sig)], sems))
        s = sig[...]
        s_high = s.astype(BF)
        s_low = (s - s_high.astype(F32)).astype(BF)
        c_own = c_all[q]
        mid = mm(s_high, c_own) + mm(s_low, c_own)
        mid_high = mid.astype(BF)
        mid_low = (mid - mid_high.astype(F32)).astype(BF)
        c_full = whole(c_all)
        base[...] += mm_t(c_full, mid_high) + mm_t(c_full, mid_low)

    pack(base, base_bf, q, n)


def pair_product(c, member):
    odd = lax.rem(member, 2)
    return mm(whole(c.at[member - odd + 1]), whole(c.at[member - odd])).astype(BF)


def near_comp_kernel(n, *refs):
    own, first, second, (c, c_t, pair), (sems,) = split(refs, n, n, n, 3, 1)
    hi, lo, q = where_am_i()
    pairs = []
    for r in range(n):
        p = lax.rem(q + r, n)
        even = 1 - lax.rem(p, 2)
        for mask, piece in ((0, own[r]), (1 + even, first[r]), (2 - even, second[r])):
            pairs.append((piece, c.at[jnp.bitwise_xor(lo, mask), p]))
    run(copy_all(pairs, sems))
    pair[...] = pair_product(c, lo)
    for mask in range(GROUP - 1):
        slot = jnp.bitwise_xor(lo, mask)
        c_t[slot] = whole(c.at[slot]).T


def group_comp_kernel(n, *refs):
    (c, pair), diag, outs, (other, sems) = split(refs, 2, n, 5, 2)
    c_out, c01, c23, agg_cols, share = outs
    hi, lo, q = where_am_i()
    far = jnp.bitwise_xor(lo, 3)
    run(copy_all(panel_pairs(diag, c_out.at[far], q), sems))
    other[...] = pair_product(c_out, far)

    @pl.when(lo < 2)
    def _():
        put(c01, pair[...])
        c23[...] = other[...]

    @pl.when(lo >= 2)
    def _():
        put(c01, other[...])
        c23[...] = pair[...]

    agg_cols[...] = mm(c23[...], c01[q]).astype(BF)
    share[...] = agg_cols[quarter_rows(lo, agg_cols.shape[0]), :]


def turn_comp_kernel(c, c_t, c01, c_t_out, c01_t):
    hi, lo, q = where_am_i()
    far = jnp.bitwise_xor(lo, 3)
    c_t_out[far] = whole(c.at[far]).T
    c01_t[...] = whole(c01).T


def tail_comp_kernel(c, c01, c23, agg, agg_t, mine, mine_t):
    hi, lo, q = where_am_i()
    put(agg, mm(c23[...], whole(c01)))
    agg_t[...] = whole(agg).T

    @pl.when(lo == 0)
    def _():
        mine[...] = agg[...]

    @pl.when(lo == 1)
    def _():
        put(mine, mm(c23[...], whole(c.at[1])))

    @pl.when(lo == 2)
    def _():
        put(mine, c23[...])

    @pl.when(lo == 3)
    def _():
        mine[...] = c[3]

    mine_t[...] = whole(mine).T


def sandwich(cov, comp, comp_t):
    return mm(comp_t, mm(cov, comp).astype(BF))


def group_cov_kernel(n, *refs):
    ins, *blocks, outs, scratch = split(refs, 5, n, n, n, n, 4, 3)
    base, c, c_t, c01, c01_t = ins
    agg, agg_bf, s3, s23 = outs
    sent, s, sems = scratch
    hi, lo, q = where_am_i()
    group_start(blocks, sent, sems, lo, q)
    group_wait(blocks[0], sent, sems, 3, 2, 1, 0)
    unpack(sent.at[3], s3, n)
    for k in range(GROUP - 1):
        unpack(sent.at[k], s.at[k], n)
    mid = mm(s3[...], whole(c.at[2])).astype(BF)
    s23[...] = (s[2].astype(F32) + mm(c_t[2], mid)).astype(BF)
    w = agg.shape[1]
    first = s[0, :, :w]
    for p in range(1, n):
        first = jnp.where(q == p, s[0, :, p * w : (p + 1) * w], first)
    total = jnp.where(lo == 0, base[...], first.astype(F32))
    total += sandwich(s[1], c[0, q], c_t[0])
    agg[...] = total + sandwich(s23[...], c01[q], c01_t[...])
    pack(agg, agg_bf, q, n)


def group_mine_kernel(base, agg, s3, s23, c, c_t, mine):
    hi, lo, q = where_am_i()

    @pl.when(lo == 0)
    def _():
        mine[...] = agg[...]

    @pl.when(lo == 1)
    def _():
        mine[...] = base[...] + sandwich(s23[...], c[1, q], c_t[1])

    @pl.when(lo == 2)
    def _():
        mine[...] = base[...] + sandwich(s3[...], c[2, q], c_t[2])

    @pl.when(lo == 3)
    def _():
        mine[...] = base[...]


def is_lower(bit):
    hi, lo, q = where_am_i()
    return lax.rem(hi // (1 << bit), 2) == 0


def panel_rows(q, r, n, w):
    return pl.ds(pl.multiple_of(lax.rem(q + r, n) * w, w), w)


def quarter_rows(place, nb):
    rows = nb // GROUP
    return pl.ds(pl.multiple_of(place * rows, rows), rows)


def times(pieces, right, q):
    n = len(pieces)
    w = right.shape[0] // n
    return sum(mm(x[...], right[panel_rows(q, r, n, w), :]) for r, x in enumerate(pieces))


def place_whole(pieces, dst, q):
    for r, piece in enumerate(pieces):
        dst[lax.rem(q + r, len(pieces))] = piece[...]


def join_kernel(*refs):
    *quarters, out = refs
    hi, lo, q = where_am_i()
    for k, piece in enumerate(quarters):
        out[quarter_rows(jnp.bitwise_xor(lo, k), out.shape[0]), :] = piece[...]


def select_kernel(*refs):
    *got, out = refs
    hi, lo, q = where_am_i()
    d = len(got)
    for k, piece in enumerate(got):

        @pl.when(lax.rem(hi, d) == d - 1 - k)
        def _():
            out[...] = piece[...]


def share_comp_kernel(n, agg_cols, *refs):
    quarters, (share,) = split(refs, n, 1)
    hi, lo, q = where_am_i()
    share[...] = times(quarters, agg_cols, q).astype(BF)


def pair_comp_kernel(n, agg, *refs):
    parts, (new_agg, new_agg_t, new_cols, share) = split(refs, n, 4)
    hi, lo, q = where_am_i()
    for p in range(n):
        new_agg[p] = times(parts, agg.at[p], q).astype(BF)
    new_agg_t[...] = whole(new_agg).T
    new_cols[...] = new_agg[q]
    share[...] = new_cols[quarter_rows(lo, new_cols.shape[0]), :]


def mine_comp_kernel(n, bit, *refs):
    (mine, mine_t), parts, (new_mine, new_mine_t) = split(refs, 2, n, 2)
    hi, lo, q = where_am_i()
    lower = is_lower(bit)

    @pl.when(lower)
    def _():
        for p in range(n):
            new_mine[p] = times(parts, mine.at[p], q).astype(BF)
        new_mine_t[...] = whole(new_mine).T

    @pl.when(jnp.logical_not(lower))
    def _():
        new_mine[...] = mine[...]
        new_mine_t[...] = mine_t[...]


def last_comp_kernel(n, bit, *refs):
    (mine,), parts, (out,) = split(refs, 1, n, 1)
    hi, lo, q = where_am_i()
    lower = is_lower(bit)

    @pl.when(lower)
    def _():
        out[0] = times(parts, mine.at[q], q).astype(BF)

    @pl.when(jnp.logical_not(lower))
    def _():
        out[0] = mine[q]


def pair_cov_kernel(n, to_last, agg, agg_cols, agg_t, *refs):
    parts, outs, (sent, total, packed) = split(refs, n, 2 if to_last else 4, 3)
    share, right = outs[:2]
    hi, lo, q = where_am_i()
    place_whole(parts, sent, q)
    unpack(sent, right, n)
    total[...] = agg[...] + sandwich(right[...], agg_cols[...], agg_t[...])
    pack(total, packed, q, n)
    share[...] = packed[quarter_rows(lo, packed.shape[0]), :]
    if not to_last:
        outs[2][...] = total[...]
        outs[3][...] = packed[...]


def mine_cov_kernel(n, bit, cov, mine, mine_t, right, out):
    hi, lo, q = where_am_i()
    lower = is_lower(bit)

    @pl.when(lower)
    def _():
        out[...] = cov[...] + sandwich(right[...], mine[q], mine_t[...])

    @pl.when(jnp.logical_not(lower))
    def _():
        out[...] = cov[...]


def last_cov_kernel(n, bit, *refs):
    (cov, mine, mine_t), parts, (out,), (sent, right) = split(refs, 3, n, 1, 2)
    hi, lo, q = where_am_i()
    lower = is_lower(bit)

    @pl.when(lower)
    def _():
        place_whole(parts, sent, q)
        unpack(sent, right, n)
        out[0] = cov[...] + sandwich(right[...], mine[q], mine_t[...])

    @pl.when(jnp.logical_not(lower))
    def _():
        out[0] = cov[...]


def over_panels(x):
    n = lax.axis_size("panel")
    return [x] + [
        lax.ppermute(x, "panel", [((i + r) % n, i) for i in range(n)]) for r in range(1, n)
    ]


def swap(value, odd_mask, even_mask):
    steps, n = lax.axis_size("tm"), lax.axis_size("panel")
    pairs = []
    for t in range(steps):
        for q in range(n):
            mask = odd_mask if q % 2 else even_mask
            pairs.append((t * n + q, (t ^ mask) * n + q))
    return lax.ppermute(value, ("tm", "panel"), pairs)


def across(x, bit):
    steps = lax.axis_size("tm")
    d = 1 << bit
    got = []
    for back in range(1, d + 1):
        pairs = [
            (g * GROUP + k, (g - back) * GROUP + k)
            for g in range(d, steps // GROUP, 2 * d)
            for k in range(GROUP)
        ]
        got.append(lax.ppermute(x, "tm", pairs))
    if d == 1:
        return got[0]
    return call(select_kernel, got, [VMEM] * d, [jax.ShapeDtypeStruct(x.shape, x.dtype)], [], 0)[0]


def in_group(x):
    return [x] + [swap(x, mask, mask) for mask in range(1, GROUP)]


def joined(quarters):
    rows, lanes = quarters[0].shape
    whole_panel = jax.ShapeDtypeStruct((rows * GROUP, lanes), BF)
    return call(join_kernel, quarters, [VMEM] * GROUP, [whole_panel], [], 0)[0]


def after(x, *others):
    return lax.optimization_barrier((x, *others))[0]


def shards(factor_inverse, coupling, sigma_after):
    steps = lax.axis_size("tm")
    n = lax.axis_size("panel")
    nb, w = factor_inverse.shape[1:]
    levels = (steps // GROUP - 1).bit_length()
    panel_bf = jax.ShapeDtypeStruct((nb, w), BF)
    panel_f32 = jax.ShapeDtypeStruct((nb, w), F32)
    full_bf = jax.ShapeDtypeStruct((n, nb, w), BF)
    square_bf = jax.ShapeDtypeStruct((nb, nb), BF)
    group_bf = jax.ShapeDtypeStruct((GROUP, n, nb, w), BF)
    turned_bf = jax.ShapeDtypeStruct((GROUP, nb, nb), BF)
    share_bf = jax.ShapeDtypeStruct((nb // GROUP, w), BF)
    full_scratch = pltpu.VMEM((n, nb, w), BF)
    rows, lanes = packed_shape(n, nb, w)
    packed_bf = jax.ShapeDtypeStruct((rows, lanes), BF)
    packed_share = jax.ShapeDtypeStruct((rows // GROUP, lanes), BF)
    packed_scratch = pltpu.VMEM((n, rows, lanes), BF)
    square_scratch = pltpu.VMEM((nb, nb), BF)
    one = 2 * nb * nb * w
    sems = pltpu.SemaphoreType.DMA

    comp = coupling[0].astype(BF)
    c_first = swap(comp, 1, 2)
    c_second = swap(comp, 2, 1)
    factor = after(factor_inverse[0], comp)
    f_parts = over_panels(factor.astype(BF))
    c_own = over_panels(comp)
    base, base_bf = call(
        functools.partial(base_kernel, n),
        [factor, sigma_after, *f_parts, *c_own],
        [VMEM] + [ANY] * (1 + 2 * n),
        [panel_f32, packed_bf],
        [full_scratch, full_scratch, pltpu.VMEM((nb, n * w), F32), sems((n + 1,))],
        2 * one,
    )
    s_first = swap(base_bf, 1, 2)
    c_diag = swap(c_first, 2, 1)
    s_second = swap(base_bf, 2, 1)
    s_diag = swap(s_first, 2, 1)
    c_near = [p for v in (c_first, c_second) for p in over_panels(v)]
    c_all, c_t, pair = call(
        functools.partial(near_comp_kernel, n),
        c_own + c_near,
        [ANY] * (3 * n),
        [group_bf, turned_bf, square_bf],
        [sems((3 * n,))],
        n * one,
    )
    c_all, c01, c23, agg_cols, c_share = call(
        functools.partial(group_comp_kernel, n),
        [c_all, pair, *over_panels(after(c_diag, s_first, pair))],
        [VMEM] * 2 + [ANY] * n,
        [group_bf, full_bf, square_bf, panel_bf, share_bf],
        [square_scratch, sems((n,))],
        2 * n * one,
        {0: 0},
    )
    c_far = across(c_share, 0)
    c_t, c01_t = call(
        turn_comp_kernel, [c_all, c_t, c01], [VMEM] * 3, [turned_bf, square_bf], [], 0, {1: 0}
    )
    s_second, s_diag = after(s_second, c_share), after(s_diag, c_far)
    s_pieces = [p for v in (base_bf, s_first, s_second, s_diag) for p in over_panels(v)]
    agg, agg_bf, s3, s23 = call(
        functools.partial(group_cov_kernel, n),
        [base, c_all, c_t, c01, c01_t, *s_pieces],
        [VMEM] * 5 + [ANY] * (GROUP * n),
        [panel_f32, packed_bf, square_bf, square_bf],
        [
            pltpu.VMEM((GROUP, n, rows, lanes), BF),
            pltpu.VMEM((GROUP - 1, nb, nb), BF),
            sems((GROUP, n)),
        ],
        (2 * n + 4) * one,
    )
    agg_c, agg_t, mine, mine_t = call(
        tail_comp_kernel,
        [c_all, c01, after(c23, agg_bf)],
        [VMEM] * 3,
        [full_bf, square_bf, full_bf, square_bf],
        [],
        2 * n * one,
    )
    (cov,) = call(
        group_mine_kernel,
        [base, agg, s3, s23, c_all, c_t],
        [VMEM] * 6,
        [panel_f32],
        [],
        2 * one,
    )
    out_cov = jax.ShapeDtypeStruct((1, nb, w), F32)
    out_comp = jax.ShapeDtypeStruct((1, nb, w), BF)
    sum_scratch = pltpu.VMEM((nb, w), F32)
    s_got = across(agg_bf, 0)
    for bit in range(levels):
        to_last = bit + 2 == levels
        if bit + 1 == levels:
            c_parts = over_panels(joined(in_group(c_far)))
            (prop,) = call(
                functools.partial(last_comp_kernel, n, bit),
                [mine, *c_parts],
                [VMEM] * (1 + n),
                [out_comp],
                [],
                one,
            )
            if bit:
                s_got = joined(in_group(after(s_far, prop, cov)))
            s_parts = over_panels(s_got)
            (cov,) = call(
                functools.partial(last_cov_kernel, n, bit),
                [cov, mine, mine_t, *s_parts],
                [VMEM] * (3 + n),
                [out_cov],
                [packed_scratch, square_scratch],
                2 * one,
            )
            break
        if to_last:
            (c_send,) = call(
                functools.partial(share_comp_kernel, n),
                [agg_cols, *over_panels(c_far)],
                [VMEM] * (1 + n),
                [share_bf],
                [],
                one // 4,
            )
            c_blocks = in_group(after(c_far, agg_bf))
            c_parts = over_panels(joined(c_blocks))
        else:
            c_blocks = in_group(c_far)
            c_parts = over_panels(joined(c_blocks))
            new_agg_c, new_agg_t, new_cols, c_send = call(
                functools.partial(pair_comp_kernel, n),
                [agg_c, *c_parts],
                [VMEM] * (1 + n),
                [full_bf, square_bf, panel_bf, share_bf],
                [],
                n * one,
            )
        c_far = after(across(c_send, bit + 1), mine)
        new_mine, new_mine_t = call(
            functools.partial(mine_comp_kernel, n, bit),
            [after(mine, c_send), mine_t, *c_parts],
            [VMEM] * (2 + n),
            [full_bf, square_bf],
            [],
            n * one,
        )
        s_parts = over_panels(after(s_got, mine, cov, *c_blocks[1:]))
        outs = call(
            functools.partial(pair_cov_kernel, n, to_last),
            [agg, agg_cols, agg_t, *s_parts],
            [VMEM] * (3 + n),
            [packed_share, square_bf] + ([] if to_last else [panel_f32, packed_bf]),
            [packed_scratch, sum_scratch, pltpu.VMEM((rows, lanes), BF)],
            2 * one,
        )
        s_send, right = outs[:2]
        s_far = across(s_send, bit + 1)
        (cov,) = call(
            functools.partial(mine_cov_kernel, n, bit),
            [cov, mine, mine_t, right],
            [VMEM] * 4,
            [panel_f32],
            [],
            2 * one,
        )
        if not to_last:
            agg, agg_bf = outs[2:]
            agg_c, agg_t, agg_cols = new_agg_c, new_agg_t, new_cols
        if not to_last:
            s_got = joined(in_group(s_far))
        mine, mine_t = new_mine, new_mine_t
    return cov, prop


def solution(mesh):
    placed = (P("tm", None, "panel"), P("tm", None, "panel"), P())
    return jax.shard_map(
        shards,
        mesh=mesh,
        in_specs=placed,
        out_specs=(P("tm", None, "panel"), P("tm", None, "panel")),
        check_vma=False,
    )
```

profile of v0, /device:TPU:0, one launch (start us, length us, event | category | flops | bytes accessed | tf_op | source)
XLA Modules:
  0.0 100.4 jit_solution(9291048631368025645)
XLA Ops:
  0.6 1.5 %convert_bitcast_fusion.refs_4_.refs_0_ = bf16[768,384]{1,0:T(8,128)(2,1)S(1)} fusion(f32[1,768,384]{2,1,0:T(8,128)} %param.4), kind=kLoop, calls=%fused_computation | loop fusion | flops 294912 | bytes 1769472 | tf_op jit(solution)/shard_map/convert_element_type | solution.py:532
  2.1 3.0 %collective-permute-start.2 = (bf16[768,384]{1,0:T(8,128)(2,1)S(1)}, bf16[768,384]{1,0:T(8,128)(2,1)S(1)}, u32[]{:S(2)}, u32[]{:S(2)}) collective-permute-start(bf16[768,384]{1,0:T(8,128)(2,1)S(1)} %convert_bitcast_fusion.refs_4_.refs_0_), channel_id=1, source_target_pairs={{0,4},{1,3},{2,6},{3,1},{4,0},{5,7},{6,2},{7,5},{8,12},{9,11},{10,... | collective-permute-start | bytes 1769480 | tf_op jit(solution)/shard_map/ppermute | solution.py:478
  5.2 1.5 %collective-permute-start.4 = (bf16[768,384]{1,0:T(8,128)(2,1)S(1)}, bf16[768,384]{1,0:T(8,128)(2,1)S(1)}, u32[]{:S(2)}, u32[]{:S(2)}) collective-permute-start(bf16[768,384]{1,0:T(8,128)(2,1)S(1)} %convert_bitcast_fusion.refs_4_.refs_0_), channel_id=1, source_target_pairs={{0,2},{1,5},{2,0},{3,7},{4,6},{5,1},{6,4},{7,3},{8,10},{9,13},{10,... | collective-permute-start | bytes 1769480 | tf_op jit(solution)/shard_map/ppermute | solution.py:478
  7.3 11.5 %collective-permute-done.2.refs_2_ = bf16[768,384]{1,0:T(8,128)(2,1)S(1)} collective-permute-done((bf16[768,384]{1,0:T(8,128)(2,1)S(1)}, bf16[768,384]{1,0:T(8,128)(2,1)S(1)}, u32[]{:S(2)}, u32[]{:S(2)}) %collective-permute-start.2) | collective-permute-done | bytes 589856 | tf_op jit(solution)/shard_map/ppermute | solution.py:478
  19.3 1.5 %collective-permute-start.6 = (bf16[768,384]{1,0:T(8,128)(2,1)S(1)}, bf16[768,384]{1,0:T(8,128)(2,1)S(1)}, u32[]{:S(2)}, u32[]{:S(2)}) collective-permute-start(bf16[768,384]{1,0:T(8,128)(2,1)S(1)} %collective-permute-done.2.refs_2_), channel_id=1, source_target_pairs={{0,2},{1,5},{2,0},{3,7},{4,6},{5,1},{6,4},{7,3},{8,10},{9,13},{10,... | collective-permute-start | bytes 1769480 | tf_op jit(solution)/shard_map/ppermute | solution.py:478
  20.8 1.7 %shard_map.50 = (f32[768,384]{1,0:T(8,128)S(1)}, bf16[1408,128]{1,0:T(8,128)(2,1)S(1)}) custom-call(f32[768,384]{1,0:T(8,128)S(1)} %bitcast.4, f32[768,768]{1,0:T(8,128)S(1)} %copy-done.1, bf16[768,384]{1,0:T(8,128)(2,1)S(1)} %convert_element_type.10.refs_2_, bf16[768,384]{1,0:T(8,128)(2,1)S(1)} %collective-permute-done.refs_3_, ...), custom_call_target="tpu_custom_call" | custom-call | flops 905969664 | bytes 7438336 | tf_op jit(solution)/shard_map/pallas_call | solution.py:167
  22.6 1.8 %collective-permute-start.7 = (bf16[1408,128]{1,0:T(8,128)(2,1)S(1)}, bf16[1408,128]{1,0:T(8,128)(2,1)S(1)}, u32[]{:S(2)}, u32[]{:S(2)}) collective-permute-start(bf16[1408,128]{1,0:T(8,128)(2,1)S(1)} %get-tuple-element.39.refs_5_), channel_id=1, source_target_pairs={{0,4},{1,3},{2,6},{3,1},{4,0},{5,7},{6,2},{7,5},{8,12},{9,11},{10,... | collective-permute-start | bytes 1081352 | tf_op jit(solution)/shard_map/ppermute | solution.py:478
  24.3 1.9 %shard_map.51 = (bf16[4,2,768,384]{3,2,1,0:T(8,128)(2,1)S(1)}, bf16[4,768,768]{2,1,0:T(8,128)(2,1)S(1)}, bf16[768,768]{1,0:T(8,128)(2,1)S(1)}) custom-call(bf16[768,384]{1,0:T(8,128)(2,1)S(1)} %convert_bitcast_fusion.refs_4_.refs_0_, bf16[768,384]{1,0:T(8,128)(2,1)S(1)} %collective-permute-done.1.refs_5_.refs_1_, ...), custom_call_target="tpu_custom_call" | custom-call | flops 905969664 | bytes 14155776 | tf_op jit(solution)/shard_map/pallas_call | solution.py:167
  26.2 6.6 %collective-permute-done.7.refs_7_ = bf16[1408,128]{1,0:T(8,128)(2,1)S(1)} collective-permute-done((bf16[1408,128]{1,0:T(8,128)(2,1)S(1)}, bf16[1408,128]{1,0:T(8,128)(2,1)S(1)}, u32[]{:S(2)}, u32[]{:S(2)}) %collective-permute-start.7) | collective-permute-done | bytes 360480 | tf_op jit(solution)/shard_map/ppermute | solution.py:478
  33.0 1.6 %collective-permute-start.11 = (bf16[1408,128]{1,0:T(8,128)(2,1)S(1)}, bf16[1408,128]{1,0:T(8,128)(2,1)S(1)}, u32[]{:S(2)}, u32[]{:S(2)}) collective-permute-start(bf16[1408,128]{1,0:T(8,128)(2,1)S(1)} %get-tuple-element.39.refs_5_), channel_id=1, source_target_pairs={{0,2},{1,5},{2,0},{3,7},{4,6},{5,1},{6,4},{7,3},{8,10},{9,13},{10,... | collective-permute-start | bytes 1081352 | tf_op jit(solution)/shard_map/ppermute | solution.py:478
  35.0 2.3 %shard_map.52 = (bf16[4,2,768,384]{3,2,1,0:T(8,128)(2,1)S(1)}, bf16[2,768,384]{2,1,0:T(8,128)(2,1)S(1)}, bf16[768,768]{1,0:T(8,128)(2,1)S(1)}, bf16[768,384]{1,0:T(8,128)(2,1)S(1)}, bf16[192,384]{1,0:T(8,128)(2,1)S(1)}) custom-call(bf16[4,2,768,384]{3,2,1,0:T(8,128)(2,1)S(1)} %get-tuple-element.37.refs_0_, ...), custom_call_target="tpu_custom_call", output_to_operand_aliasing={{0}: (0, {})} | custom-call | flops 1811939328 | bytes 14893056 | tf_op jit(solution)/shard_map/pallas_call | solution.py:167
  37.4 1.3 %collective-permute-start.14 = (bf16[192,384]{1,0:T(8,128)(2,1)S(1)}, bf16[192,384]{1,0:T(8,128)(2,1)S(1)}, u32[]{:S(2)}, u32[]{:S(2)}) collective-permute-start(bf16[192,384]{1,0:T(8,128)(2,1)S(1)} %get-tuple-element.46), channel_id=1, source_target_pairs={{8,0},{10,2},{12,4},{14,6},{24,16},{26,18},{28,20},{30,22},{9,1},{... | collective-permute-start | bytes 442376 | tf_op jit(solution)/shard_map/ppermute | solution.py:491
  40.9 3.4 %collective-permute-done.13.refs_11_ = bf16[1408,128]{1,0:T(8,128)(2,1)S(1)} collective-permute-done((bf16[1408,128]{1,0:T(8,128)(2,1)S(1)}, bf16[1408,128]{1,0:T(8,128)(2,1)S(1)}, u32[]{:S(2)}, u32[]{:S(2)}) %collective-permute-start.13) | collective-permute-done | bytes 360480 | tf_op jit(solution)/shard_map/ppermute | solution.py:478
  44.3 1.6 %collective-permute-done.14.refs_0_ = bf16[192,384]{1,0:T(8,128)(2,1)S(1)} collective-permute-done((bf16[192,384]{1,0:T(8,128)(2,1)S(1)}, bf16[192,384]{1,0:T(8,128)(2,1)S(1)}, u32[]{:S(2)}, u32[]{:S(2)}) %collective-permute-start.14) | collective-permute-done | bytes 147488 | tf_op jit(solution)/shard_map/ppermute | solution.py:491
  48.7 1.5 %collective-permute-start.26 = (bf16[192,384]{1,0:T(8,128)(2,1)S(1)}, bf16[192,384]{1,0:T(8,128)(2,1)S(1)}, u32[]{:S(2)}, u32[]{:S(2)}) collective-permute-start(bf16[192,384]{1,0:T(8,128)(2,1)S(1)} %shard_map.59), channel_id=1, source_target_pairs={{16,0},{18,2},{20,4},{22,6},{17,1},{19,3},{21,5},{23,7}} | collective-permute-start | bytes 442376 | tf_op jit(solution)/shard_map/ppermute | solution.py:491
  50.3 5.9 %shard_map.54 = (f32[768,384]{1,0:T(8,128)S(1)}, bf16[1408,128]{1,0:T(8,128)(2,1)S(1)}, bf16[768,768]{1,0:T(8,128)(2,1)S(1)}, bf16[768,768]{1,0:T(8,128)(2,1)S(1)}) custom-call(f32[768,384]{1,0:T(8,128)S(1)} %get-tuple-element.36.refs_0_.base, bf16[4,2,768,384]{3,2,1,0:T(8,128)(2,1)S(1)} %get-tuple-element.41.c.refs_1_, ...), custom_call_target="tpu_custom_call" | custom-call | flops 3623878656 | bytes 19759104 | tf_op jit(solution)/shard_map/pallas_call | solution.py:167
  57.5 2.1 %collective-permute-done.26.refs_1_ = bf16[192,384]{1,0:T(8,128)(2,1)S(1)} collective-permute-done((bf16[192,384]{1,0:T(8,128)(2,1)S(1)}, bf16[192,384]{1,0:T(8,128)(2,1)S(1)}, u32[]{:S(2)}, u32[]{:S(2)}) %collective-permute-start.26) | collective-permute-done | bytes 147488 | tf_op jit(solution)/shard_map/ppermute | solution.py:491
  60.3 1.5 %collective-permute-start.18 = (bf16[192,384]{1,0:T(8,128)(2,1)S(1)}, bf16[192,384]{1,0:T(8,128)(2,1)S(1)}, u32[]{:S(2)}, u32[]{:S(2)}) collective-permute-start(bf16[192,384]{1,0:T(8,128)(2,1)S(1)} %collective-permute-done.14.refs_0_), channel_id=1, source_target_pairs={{0,4},{1,5},{2,6},{3,7},{4,0},{5,1},{6,2},{7,3},{8,12},{9,13},{10,... | collective-permute-start | bytes 442376 | tf_op jit(solution)/shard_map/ppermute | solution.py:478
  63.1 2.3 %shard_map.56 = (bf16[2,768,384]{2,1,0:T(8,128)(2,1)}, bf16[768,768]{1,0:T(8,128)(2,1)S(1)}, bf16[2,768,384]{2,1,0:T(8,128)(2,1)S(1)}, bf16[768,768]{1,0:T(8,128)(2,1)S(1)}) custom-call(bf16[4,2,768,384]{3,2,1,0:T(8,128)(2,1)S(1)} %get-tuple-element.41.c.refs_1_, bf16[2,768,384]{2,1,0:T(8,128)(2,1)S(1)} %get-tuple-element.43.c01.refs_3_, ...), custom_call_target="tpu_custom_call" | custom-call | flops 1811939328 | bytes 11796480 | tf_op jit(solution)/shard_map/pallas_call | solution.py:167
  65.5 1.7 %collective-permute-start.27 = (bf16[192,384]{1,0:T(8,128)(2,1)S(1)}, bf16[192,384]{1,0:T(8,128)(2,1)S(1)}, u32[]{:S(2)}, u32[]{:S(2)}) collective-permute-start(bf16[192,384]{1,0:T(8,128)(2,1)S(1)} %shard_map.63.refs_0_), channel_id=1, source_target_pairs={{0,2},{1,3},{2,0},{3,1},{4,6},{5,7},{6,4},{7,5},{8,10},{9,11},{10,... | collective-permute-start | bytes 442376 | tf_op jit(solution)/shard_map/ppermute | solution.py:478
  67.9 4.8 %collective-permute-start.29 = (bf16[192,384]{1,0:T(8,128)(2,1)S(1)}, bf16[192,384]{1,0:T(8,128)(2,1)S(1)}, u32[]{:S(2)}, u32[]{:S(2)}) collective-permute-start(bf16[192,384]{1,0:T(8,128)(2,1)S(1)} %shard_map.63.refs_0_), channel_id=1, source_target_pairs={{0,6},{1,7},{2,4},{3,5},{4,2},{5,3},{6,0},{7,1},{8,14},{9,15},{10,... | collective-permute-start | bytes 442376 | tf_op jit(solution)/shard_map/ppermute | solution.py:478
  73.9 1.9 %collective-permute-done.29.refs_3_ = bf16[192,384]{1,0:T(8,128)(2,1)S(1)} collective-permute-done((bf16[192,384]{1,0:T(8,128)(2,1)S(1)}, bf16[192,384]{1,0:T(8,128)(2,1)S(1)}, u32[]{:S(2)}, u32[]{:S(2)}) %collective-permute-start.29) | collective-permute-done | bytes 147488 | tf_op jit(solution)/shard_map/ppermute | solution.py:478
  76.0 1.6 %shard_map.57 = (bf16[352,128]{1,0:T(8,128)(2,1)S(1)}, bf16[768,768]{1,0:T(8,128)(2,1)S(1)}) custom-call(f32[768,384]{1,0:T(8,128)S(1)} %get-tuple-element.49.agg, bf16[768,384]{1,0:T(8,128)(2,1)S(1)} %get-tuple-element.57.agg_cols, bf16[768,768]{1,0:T(8,128)(2,1)S(1)} %get-tuple-element.58.agg_t, bf16[1408,128]{1,0:T(8,128)(2,1)S(1)} %collective-permute-done.16.refs_0_, ...), custom_call_target="tpu_custom_call" | custom-call | flops 905969664 | bytes 4939776 | tf_op jit(solution)/shard_map/pallas_call | solution.py:167
  79.5 1.6 %shard_map.58.refs_0_ = f32[768,384]{1,0:T(8,128)S(1)} custom-call(f32[768,384]{1,0:T(8,128)S(1)} %shard_map.55.cov, bf16[2,768,384]{2,1,0:T(8,128)(2,1)S(1)} %get-tuple-element.62.mine.refs_0_, bf16[768,768]{1,0:T(8,128)(2,1)S(1)} %get-tuple-element.56.mine_t.refs_1_, bf16[768,768]{1,0:T(8,128)(2,1)S(1)} %get-tuple-element.61.right), custom_call_target="tpu_custom_call" | custom-call | flops 905969664 | bytes 5898240 | tf_op jit(solution)/shard_map/pallas_call | solution.py:167
  81.2 1.8 %shard_map.61 = (bf16[2,768,384]{2,1,0:T(8,128)(2,1)S(1)}, bf16[768,768]{1,0:T(8,128)(2,1)S(1)}) custom-call(bf16[2,768,384]{2,1,0:T(8,128)(2,1)S(1)} %get-tuple-element.62.mine.refs_0_, bf16[768,768]{1,0:T(8,128)(2,1)S(1)} %get-tuple-element.56.mine_t.refs_1_, bf16[768,384]{1,0:T(8,128)(2,1)S(1)} %shard_map.60.refs_2_, ...), custom_call_target="tpu_custom_call" | custom-call | flops 905969664 | bytes 5898240 | tf_op jit(solution)/shard_map/pallas_call | solution.py:167
  83.0 1.7 %shard_map.65 = bf16[1,768,384]{2,1,0:T(8,128)(2,1)} custom-call(bf16[2,768,384]{2,1,0:T(8,128)(2,1)S(1)} %get-tuple-element.63.refs_0_.refs_1_, bf16[768,384]{1,0:T(8,128)(2,1)S(1)} %shard_map.64.refs_1_, bf16[768,384]{1,0:T(8,128)(2,1)S(1)} %collective-permute-done.30.refs_2_), custom_call_target="tpu_custom_call" | custom-call | flops 452984832 | bytes 2949120 | tf_op jit(solution)/shard_map/pallas_call | solution.py:167
  84.7 2.4 %collective-permute-done.24.refs_1_ = bf16[352,128]{1,0:T(8,128)(2,1)S(1)} collective-permute-done((bf16[352,128]{1,0:T(8,128)(2,1)S(1)}, bf16[352,128]{1,0:T(8,128)(2,1)S(1)}, u32[]{:S(2)}, u32[]{:S(2)}) %collective-permute-start.24) | collective-permute-done | bytes 90144 | tf_op jit(solution)/shard_map/ppermute | solution.py:491
  87.7 3.0 %collective-permute-start.32 = (bf16[352,128]{1,0:T(8,128)(2,1)S(1)}, bf16[352,128]{1,0:T(8,128)(2,1)S(1)}, u32[]{:S(2)}, u32[]{:S(2)}) collective-permute-start(bf16[352,128]{1,0:T(8,128)(2,1)S(1)} %shard_map.62.refs_0_), channel_id=1, source_target_pairs={{0,4},{1,5},{2,6},{3,7},{4,0},{5,1},{6,2},{7,3},{8,12},{9,13},{10,... | collective-permute-start | bytes 270344 | tf_op jit(solution)/shard_map/ppermute | solution.py:478
  91.7 2.4 %collective-permute-done.32.refs_2_ = bf16[352,128]{1,0:T(8,128)(2,1)S(1)} collective-permute-done((bf16[352,128]{1,0:T(8,128)(2,1)S(1)}, bf16[352,128]{1,0:T(8,128)(2,1)S(1)}, u32[]{:S(2)}, u32[]{:S(2)}) %collective-permute-start.32) | collective-permute-done | bytes 90144 | tf_op jit(solution)/shard_map/ppermute | solution.py:478
  94.1 1.9 %collective-permute-done.33.refs_3_ = bf16[352,128]{1,0:T(8,128)(2,1)S(1)} collective-permute-done((bf16[352,128]{1,0:T(8,128)(2,1)S(1)}, bf16[352,128]{1,0:T(8,128)(2,1)S(1)}, u32[]{:S(2)}, u32[]{:S(2)}) %collective-permute-start.33) | collective-permute-done | bytes 90144 | tf_op jit(solution)/shard_map/ppermute | solution.py:478
  96.2 1.7 %collective-permute-done.34.refs_4_ = bf16[1408,128]{1,0:T(8,128)(2,1)S(1)} collective-permute-done((bf16[1408,128]{1,0:T(8,128)(2,1)S(1)}, bf16[1408,128]{1,0:T(8,128)(2,1)S(1)}, u32[]{:S(2)}, u32[]{:S(2)}) %collective-permute-start.34) | collective-permute-done | bytes 360480 | tf_op jit(solution)/shard_map/ppermute | solution.py:467
  97.9 2.5 %shard_map.67 = f32[1,768,384]{2,1,0:T(8,128)} custom-call(f32[768,384]{1,0:T(8,128)S(1)} %shard_map.58.refs_0_, bf16[2,768,384]{2,1,0:T(8,128)(2,1)S(1)} %get-tuple-element.63.refs_0_.refs_1_, bf16[768,768]{1,0:T(8,128)(2,1)S(1)} %get-tuple-element.64.refs_2_, bf16[1408,128]{1,0:T(8,128)(2,1)S(1)} %shard_map.66.refs_3_, ...), custom_call_target="tpu_custom_call" | custom-call | flops 905969664 | bytes 5439488 | tf_op jit(solution)/shard_map/pallas_call | solution.py:167
  (62 shorter events, 15.9 us)
Async XLA Ops:
  2.1 16.7 %collective-permute-start.2 = (bf16[768,384]{1,0:T(8,128)(2,1)S(1)}, bf16[768,384]{1,0:T(8,128)(2,1)S(1)}, u32[]{:S(2)}, u32[]{:S(2)}) collective-permute-start(bf16[768,384]{1,0:T(8,128)(2,1)S(1)} %convert_bitcast_fusion.refs_4_.refs_0_), channel_id=1, source_target_pairs={{0,4},{1,3},{2,6},{3,1},{4,0},{5,7},{6,2},{7,5},{8,12},{9,11},{10,... | collective-permute-start | bytes 1769480 | tf_op jit(solution)/shard_map/ppermute | solution.py:478
  5.2 13.7 %collective-permute-start.4 = (bf16[768,384]{1,0:T(8,128)(2,1)S(1)}, bf16[768,384]{1,0:T(8,128)(2,1)S(1)}, u32[]{:S(2)}, u32[]{:S(2)}) collective-permute-start(bf16[768,384]{1,0:T(8,128)(2,1)S(1)} %convert_bitcast_fusion.refs_4_.refs_0_), channel_id=1, source_target_pairs={{0,2},{1,5},{2,0},{3,7},{4,6},{5,1},{6,4},{7,3},{8,10},{9,13},{10,... | collective-permute-start | bytes 1769480 | tf_op jit(solution)/shard_map/ppermute | solution.py:478
  6.7 14.1 %collective-permute-start = (bf16[768,384]{1,0:T(8,128)(2,1)S(1)}, bf16[768,384]{1,0:T(8,128)(2,1)S(1)}, u32[]{:S(2)}, u32[]{:S(2)}) collective-permute-start(bf16[768,384]{1,0:T(8,128)(2,1)S(1)} %convert_element_type.10.refs_2_), channel_id=1, source_target_pairs={{1,0},{0,1},{3,2},{2,3},{5,4},{4,5},{7,6},{6,7},{9,8},{8,9},{11,10... | collective-permute-start | bytes 1769480 | tf_op jit(solution)/shard_map/ppermute | solution.py:467
  6.8 14.0 %collective-permute-start.1 = (bf16[768,384]{1,0:T(8,128)(2,1)S(1)}, bf16[768,384]{1,0:T(8,128)(2,1)S(1)}, u32[]{:S(2)}, u32[]{:S(2)}) collective-permute-start(bf16[768,384]{1,0:T(8,128)(2,1)S(1)} %convert_bitcast_fusion.refs_4_.refs_0_), channel_id=1, source_target_pairs={{1,0},{0,1},{3,2},{2,3},{5,4},{4,5},{7,6},{6,7},{9,8},{8,9},{11,10... | collective-permute-start | bytes 1769480 | tf_op jit(solution)/shard_map/ppermute | solution.py:467
  18.8 5.5 %collective-permute-start.3 = (bf16[768,384]{1,0:T(8,128)(2,1)S(1)}, bf16[768,384]{1,0:T(8,128)(2,1)S(1)}, u32[]{:S(2)}, u32[]{:S(2)}) collective-permute-start(bf16[768,384]{1,0:T(8,128)(2,1)S(1)} %collective-permute-done.2.refs_2_), channel_id=1, source_target_pairs={{1,0},{0,1},{3,2},{2,3},{5,4},{4,5},{7,6},{6,7},{9,8},{8,9},{11,10... | collective-permute-start | bytes 1769480 | tf_op jit(solution)/shard_map/ppermute | solution.py:467
  18.8 5.5 %collective-permute-start.5 = (bf16[768,384]{1,0:T(8,128)(2,1)S(1)}, bf16[768,384]{1,0:T(8,128)(2,1)S(1)}, u32[]{:S(2)}, u32[]{:S(2)}) collective-permute-start(bf16[768,384]{1,0:T(8,128)(2,1)S(1)} %collective-permute-done.4.refs_4_), channel_id=1, source_target_pairs={{1,0},{0,1},{3,2},{2,3},{5,4},{4,5},{7,6},{6,7},{9,8},{8,9},{11,10... | collective-permute-start | bytes 1769480 | tf_op jit(solution)/shard_map/ppermute | solution.py:467
  19.3 13.5 %collective-permute-start.6 = (bf16[768,384]{1,0:T(8,128)(2,1)S(1)}, bf16[768,384]{1,0:T(8,128)(2,1)S(1)}, u32[]{:S(2)}, u32[]{:S(2)}) collective-permute-start(bf16[768,384]{1,0:T(8,128)(2,1)S(1)} %collective-permute-done.2.refs_2_), channel_id=1, source_target_pairs={{0,2},{1,5},{2,0},{3,7},{4,6},{5,1},{6,4},{7,3},{8,10},{9,13},{10,... | collective-permute-start | bytes 1769480 | tf_op jit(solution)/shard_map/ppermute | solution.py:478
  22.6 10.3 %collective-permute-start.7 = (bf16[1408,128]{1,0:T(8,128)(2,1)S(1)}, bf16[1408,128]{1,0:T(8,128)(2,1)S(1)}, u32[]{:S(2)}, u32[]{:S(2)}) collective-permute-start(bf16[1408,128]{1,0:T(8,128)(2,1)S(1)} %get-tuple-element.39.refs_5_), channel_id=1, source_target_pairs={{0,4},{1,3},{2,6},{3,1},{4,0},{5,7},{6,2},{7,5},{8,12},{9,11},{10,... | collective-permute-start | bytes 1081352 | tf_op jit(solution)/shard_map/ppermute | solution.py:478
  33.0 7.4 %collective-permute-start.11 = (bf16[1408,128]{1,0:T(8,128)(2,1)S(1)}, bf16[1408,128]{1,0:T(8,128)(2,1)S(1)}, u32[]{:S(2)}, u32[]{:S(2)}) collective-permute-start(bf16[1408,128]{1,0:T(8,128)(2,1)S(1)} %get-tuple-element.39.refs_5_), channel_id=1, source_target_pairs={{0,2},{1,5},{2,0},{3,7},{4,6},{5,1},{6,4},{7,3},{8,10},{9,13},{10,... | collective-permute-start | bytes 1081352 | tf_op jit(solution)/shard_map/ppermute | solution.py:478
  34.6 9.7 %collective-permute-start.13 = (bf16[1408,128]{1,0:T(8,128)(2,1)S(1)}, bf16[1408,128]{1,0:T(8,128)(2,1)S(1)}, u32[]{:S(2)}, u32[]{:S(2)}) collective-permute-start(bf16[1408,128]{1,0:T(8,128)(2,1)S(1)} %collective-permute-done.7.refs_7_), channel_id=1, source_target_pairs={{0,2},{1,5},{2,0},{3,7},{4,6},{5,1},{6,4},{7,3},{8,10},{9,13},{10,... | collective-permute-start | bytes 1081352 | tf_op jit(solution)/shard_map/ppermute | solution.py:478
  37.4 8.5 %collective-permute-start.14 = (bf16[192,384]{1,0:T(8,128)(2,1)S(1)}, bf16[192,384]{1,0:T(8,128)(2,1)S(1)}, u32[]{:S(2)}, u32[]{:S(2)}) collective-permute-start(bf16[192,384]{1,0:T(8,128)(2,1)S(1)} %get-tuple-element.46), channel_id=1, source_target_pairs={{8,0},{10,2},{12,4},{14,6},{24,16},{26,18},{28,20},{30,22},{9,1},{... | collective-permute-start | bytes 442376 | tf_op jit(solution)/shard_map/ppermute | solution.py:491
  38.7 10.1 %collective-permute-start.9 = (bf16[1408,128]{1,0:T(8,128)(2,1)S(1)}, bf16[1408,128]{1,0:T(8,128)(2,1)S(1)}, u32[]{:S(2)}, u32[]{:S(2)}) collective-permute-start(bf16[1408,128]{1,0:T(8,128)(2,1)S(1)} %get-tuple-element.39.refs_5_), channel_id=1, source_target_pairs={{1,0},{0,1},{3,2},{2,3},{5,4},{4,5},{7,6},{6,7},{9,8},{8,9},{11,10... | collective-permute-start | bytes 1081352 | tf_op jit(solution)/shard_map/ppermute | solution.py:467
  39.5 10.7 %collective-permute-start.10 = (bf16[1408,128]{1,0:T(8,128)(2,1)S(1)}, bf16[1408,128]{1,0:T(8,128)(2,1)S(1)}, u32[]{:S(2)}, u32[]{:S(2)}) collective-permute-start(bf16[1408,128]{1,0:T(8,128)(2,1)S(1)} %collective-permute-done.7.refs_7_), channel_id=1, source_target_pairs={{1,0},{0,1},{3,2},{2,3},{5,4},{4,5},{7,6},{6,7},{9,8},{8,9},{11,10... | collective-permute-start | bytes 1081352 | tf_op jit(solution)/shard_map/ppermute | solution.py:467
  40.4 9.8 %collective-permute-start.12 = (bf16[1408,128]{1,0:T(8,128)(2,1)S(1)}, bf16[1408,128]{1,0:T(8,128)(2,1)S(1)}, u32[]{:S(2)}, u32[]{:S(2)}) collective-permute-start(bf16[1408,128]{1,0:T(8,128)(2,1)S(1)} %collective-permute-done.11.refs_9_), channel_id=1, source_target_pairs={{1,0},{0,1},{3,2},{2,3},{5,4},{4,5},{7,6},{6,7},{9,8},{8,9},{11,10... | collective-permute-start | bytes 1081352 | tf_op jit(solution)/shard_map/ppermute | solution.py:467
  45.8 4.4 %collective-permute-start.15 = (bf16[1408,128]{1,0:T(8,128)(2,1)S(1)}, bf16[1408,128]{1,0:T(8,128)(2,1)S(1)}, u32[]{:S(2)}, u32[]{:S(2)}) collective-permute-start(bf16[1408,128]{1,0:T(8,128)(2,1)S(1)} %collective-permute-done.13.refs_11_), channel_id=1, source_target_pairs={{1,0},{0,1},{3,2},{2,3},{5,4},{4,5},{7,6},{6,7},{9,8},{8,9},{11,10... | collective-permute-start | bytes 1081352 | tf_op jit(solution)/shard_map/ppermute | solution.py:467
  48.1 9.4 %collective-permute-start.25 = (bf16[192,384]{1,0:T(8,128)(2,1)S(1)}, bf16[192,384]{1,0:T(8,128)(2,1)S(1)}, u32[]{:S(2)}, u32[]{:S(2)}) collective-permute-start(bf16[192,384]{1,0:T(8,128)(2,1)S(1)} %shard_map.59), channel_id=1, source_target_pairs={{16,8},{18,10},{20,12},{22,14},{17,9},{19,11},{21,13},{23,15}} | collective-permute-start | bytes 442376 | tf_op jit(solution)/shard_map/ppermute | solution.py:491
  48.7 10.8 %collective-permute-start.26 = (bf16[192,384]{1,0:T(8,128)(2,1)S(1)}, bf16[192,384]{1,0:T(8,128)(2,1)S(1)}, u32[]{:S(2)}, u32[]{:S(2)}) collective-permute-start(bf16[192,384]{1,0:T(8,128)(2,1)S(1)} %shard_map.59), channel_id=1, source_target_pairs={{16,0},{18,2},{20,4},{22,6},{17,1},{19,3},{21,5},{23,7}} | collective-permute-start | bytes 442376 | tf_op jit(solution)/shard_map/ppermute | solution.py:491
  56.1 16.8 %collective-permute-start.16 = (bf16[1408,128]{1,0:T(8,128)(2,1)S(1)}, bf16[1408,128]{1,0:T(8,128)(2,1)S(1)}, u32[]{:S(2)}, u32[]{:S(2)}) collective-permute-start(bf16[1408,128]{1,0:T(8,128)(2,1)S(1)} %get-tuple-element.53), channel_id=1, source_target_pairs={{8,0},{10,2},{12,4},{14,6},{24,16},{26,18},{28,20},{30,22},{9,1},{... | collective-permute-start | bytes 1081352 | tf_op jit(solution)/shard_map/ppermute | solution.py:491
  59.6 7.6 %collective-permute-start.17 = (bf16[192,384]{1,0:T(8,128)(2,1)S(1)}, bf16[192,384]{1,0:T(8,128)(2,1)S(1)}, u32[]{:S(2)}, u32[]{:S(2)}) collective-permute-start(bf16[192,384]{1,0:T(8,128)(2,1)S(1)} %collective-permute-done.14.refs_0_), channel_id=1, source_target_pairs={{0,2},{1,3},{2,0},{3,1},{4,6},{5,7},{6,4},{7,5},{8,10},{9,11},{10,... | collective-permute-start | bytes 442376 | tf_op jit(solution)/shard_map/ppermute | solution.py:478
  60.3 7.5 %collective-permute-start.18 = (bf16[192,384]{1,0:T(8,128)(2,1)S(1)}, bf16[192,384]{1,0:T(8,128)(2,1)S(1)}, u32[]{:S(2)}, u32[]{:S(2)}) collective-permute-start(bf16[192,384]{1,0:T(8,128)(2,1)S(1)} %collective-permute-done.14.refs_0_), channel_id=1, source_target_pairs={{0,4},{1,5},{2,6},{3,7},{4,0},{5,1},{6,2},{7,3},{8,12},{9,13},{10,... | collective-permute-start | bytes 442376 | tf_op jit(solution)/shard_map/ppermute | solution.py:478
  61.9 10.8 %collective-permute-start.19 = (bf16[192,384]{1,0:T(8,128)(2,1)S(1)}, bf16[192,384]{1,0:T(8,128)(2,1)S(1)}, u32[]{:S(2)}, u32[]{:S(2)}) collective-permute-start(bf16[192,384]{1,0:T(8,128)(2,1)S(1)} %collective-permute-done.14.refs_0_), channel_id=1, source_target_pairs={{0,6},{1,7},{2,4},{3,5},{4,2},{5,3},{6,0},{7,1},{8,14},{9,15},{10,... | collective-permute-start | bytes 442376 | tf_op jit(solution)/shard_map/ppermute | solution.py:478
  65.5 8.0 %collective-permute-start.27 = (bf16[192,384]{1,0:T(8,128)(2,1)S(1)}, bf16[192,384]{1,0:T(8,128)(2,1)S(1)}, u32[]{:S(2)}, u32[]{:S(2)}) collective-permute-start(bf16[192,384]{1,0:T(8,128)(2,1)S(1)} %shard_map.63.refs_0_), channel_id=1, source_target_pairs={{0,2},{1,3},{2,0},{3,1},{4,6},{5,7},{6,4},{7,5},{8,10},{9,11},{10,... | collective-permute-start | bytes 442376 | tf_op jit(solution)/shard_map/ppermute | solution.py:478
  67.2 6.7 %collective-permute-start.28 = (bf16[192,384]{1,0:T(8,128)(2,1)S(1)}, bf16[192,384]{1,0:T(8,128)(2,1)S(1)}, u32[]{:S(2)}, u32[]{:S(2)}) collective-permute-start(bf16[192,384]{1,0:T(8,128)(2,1)S(1)} %shard_map.63.refs_0_), channel_id=1, source_target_pairs={{0,4},{1,5},{2,6},{3,7},{4,0},{5,1},{6,2},{7,3},{8,12},{9,13},{10,... | collective-permute-start | bytes 442376 | tf_op jit(solution)/shard_map/ppermute | solution.py:478
  67.9 7.9 %collective-permute-start.29 = (bf16[192,384]{1,0:T(8,128)(2,1)S(1)}, bf16[192,384]{1,0:T(8,128)(2,1)S(1)}, u32[]{:S(2)}, u32[]{:S(2)}) collective-permute-start(bf16[192,384]{1,0:T(8,128)(2,1)S(1)} %shard_map.63.refs_0_), channel_id=1, source_target_pairs={{0,6},{1,7},{2,4},{3,5},{4,2},{5,3},{6,0},{7,1},{8,14},{9,15},{10,... | collective-permute-start | bytes 442376 | tf_op jit(solution)/shard_map/ppermute | solution.py:478
  72.8 8.4 %collective-permute-start.22 = (bf16[768,384]{1,0:T(8,128)(2,1)S(1)}, bf16[768,384]{1,0:T(8,128)(2,1)S(1)}, u32[]{:S(2)}, u32[]{:S(2)}) collective-permute-start(bf16[768,384]{1,0:T(8,128)(2,1)S(1)} %shard_map.60.refs_2_), channel_id=1, source_target_pairs={{1,0},{0,1},{3,2},{2,3},{5,4},{4,5},{7,6},{6,7},{9,8},{8,9},{11,10... | collective-permute-start | bytes 1769480 | tf_op jit(solution)/shard_map/ppermute | solution.py:467
  73.0 3.0 %collective-permute-start.20 = (bf16[1408,128]{1,0:T(8,128)(2,1)S(1)}, bf16[1408,128]{1,0:T(8,128)(2,1)S(1)}, u32[]{:S(2)}, u32[]{:S(2)}) collective-permute-start(bf16[1408,128]{1,0:T(8,128)(2,1)S(1)} %collective-permute-done.16.refs_0_), channel_id=1, source_target_pairs={{1,0},{0,1},{3,2},{2,3},{5,4},{4,5},{7,6},{6,7},{9,8},{8,9},{11,10... | collective-permute-start | bytes 1081352 | tf_op jit(solution)/shard_map/ppermute | solution.py:467
  75.9 7.1 %collective-permute-start.30 = (bf16[768,384]{1,0:T(8,128)(2,1)S(1)}, bf16[768,384]{1,0:T(8,128)(2,1)S(1)}, u32[]{:S(2)}, u32[]{:S(2)}) collective-permute-start(bf16[768,384]{1,0:T(8,128)(2,1)S(1)} %shard_map.64.refs_1_), channel_id=1, source_target_pairs={{1,0},{0,1},{3,2},{2,3},{5,4},{4,5},{7,6},{6,7},{9,8},{8,9},{11,10... | collective-permute-start | bytes 1769480 | tf_op jit(solution)/shard_map/ppermute | solution.py:467
  77.6 7.1 %collective-permute-start.23 = (bf16[352,128]{1,0:T(8,128)(2,1)S(1)}, bf16[352,128]{1,0:T(8,128)(2,1)S(1)}, u32[]{:S(2)}, u32[]{:S(2)}) collective-permute-start(bf16[352,128]{1,0:T(8,128)(2,1)S(1)} %get-tuple-element.65), channel_id=1, source_target_pairs={{16,8},{18,10},{20,12},{22,14},{17,9},{19,11},{21,13},{23,15}} | collective-permute-start | bytes 270344 | tf_op jit(solution)/shard_map/ppermute | solution.py:491
  78.2 8.8 %collective-permute-start.24 = (bf16[352,128]{1,0:T(8,128)(2,1)S(1)}, bf16[352,128]{1,0:T(8,128)(2,1)S(1)}, u32[]{:S(2)}, u32[]{:S(2)}) collective-permute-start(bf16[352,128]{1,0:T(8,128)(2,1)S(1)} %get-tuple-element.65), channel_id=1, source_target_pairs={{16,0},{18,2},{20,4},{22,6},{17,1},{19,3},{21,5},{23,7}} | collective-permute-start | bytes 270344 | tf_op jit(solution)/shard_map/ppermute | solution.py:491
  87.1 4.6 %collective-permute-start.31 = (bf16[352,128]{1,0:T(8,128)(2,1)S(1)}, bf16[352,128]{1,0:T(8,128)(2,1)S(1)}, u32[]{:S(2)}, u32[]{:S(2)}) collective-permute-start(bf16[352,128]{1,0:T(8,128)(2,1)S(1)} %shard_map.62.refs_0_), channel_id=1, source_target_pairs={{0,2},{1,3},{2,0},{3,1},{4,6},{5,7},{6,4},{7,5},{8,10},{9,11},{10,... | collective-permute-start | bytes 270344 | tf_op jit(solution)/shard_map/ppermute | solution.py:478
  87.7 6.5 %collective-permute-start.32 = (bf16[352,128]{1,0:T(8,128)(2,1)S(1)}, bf16[352,128]{1,0:T(8,128)(2,1)S(1)}, u32[]{:S(2)}, u32[]{:S(2)}) collective-permute-start(bf16[352,128]{1,0:T(8,128)(2,1)S(1)} %shard_map.62.refs_0_), channel_id=1, source_target_pairs={{0,4},{1,5},{2,6},{3,7},{4,0},{5,1},{6,2},{7,3},{8,12},{9,13},{10,... | collective-permute-start | bytes 270344 | tf_op jit(solution)/shard_map/ppermute | solution.py:478
  90.6 5.4 %collective-permute-start.33 = (bf16[352,128]{1,0:T(8,128)(2,1)S(1)}, bf16[352,128]{1,0:T(8,128)(2,1)S(1)}, u32[]{:S(2)}, u32[]{:S(2)}) collective-permute-start(bf16[352,128]{1,0:T(8,128)(2,1)S(1)} %shard_map.62.refs_0_), channel_id=1, source_target_pairs={{0,6},{1,7},{2,4},{3,5},{4,2},{5,3},{6,0},{7,1},{8,14},{9,15},{10,... | collective-permute-start | bytes 270344 | tf_op jit(solution)/shard_map/ppermute | solution.py:478
  (5 other events, 32.0 us)
where the time goes:
time: 101 us; the launch traced here: 100 us
  waiting for transfers between devices  38.5 us (38%)
  starting transfers between devices  34.7 us (34%)
  Pallas kernels  24.7 us (24%)
  other arithmetic  1.55 us (2%)
    ppermute x15, waiting for transfers between devices, swap(): return lax.ppermute(value, ('tm', 'panel'), pairs)  30 us
    pallas_call x18, Pallas kernels, call(): pl.pallas_call(kernel, in_specs=in_specs, out_specs=[VMEM] * len(outs), o...  24.7 us
    ppermute x15, starting transfers between devices, swap(): return lax.ppermute(value, ('tm', 'panel'), pairs)  24.1 us
    ppermute x6, starting transfers between devices, across(): got.append(lax.ppermute(x, 'tm', pairs))  6.69 us
    ppermute x6, waiting for transfers between devices, across(): got.append(lax.ppermute(x, 'tm', pairs))  6.07 us
    ppermute x14, starting transfers between devices, over_panels(): lax.ppermute(x, 'panel', [((i + r) % n, i) for i in range(n)])  3.93 us
    ppermute x14, waiting for transfers between devices, over_panels(): lax.ppermute(x, 'panel', [((i + r) % n, i) for i in range(n)])  2.41 us
  transfers between devices with their start and end apart: 35, of which 14 were waited for; matrix products, arithmetic and copies ran while one was open for 0% of the time, Pallas kernels for 22%

commit v1 on v0

--- a/solution.py
+++ b/solution.py
@@ -569,7 +569,18 @@
     c_t, c01_t = call(
         turn_comp_kernel, [c_all, c_t, c01], [VMEM] * 3, [turned_bf, square_bf], [], 0, {1: 0}
     )
-    s_second, s_diag = after(s_second, c_share), after(s_diag, c_far)
+    first_share = None
+    if levels == 2:
+        (first_share,) = call(
+            functools.partial(share_comp_kernel, n),
+            [agg_cols, *over_panels(c_far)],
+            [VMEM] * (1 + n),
+            [share_bf],
+            [],
+            one // 4,
+        )
+    s_second = after(s_second, c_share)
+    s_diag = after(s_diag, c_far if first_share is None else first_share)
     s_pieces = [p for v in (base_bf, s_first, s_second, s_diag) for p in over_panels(v)]
     agg, agg_bf, s3, s23 = call(
         functools.partial(group_cov_kernel, n),
@@ -606,17 +617,21 @@
     for bit in range(levels):
         to_last = bit + 2 == levels
         if bit + 1 == levels:
-            c_parts = over_panels(joined(in_group(c_far)))
+            c_blocks = in_group(c_far)
+            if bit:
+                c_blocks[0] = after(c_blocks[0], cov)
+            c_panel = joined(c_blocks)
+            if bit:
+                c_panel = after(c_panel, *s_blocks[1:])
+            c_parts = over_panels(c_panel)
             (prop,) = call(
                 functools.partial(last_comp_kernel, n, bit),
-                [mine, *c_parts],
+                [after(mine, s_got), *c_parts],
                 [VMEM] * (1 + n),
                 [out_comp],
                 [],
                 one,
             )
-            if bit:
-                s_got = joined(in_group(after(s_far, prop, cov)))
             s_parts = over_panels(s_got)
             (cov,) = call(
                 functools.partial(last_cov_kernel, n, bit),
@@ -628,14 +643,16 @@
             )
             break
         if to_last:
-            (c_send,) = call(
-                functools.partial(share_comp_kernel, n),
-                [agg_cols, *over_panels(c_far)],
-                [VMEM] * (1 + n),
-                [share_bf],
-                [],
-                one // 4,
-            )
+            c_send = first_share
+            if c_send is None:
+                (c_send,) = call(
+                    functools.partial(share_comp_kernel, n),
+                    [agg_cols, *over_panels(c_far)],
+                    [VMEM] * (1 + n),
+                    [share_bf],
+                    [],
+                    one // 4,
+                )
             c_blocks = in_group(after(c_far, agg_bf))
             c_parts = over_panels(joined(c_blocks))
         else:
@@ -649,7 +666,7 @@
                 [],
                 n * one,
             )
-        c_far = after(across(c_send, bit + 1), mine)
+        c_far = across(c_send, bit + 1)
         new_mine, new_mine_t = call(
             functools.partial(mine_comp_kernel, n, bit),
             [after(mine, c_send), mine_t, *c_parts],
@@ -658,7 +675,7 @@
             [],
             n * one,
         )
-        s_parts = over_panels(after(s_got, mine, cov, *c_blocks[1:]))
+        s_parts = over_panels(after(s_got, mine, cov, c_far, c_blocks[2], c_blocks[3]))
         outs = call(
             functools.partial(pair_cov_kernel, n, to_last),
             [agg, agg_cols, agg_t, *s_parts],
@@ -671,7 +688,7 @@
         s_far = across(s_send, bit + 1)
         (cov,) = call(
             functools.partial(mine_cov_kernel, n, bit),
-            [cov, mine, mine_t, right],
+            [after(cov, s_far), mine, mine_t, right],
             [VMEM] * 4,
             [panel_f32],
             [],
@@ -680,8 +697,9 @@
         if not to_last:
             agg, agg_bf = outs[2:]
             agg_c, agg_t, agg_cols = new_agg_c, new_agg_t, new_cols
-        if not to_last:
-            s_got = joined(in_group(s_far))
+        s_blocks = in_group(s_far)
+        s_got = joined(s_blocks)
+        c_far = after(c_far, s_send)
         mine, mine_t = new_mine, new_mine_t
     return cov, prop
 

time: 101 us -> 97.6 us (0.966)
  starting transfers between devices: 34.7 us -> 29.8 us
  waiting for transfers between devices: 38.5 us -> 40.7 us
    ppermute x6, waiting for transfers between devices: 6.07 us -> 14.9 us  [across(): got.append(lax.ppermute(x, 'tm', pairs))]
    ppermute x15, waiting for transfers between devices: 30 us -> 24.5 us  [swap(): return lax.ppermute(value, ('tm', 'panel'), pairs)]
    ppermute x15, starting transfers between devices: 24.1 us -> 20 us  [swap(): return lax.ppermute(value, ('tm', 'panel'), pairs)]
    ppermute x14, waiting for transfers between devices: 2.41 us -> 1.32 us  [over_panels(): lax.ppermute(x, 'panel', [((i + r) % n, i) for i in range(n)])]
  transfers between devices with their start and end apart: 35 -> 35, of which waited for: 14 -> 13; matrix products, arithmetic and copies ran while one was open for 0% -> 0% of each run, Pallas kernels for 22% -> 23%
where the time goes in v1:
time: 97.6 us; the launch traced here: 97.4 us
  waiting for transfers between devices  40.7 us (42%)
  starting transfers between devices  29.8 us (31%)
  Pallas kernels  24.4 us (25%)
  other arithmetic  1.55 us (2%)
    ppermute x15, waiting for transfers between devices, swap(): return lax.ppermute(value, ('tm', 'panel'), pairs)  24.5 us
    pallas_call x18, Pallas kernels, call(): pl.pallas_call(kernel, in_specs=in_specs, out_specs=[VMEM] * len(outs), o...  24.4 us
    ppermute x15, starting transfers between devices, swap(): return lax.ppermute(value, ('tm', 'panel'), pairs)  20 us
    ppermute x6, waiting for transfers between devices, across(): got.append(lax.ppermute(x, 'tm', pairs))  14.9 us
    ppermute x6, starting transfers between devices, across(): got.append(lax.ppermute(x, 'tm', pairs))  6.67 us
    ppermute x14, starting transfers between devices, over_panels(): lax.ppermute(x, 'panel', [((i + r) % n, i) for i in range(n)])  3.07 us
  transfers between devices with their start and end apart: 35, of which 13 were waited for; matrix products, arithmetic and copies ran while one was open for 0% of the time, Pallas kernels for 23%

profile of v1, /device:TPU:0, one launch (start us, length us, event | category | flops | bytes accessed | tf_op | source)
XLA Modules:
  0.0 97.4 jit_solution(10070310859136048269)
XLA Ops:
  0.6 1.5 %convert_bitcast_fusion.refs_4_.refs_0_ = bf16[768,384]{1,0:T(8,128)(2,1)S(1)} fusion(f32[1,768,384]{2,1,0:T(8,128)} %param.4), kind=kLoop, calls=%fused_computation | loop fusion | flops 294912 | bytes 1769472 | tf_op jit(solution)/shard_map/convert_element_type | solution.py:532
  2.1 3.0 %collective-permute-start.2 = (bf16[768,384]{1,0:T(8,128)(2,1)S(1)}, bf16[768,384]{1,0:T(8,128)(2,1)S(1)}, u32[]{:S(2)}, u32[]{:S(2)}) collective-permute-start(bf16[768,384]{1,0:T(8,128)(2,1)S(1)} %convert_bitcast_fusion.refs_4_.refs_0_), channel_id=1, source_target_pairs={{0,4},{1,3},{2,6},{3,1},{4,0},{5,7},{6,2},{7,5},{8,12},{9,11},{10,... | collective-permute-start | bytes 1769480 | tf_op jit(solution)/shard_map/ppermute | solution.py:478
  5.2 1.5 %collective-permute-start.4 = (bf16[768,384]{1,0:T(8,128)(2,1)S(1)}, bf16[768,384]{1,0:T(8,128)(2,1)S(1)}, u32[]{:S(2)}, u32[]{:S(2)}) collective-permute-start(bf16[768,384]{1,0:T(8,128)(2,1)S(1)} %convert_bitcast_fusion.refs_4_.refs_0_), channel_id=1, source_target_pairs={{0,2},{1,5},{2,0},{3,7},{4,6},{5,1},{6,4},{7,3},{8,10},{9,13},{10,... | collective-permute-start | bytes 1769480 | tf_op jit(solution)/shard_map/ppermute | solution.py:478
  7.3 11.5 %collective-permute-done.2.refs_2_ = bf16[768,384]{1,0:T(8,128)(2,1)S(1)} collective-permute-done((bf16[768,384]{1,0:T(8,128)(2,1)S(1)}, bf16[768,384]{1,0:T(8,128)(2,1)S(1)}, u32[]{:S(2)}, u32[]{:S(2)}) %collective-permute-start.2) | collective-permute-done | bytes 589856 | tf_op jit(solution)/shard_map/ppermute | solution.py:478
  19.3 1.5 %collective-permute-start.6 = (bf16[768,384]{1,0:T(8,128)(2,1)S(1)}, bf16[768,384]{1,0:T(8,128)(2,1)S(1)}, u32[]{:S(2)}, u32[]{:S(2)}) collective-permute-start(bf16[768,384]{1,0:T(8,128)(2,1)S(1)} %collective-permute-done.2.refs_2_), channel_id=1, source_target_pairs={{0,2},{1,5},{2,0},{3,7},{4,6},{5,1},{6,4},{7,3},{8,10},{9,13},{10,... | collective-permute-start | bytes 1769480 | tf_op jit(solution)/shard_map/ppermute | solution.py:478
  20.8 1.7 %shard_map.50 = (f32[768,384]{1,0:T(8,128)S(1)}, bf16[1408,128]{1,0:T(8,128)(2,1)S(1)}) custom-call(f32[768,384]{1,0:T(8,128)S(1)} %bitcast.4, f32[768,768]{1,0:T(8,128)S(1)} %copy-done.1, bf16[768,384]{1,0:T(8,128)(2,1)S(1)} %convert_element_type.10.refs_2_, bf16[768,384]{1,0:T(8,128)(2,1)S(1)} %collective-permute-done.refs_3_, ...), custom_call_target="tpu_custom_call" | custom-call | flops 905969664 | bytes 7438336 | tf_op jit(solution)/shard_map/pallas_call | solution.py:167
  22.6 1.8 %collective-permute-start.7 = (bf16[1408,128]{1,0:T(8,128)(2,1)S(1)}, bf16[1408,128]{1,0:T(8,128)(2,1)S(1)}, u32[]{:S(2)}, u32[]{:S(2)}) collective-permute-start(bf16[1408,128]{1,0:T(8,128)(2,1)S(1)} %get-tuple-element.42.refs_5_), channel_id=1, source_target_pairs={{0,4},{1,3},{2,6},{3,1},{4,0},{5,7},{6,2},{7,5},{8,12},{9,11},{10,... | collective-permute-start | bytes 1081352 | tf_op jit(solution)/shard_map/ppermute | solution.py:478
  24.3 1.9 %shard_map.51 = (bf16[4,2,768,384]{3,2,1,0:T(8,128)(2,1)S(1)}, bf16[4,768,768]{2,1,0:T(8,128)(2,1)S(1)}, bf16[768,768]{1,0:T(8,128)(2,1)S(1)}) custom-call(bf16[768,384]{1,0:T(8,128)(2,1)S(1)} %convert_bitcast_fusion.refs_4_.refs_0_, bf16[768,384]{1,0:T(8,128)(2,1)S(1)} %collective-permute-done.1.refs_5_.refs_1_, ...), custom_call_target="tpu_custom_call" | custom-call | flops 905969664 | bytes 14155776 | tf_op jit(solution)/shard_map/pallas_call | solution.py:167
  26.2 6.6 %collective-permute-done.7.refs_7_ = bf16[1408,128]{1,0:T(8,128)(2,1)S(1)} collective-permute-done((bf16[1408,128]{1,0:T(8,128)(2,1)S(1)}, bf16[1408,128]{1,0:T(8,128)(2,1)S(1)}, u32[]{:S(2)}, u32[]{:S(2)}) %collective-permute-start.7) | collective-permute-done | bytes 360480 | tf_op jit(solution)/shard_map/ppermute | solution.py:478
  33.0 1.6 %collective-permute-start.11 = (bf16[1408,128]{1,0:T(8,128)(2,1)S(1)}, bf16[1408,128]{1,0:T(8,128)(2,1)S(1)}, u32[]{:S(2)}, u32[]{:S(2)}) collective-permute-start(bf16[1408,128]{1,0:T(8,128)(2,1)S(1)} %get-tuple-element.42.refs_5_), channel_id=1, source_target_pairs={{0,2},{1,5},{2,0},{3,7},{4,6},{5,1},{6,4},{7,3},{8,10},{9,13},{10,... | collective-permute-start | bytes 1081352 | tf_op jit(solution)/shard_map/ppermute | solution.py:478
  35.0 2.3 %shard_map.52 = (bf16[4,2,768,384]{3,2,1,0:T(8,128)(2,1)S(1)}, bf16[2,768,384]{2,1,0:T(8,128)(2,1)S(1)}, bf16[768,768]{1,0:T(8,128)(2,1)S(1)}, bf16[768,384]{1,0:T(8,128)(2,1)S(1)}, bf16[192,384]{1,0:T(8,128)(2,1)S(1)}) custom-call(bf16[4,2,768,384]{3,2,1,0:T(8,128)(2,1)S(1)} %get-tuple-element.40.refs_0_, ...), custom_call_target="tpu_custom_call", output_to_operand_aliasing={{0}: (0, {})} | custom-call | flops 1811939328 | bytes 14893056 | tf_op jit(solution)/shard_map/pallas_call | solution.py:167
  37.4 1.3 %collective-permute-start.14 = (bf16[192,384]{1,0:T(8,128)(2,1)S(1)}, bf16[192,384]{1,0:T(8,128)(2,1)S(1)}, u32[]{:S(2)}, u32[]{:S(2)}) collective-permute-start(bf16[192,384]{1,0:T(8,128)(2,1)S(1)} %get-tuple-element.49), channel_id=1, source_target_pairs={{8,0},{10,2},{12,4},{14,6},{24,16},{26,18},{28,20},{30,22},{9,1},{... | collective-permute-start | bytes 442376 | tf_op jit(solution)/shard_map/ppermute | solution.py:491
  38.7 7.2 %collective-permute-done.14.refs_0_ = bf16[192,384]{1,0:T(8,128)(2,1)S(1)} collective-permute-done((bf16[192,384]{1,0:T(8,128)(2,1)S(1)}, bf16[192,384]{1,0:T(8,128)(2,1)S(1)}, u32[]{:S(2)}, u32[]{:S(2)}) %collective-permute-start.14) | collective-permute-done | bytes 147488 | tf_op jit(solution)/shard_map/ppermute | solution.py:491
  49.1 1.5 %collective-permute-start.19 = (bf16[192,384]{1,0:T(8,128)(2,1)S(1)}, bf16[192,384]{1,0:T(8,128)(2,1)S(1)}, u32[]{:S(2)}, u32[]{:S(2)}) collective-permute-start(bf16[192,384]{1,0:T(8,128)(2,1)S(1)} %shard_map.54), channel_id=1, source_target_pairs={{16,0},{18,2},{20,4},{22,6},{17,1},{19,3},{21,5},{23,7}} | collective-permute-start | bytes 442376 | tf_op jit(solution)/shard_map/ppermute | solution.py:491
  50.6 5.9 %shard_map.55 = (f32[768,384]{1,0:T(8,128)S(1)}, bf16[1408,128]{1,0:T(8,128)(2,1)S(1)}, bf16[768,768]{1,0:T(8,128)(2,1)S(1)}, bf16[768,768]{1,0:T(8,128)(2,1)S(1)}) custom-call(f32[768,384]{1,0:T(8,128)S(1)} %get-tuple-element.39.refs_0_.base, bf16[4,2,768,384]{3,2,1,0:T(8,128)(2,1)S(1)} %get-tuple-element.44.c.refs_1_, ...), custom_call_target="tpu_custom_call" | custom-call | flops 3623878656 | bytes 19759104 | tf_op jit(solution)/shard_map/pallas_call | solution.py:167
  56.5 1.3 %collective-permute-start.17 = (bf16[1408,128]{1,0:T(8,128)(2,1)S(1)}, bf16[1408,128]{1,0:T(8,128)(2,1)S(1)}, u32[]{:S(2)}, u32[]{:S(2)}) collective-permute-start(bf16[1408,128]{1,0:T(8,128)(2,1)S(1)} %get-tuple-element.57), channel_id=1, source_target_pairs={{8,0},{10,2},{12,4},{14,6},{24,16},{26,18},{28,20},{30,22},{9,1},{... | collective-permute-start | bytes 1081352 | tf_op jit(solution)/shard_map/ppermute | solution.py:491
  57.8 2.4 %collective-permute-done.19.refs_1_ = bf16[192,384]{1,0:T(8,128)(2,1)S(1)} collective-permute-done((bf16[192,384]{1,0:T(8,128)(2,1)S(1)}, bf16[192,384]{1,0:T(8,128)(2,1)S(1)}, u32[]{:S(2)}, u32[]{:S(2)}) %collective-permute-start.19) | collective-permute-done | bytes 147488 | tf_op jit(solution)/shard_map/ppermute | solution.py:491
  60.2 1.6 %collective-permute-start.20 = (bf16[192,384]{1,0:T(8,128)(2,1)S(1)}, bf16[192,384]{1,0:T(8,128)(2,1)S(1)}, u32[]{:S(2)}, u32[]{:S(2)}) collective-permute-start(bf16[192,384]{1,0:T(8,128)(2,1)S(1)} %collective-permute-done.14.refs_0_), channel_id=1, source_target_pairs={{0,4},{1,5},{2,6},{3,7},{4,0},{5,1},{6,2},{7,3},{8,12},{9,13},{10,... | collective-permute-start | bytes 442376 | tf_op jit(solution)/shard_map/ppermute | solution.py:478
  62.5 2.3 %shard_map.57 = (bf16[2,768,384]{2,1,0:T(8,128)(2,1)}, bf16[768,768]{1,0:T(8,128)(2,1)S(1)}, bf16[2,768,384]{2,1,0:T(8,128)(2,1)S(1)}, bf16[768,768]{1,0:T(8,128)(2,1)S(1)}) custom-call(bf16[4,2,768,384]{3,2,1,0:T(8,128)(2,1)S(1)} %get-tuple-element.44.c.refs_1_, bf16[2,768,384]{2,1,0:T(8,128)(2,1)S(1)} %get-tuple-element.46.c01.refs_3_, ...), custom_call_target="tpu_custom_call" | custom-call | flops 1811939328 | bytes 11796480 | tf_op jit(solution)/shard_map/pallas_call | solution.py:167
  64.8 4.1 %collective-permute-done.20.refs_2_ = bf16[192,384]{1,0:T(8,128)(2,1)S(1)} collective-permute-done((bf16[192,384]{1,0:T(8,128)(2,1)S(1)}, bf16[192,384]{1,0:T(8,128)(2,1)S(1)}, u32[]{:S(2)}, u32[]{:S(2)}) %collective-permute-start.20) | collective-permute-done | bytes 147488 | tf_op jit(solution)/shard_map/ppermute | solution.py:478
  70.8 1.6 %shard_map.59 = (bf16[352,128]{1,0:T(8,128)(2,1)S(1)}, bf16[768,768]{1,0:T(8,128)(2,1)S(1)}) custom-call(f32[768,384]{1,0:T(8,128)S(1)} %get-tuple-element.53.agg, bf16[768,384]{1,0:T(8,128)(2,1)S(1)} %get-tuple-element.51.agg_cols, bf16[768,768]{1,0:T(8,128)(2,1)S(1)} %get-tuple-element.59.agg_t, bf16[1408,128]{1,0:T(8,128)(2,1)S(1)} %collective-permute-done.17.refs_0_, ...), custom_call_target="tpu_custom_call" | custom-call | flops 905969664 | bytes 4939776 | tf_op jit(solution)/shard_map/pallas_call | solution.py:167
  74.0 1.7 %collective-permute-start.32 = (bf16[192,384]{1,0:T(8,128)(2,1)S(1)}, bf16[192,384]{1,0:T(8,128)(2,1)S(1)}, u32[]{:S(2)}, u32[]{:S(2)}) collective-permute-start(bf16[192,384]{1,0:T(8,128)(2,1)S(1)} %shard_map.58.refs_0_), channel_id=1, source_target_pairs={{0,4},{1,5},{2,6},{3,7},{4,0},{5,1},{6,2},{7,3},{8,12},{9,13},{10,... | collective-permute-start | bytes 442376 | tf_op jit(solution)/shard_map/ppermute | solution.py:478
  75.7 1.3 %collective-permute-start.24 = (bf16[352,128]{1,0:T(8,128)(2,1)S(1)}, bf16[352,128]{1,0:T(8,128)(2,1)S(1)}, u32[]{:S(2)}, u32[]{:S(2)}) collective-permute-start(bf16[352,128]{1,0:T(8,128)(2,1)S(1)} %get-tuple-element.63), channel_id=1, source_target_pairs={{16,0},{18,2},{20,4},{22,6},{17,1},{19,3},{21,5},{23,7}} | collective-permute-start | bytes 270344 | tf_op jit(solution)/shard_map/ppermute | solution.py:491
  77.2 1.0 collective-permute-start.33
  78.2 5.2 %collective-permute-done.24.refs_1_ = bf16[352,128]{1,0:T(8,128)(2,1)S(1)} collective-permute-done((bf16[352,128]{1,0:T(8,128)(2,1)S(1)}, bf16[352,128]{1,0:T(8,128)(2,1)S(1)}, u32[]{:S(2)}, u32[]{:S(2)}) %collective-permute-start.24) | collective-permute-done | bytes 90144 | tf_op jit(solution)/shard_map/ppermute | solution.py:491
  83.4 1.4 %collective-permute-start.27 = (bf16[352,128]{1,0:T(8,128)(2,1)S(1)}, bf16[352,128]{1,0:T(8,128)(2,1)S(1)}, u32[]{:S(2)}, u32[]{:S(2)}) collective-permute-start(bf16[352,128]{1,0:T(8,128)(2,1)S(1)} %shard_map.60.refs_0_), channel_id=1, source_target_pairs={{0,2},{1,3},{2,0},{3,1},{4,6},{5,7},{6,4},{7,5},{8,10},{9,11},{10,... | collective-permute-start | bytes 270344 | tf_op jit(solution)/shard_map/ppermute | solution.py:478
  85.2 1.7 %collective-permute-start.29 = (bf16[352,128]{1,0:T(8,128)(2,1)S(1)}, bf16[352,128]{1,0:T(8,128)(2,1)S(1)}, u32[]{:S(2)}, u32[]{:S(2)}) collective-permute-start(bf16[352,128]{1,0:T(8,128)(2,1)S(1)} %shard_map.60.refs_0_), channel_id=1, source_target_pairs={{0,6},{1,7},{2,4},{3,5},{4,2},{5,3},{6,0},{7,1},{8,14},{9,15},{10,... | collective-permute-start | bytes 270344 | tf_op jit(solution)/shard_map/ppermute | solution.py:478
  87.0 1.4 %shard_map.61.refs_0_ = f32[768,384]{1,0:T(8,128)S(1)} custom-call(f32[768,384]{1,0:T(8,128)S(1)} %shard_map.56.cov, bf16[2,768,384]{2,1,0:T(8,128)(2,1)S(1)} %get-tuple-element.67.mine.refs_0_, bf16[768,768]{1,0:T(8,128)(2,1)S(1)} %get-tuple-element.65.mine_t.refs_1_, bf16[768,768]{1,0:T(8,128)(2,1)S(1)} %get-tuple-element.66.right), custom_call_target="tpu_custom_call" | custom-call | flops 905969664 | bytes 5898240 | tf_op jit(solution)/shard_map/pallas_call | solution.py:167
  88.7 1.1 %collective-permute-done.28.refs_2_ = bf16[352,128]{1,0:T(8,128)(2,1)S(1)} collective-permute-done((bf16[352,128]{1,0:T(8,128)(2,1)S(1)}, bf16[352,128]{1,0:T(8,128)(2,1)S(1)}, u32[]{:S(2)}, u32[]{:S(2)}) %collective-permute-start.28) | collective-permute-done | bytes 90144 | tf_op jit(solution)/shard_map/ppermute | solution.py:478
  91.3 1.8 %shard_map.63 = (bf16[2,768,384]{2,1,0:T(8,128)(2,1)S(1)}, bf16[768,768]{1,0:T(8,128)(2,1)S(1)}) custom-call(bf16[2,768,384]{2,1,0:T(8,128)(2,1)S(1)} %get-tuple-element.67.mine.refs_0_, bf16[768,768]{1,0:T(8,128)(2,1)S(1)} %get-tuple-element.65.mine_t.refs_1_, bf16[768,384]{1,0:T(8,128)(2,1)S(1)} %shard_map.62.refs_2_, ...), custom_call_target="tpu_custom_call" | custom-call | flops 905969664 | bytes 5898240 | tf_op jit(solution)/shard_map/pallas_call | solution.py:167
  93.2 2.5 %shard_map.65 = f32[1,768,384]{2,1,0:T(8,128)} custom-call(f32[768,384]{1,0:T(8,128)S(1)} %shard_map.61.refs_0_, bf16[2,768,384]{2,1,0:T(8,128)(2,1)S(1)} %get-tuple-element.70.refs_1_.refs_0_, bf16[768,768]{1,0:T(8,128)(2,1)S(1)} %get-tuple-element.69.refs_2_, bf16[1408,128]{1,0:T(8,128)(2,1)S(1)} %shard_map.64.refs_3_, ...), custom_call_target="tpu_custom_call" | custom-call | flops 905969664 | bytes 5439488 | tf_op jit(solution)/shard_map/pallas_call | solution.py:167
  95.7 1.7 %shard_map.67 = bf16[1,768,384]{2,1,0:T(8,128)(2,1)} custom-call(bf16[2,768,384]{2,1,0:T(8,128)(2,1)S(1)} %get-tuple-element.70.refs_1_.refs_0_, bf16[768,384]{1,0:T(8,128)(2,1)S(1)} %shard_map.66.refs_1_, bf16[768,384]{1,0:T(8,128)(2,1)S(1)} %collective-permute-done.34.refs_2_), custom_call_target="tpu_custom_call" | custom-call | flops 452984832 | bytes 2949120 | tf_op jit(solution)/shard_map/pallas_call | solution.py:167
  (62 shorter events, 11.7 us)
Async XLA Ops:
  2.1 16.7 %collective-permute-start.2 = (bf16[768,384]{1,0:T(8,128)(2,1)S(1)}, bf16[768,384]{1,0:T(8,128)(2,1)S(1)}, u32[]{:S(2)}, u32[]{:S(2)}) collective-permute-start(bf16[768,384]{1,0:T(8,128)(2,1)S(1)} %convert_bitcast_fusion.refs_4_.refs_0_), channel_id=1, source_target_pairs={{0,4},{1,3},{2,6},{3,1},{4,0},{5,7},{6,2},{7,5},{8,12},{9,11},{10,... | collective-permute-start | bytes 1769480 | tf_op jit(solution)/shard_map/ppermute | solution.py:478
  5.2 13.7 %collective-permute-start.4 = (bf16[768,384]{1,0:T(8,128)(2,1)S(1)}, bf16[768,384]{1,0:T(8,128)(2,1)S(1)}, u32[]{:S(2)}, u32[]{:S(2)}) collective-permute-start(bf16[768,384]{1,0:T(8,128)(2,1)S(1)} %convert_bitcast_fusion.refs_4_.refs_0_), channel_id=1, source_target_pairs={{0,2},{1,5},{2,0},{3,7},{4,6},{5,1},{6,4},{7,3},{8,10},{9,13},{10,... | collective-permute-start | bytes 1769480 | tf_op jit(solution)/shard_map/ppermute | solution.py:478
  6.7 14.1 %collective-permute-start = (bf16[768,384]{1,0:T(8,128)(2,1)S(1)}, bf16[768,384]{1,0:T(8,128)(2,1)S(1)}, u32[]{:S(2)}, u32[]{:S(2)}) collective-permute-start(bf16[768,384]{1,0:T(8,128)(2,1)S(1)} %convert_element_type.10.refs_2_), channel_id=1, source_target_pairs={{1,0},{0,1},{3,2},{2,3},{5,4},{4,5},{7,6},{6,7},{9,8},{8,9},{11,10... | collective-permute-start | bytes 1769480 | tf_op jit(solution)/shard_map/ppermute | solution.py:467
  6.8 14.0 %collective-permute-start.1 = (bf16[768,384]{1,0:T(8,128)(2,1)S(1)}, bf16[768,384]{1,0:T(8,128)(2,1)S(1)}, u32[]{:S(2)}, u32[]{:S(2)}) collective-permute-start(bf16[768,384]{1,0:T(8,128)(2,1)S(1)} %convert_bitcast_fusion.refs_4_.refs_0_), channel_id=1, source_target_pairs={{1,0},{0,1},{3,2},{2,3},{5,4},{4,5},{7,6},{6,7},{9,8},{8,9},{11,10... | collective-permute-start | bytes 1769480 | tf_op jit(solution)/shard_map/ppermute | solution.py:467
  18.8 5.5 %collective-permute-start.3 = (bf16[768,384]{1,0:T(8,128)(2,1)S(1)}, bf16[768,384]{1,0:T(8,128)(2,1)S(1)}, u32[]{:S(2)}, u32[]{:S(2)}) collective-permute-start(bf16[768,384]{1,0:T(8,128)(2,1)S(1)} %collective-permute-done.2.refs_2_), channel_id=1, source_target_pairs={{1,0},{0,1},{3,2},{2,3},{5,4},{4,5},{7,6},{6,7},{9,8},{8,9},{11,10... | collective-permute-start | bytes 1769480 | tf_op jit(solution)/shard_map/ppermute | solution.py:467
  18.8 5.5 %collective-permute-start.5 = (bf16[768,384]{1,0:T(8,128)(2,1)S(1)}, bf16[768,384]{1,0:T(8,128)(2,1)S(1)}, u32[]{:S(2)}, u32[]{:S(2)}) collective-permute-start(bf16[768,384]{1,0:T(8,128)(2,1)S(1)} %collective-permute-done.4.refs_4_), channel_id=1, source_target_pairs={{1,0},{0,1},{3,2},{2,3},{5,4},{4,5},{7,6},{6,7},{9,8},{8,9},{11,10... | collective-permute-start | bytes 1769480 | tf_op jit(solution)/shard_map/ppermute | solution.py:467
  19.3 13.5 %collective-permute-start.6 = (bf16[768,384]{1,0:T(8,128)(2,1)S(1)}, bf16[768,384]{1,0:T(8,128)(2,1)S(1)}, u32[]{:S(2)}, u32[]{:S(2)}) collective-permute-start(bf16[768,384]{1,0:T(8,128)(2,1)S(1)} %collective-permute-done.2.refs_2_), channel_id=1, source_target_pairs={{0,2},{1,5},{2,0},{3,7},{4,6},{5,1},{6,4},{7,3},{8,10},{9,13},{10,... | collective-permute-start | bytes 1769480 | tf_op jit(solution)/shard_map/ppermute | solution.py:478
  22.6 10.3 %collective-permute-start.7 = (bf16[1408,128]{1,0:T(8,128)(2,1)S(1)}, bf16[1408,128]{1,0:T(8,128)(2,1)S(1)}, u32[]{:S(2)}, u32[]{:S(2)}) collective-permute-start(bf16[1408,128]{1,0:T(8,128)(2,1)S(1)} %get-tuple-element.42.refs_5_), channel_id=1, source_target_pairs={{0,4},{1,3},{2,6},{3,1},{4,0},{5,7},{6,2},{7,5},{8,12},{9,11},{10,... | collective-permute-start | bytes 1081352 | tf_op jit(solution)/shard_map/ppermute | solution.py:478
  33.0 13.4 %collective-permute-start.11 = (bf16[1408,128]{1,0:T(8,128)(2,1)S(1)}, bf16[1408,128]{1,0:T(8,128)(2,1)S(1)}, u32[]{:S(2)}, u32[]{:S(2)}) collective-permute-start(bf16[1408,128]{1,0:T(8,128)(2,1)S(1)} %get-tuple-element.42.refs_5_), channel_id=1, source_target_pairs={{0,2},{1,5},{2,0},{3,7},{4,6},{5,1},{6,4},{7,3},{8,10},{9,13},{10,... | collective-permute-start | bytes 1081352 | tf_op jit(solution)/shard_map/ppermute | solution.py:478
  34.6 13.0 %collective-permute-start.13 = (bf16[1408,128]{1,0:T(8,128)(2,1)S(1)}, bf16[1408,128]{1,0:T(8,128)(2,1)S(1)}, u32[]{:S(2)}, u32[]{:S(2)}) collective-permute-start(bf16[1408,128]{1,0:T(8,128)(2,1)S(1)} %collective-permute-done.7.refs_7_), channel_id=1, source_target_pairs={{0,2},{1,5},{2,0},{3,7},{4,6},{5,1},{6,4},{7,3},{8,10},{9,13},{10,... | collective-permute-start | bytes 1081352 | tf_op jit(solution)/shard_map/ppermute | solution.py:478
  37.4 8.5 %collective-permute-start.14 = (bf16[192,384]{1,0:T(8,128)(2,1)S(1)}, bf16[192,384]{1,0:T(8,128)(2,1)S(1)}, u32[]{:S(2)}, u32[]{:S(2)}) collective-permute-start(bf16[192,384]{1,0:T(8,128)(2,1)S(1)} %get-tuple-element.49), channel_id=1, source_target_pairs={{8,0},{10,2},{12,4},{14,6},{24,16},{26,18},{28,20},{30,22},{9,1},{... | collective-permute-start | bytes 442376 | tf_op jit(solution)/shard_map/ppermute | solution.py:491
  45.8 3.3 %collective-permute-start.9 = (bf16[1408,128]{1,0:T(8,128)(2,1)S(1)}, bf16[1408,128]{1,0:T(8,128)(2,1)S(1)}, u32[]{:S(2)}, u32[]{:S(2)}) collective-permute-start(bf16[1408,128]{1,0:T(8,128)(2,1)S(1)} %get-tuple-element.42.refs_5_), channel_id=1, source_target_pairs={{1,0},{0,1},{3,2},{2,3},{5,4},{4,5},{7,6},{6,7},{9,8},{8,9},{11,10... | collective-permute-start | bytes 1081352 | tf_op jit(solution)/shard_map/ppermute | solution.py:467
  46.3 4.2 %collective-permute-start.10 = (bf16[1408,128]{1,0:T(8,128)(2,1)S(1)}, bf16[1408,128]{1,0:T(8,128)(2,1)S(1)}, u32[]{:S(2)}, u32[]{:S(2)}) collective-permute-start(bf16[1408,128]{1,0:T(8,128)(2,1)S(1)} %collective-permute-done.7.refs_7_), channel_id=1, source_target_pairs={{1,0},{0,1},{3,2},{2,3},{5,4},{4,5},{7,6},{6,7},{9,8},{8,9},{11,10... | collective-permute-start | bytes 1081352 | tf_op jit(solution)/shard_map/ppermute | solution.py:467
  46.3 4.3 %collective-permute-start.12 = (bf16[1408,128]{1,0:T(8,128)(2,1)S(1)}, bf16[1408,128]{1,0:T(8,128)(2,1)S(1)}, u32[]{:S(2)}, u32[]{:S(2)}) collective-permute-start(bf16[1408,128]{1,0:T(8,128)(2,1)S(1)} %collective-permute-done.11.refs_9_), channel_id=1, source_target_pairs={{1,0},{0,1},{3,2},{2,3},{5,4},{4,5},{7,6},{6,7},{9,8},{8,9},{11,10... | collective-permute-start | bytes 1081352 | tf_op jit(solution)/shard_map/ppermute | solution.py:467
  47.5 3.1 %collective-permute-start.16 = (bf16[1408,128]{1,0:T(8,128)(2,1)S(1)}, bf16[1408,128]{1,0:T(8,128)(2,1)S(1)}, u32[]{:S(2)}, u32[]{:S(2)}) collective-permute-start(bf16[1408,128]{1,0:T(8,128)(2,1)S(1)} %collective-permute-done.13.refs_11_), channel_id=1, source_target_pairs={{1,0},{0,1},{3,2},{2,3},{5,4},{4,5},{7,6},{6,7},{9,8},{8,9},{11,10... | collective-permute-start | bytes 1081352 | tf_op jit(solution)/shard_map/ppermute | solution.py:467
  48.4 9.4 %collective-permute-start.18 = (bf16[192,384]{1,0:T(8,128)(2,1)S(1)}, bf16[192,384]{1,0:T(8,128)(2,1)S(1)}, u32[]{:S(2)}, u32[]{:S(2)}) collective-permute-start(bf16[192,384]{1,0:T(8,128)(2,1)S(1)} %shard_map.54), channel_id=1, source_target_pairs={{16,8},{18,10},{20,12},{22,14},{17,9},{19,11},{21,13},{23,15}} | collective-permute-start | bytes 442376 | tf_op jit(solution)/shard_map/ppermute | solution.py:491
  49.1 11.1 %collective-permute-start.19 = (bf16[192,384]{1,0:T(8,128)(2,1)S(1)}, bf16[192,384]{1,0:T(8,128)(2,1)S(1)}, u32[]{:S(2)}, u32[]{:S(2)}) collective-permute-start(bf16[192,384]{1,0:T(8,128)(2,1)S(1)} %shard_map.54), channel_id=1, source_target_pairs={{16,0},{18,2},{20,4},{22,6},{17,1},{19,3},{21,5},{23,7}} | collective-permute-start | bytes 442376 | tf_op jit(solution)/shard_map/ppermute | solution.py:491
  56.5 12.6 %collective-permute-start.17 = (bf16[1408,128]{1,0:T(8,128)(2,1)S(1)}, bf16[1408,128]{1,0:T(8,128)(2,1)S(1)}, u32[]{:S(2)}, u32[]{:S(2)}) collective-permute-start(bf16[1408,128]{1,0:T(8,128)(2,1)S(1)} %get-tuple-element.57), channel_id=1, source_target_pairs={{8,0},{10,2},{12,4},{14,6},{24,16},{26,18},{28,20},{30,22},{9,1},{... | collective-permute-start | bytes 1081352 | tf_op jit(solution)/shard_map/ppermute | solution.py:491
  60.2 8.8 %collective-permute-start.20 = (bf16[192,384]{1,0:T(8,128)(2,1)S(1)}, bf16[192,384]{1,0:T(8,128)(2,1)S(1)}, u32[]{:S(2)}, u32[]{:S(2)}) collective-permute-start(bf16[192,384]{1,0:T(8,128)(2,1)S(1)} %collective-permute-done.14.refs_0_), channel_id=1, source_target_pairs={{0,4},{1,5},{2,6},{3,7},{4,0},{5,1},{6,2},{7,3},{8,12},{9,13},{10,... | collective-permute-start | bytes 442376 | tf_op jit(solution)/shard_map/ppermute | solution.py:478
  61.8 7.2 %collective-permute-start.21 = (bf16[192,384]{1,0:T(8,128)(2,1)S(1)}, bf16[192,384]{1,0:T(8,128)(2,1)S(1)}, u32[]{:S(2)}, u32[]{:S(2)}) collective-permute-start(bf16[192,384]{1,0:T(8,128)(2,1)S(1)} %collective-permute-done.14.refs_0_), channel_id=1, source_target_pairs={{0,6},{1,7},{2,4},{3,5},{4,2},{5,3},{6,0},{7,1},{8,14},{9,15},{10,... | collective-permute-start | bytes 442376 | tf_op jit(solution)/shard_map/ppermute | solution.py:478
  69.1 7.9 %collective-permute-start.25 = (bf16[192,384]{1,0:T(8,128)(2,1)S(1)}, bf16[192,384]{1,0:T(8,128)(2,1)S(1)}, u32[]{:S(2)}, u32[]{:S(2)}) collective-permute-start(bf16[192,384]{1,0:T(8,128)(2,1)S(1)} %collective-permute-done.14.refs_0_), channel_id=1, source_target_pairs={{0,2},{1,3},{2,0},{3,1},{4,6},{5,7},{6,4},{7,5},{8,10},{9,11},{10,... | collective-permute-start | bytes 442376 | tf_op jit(solution)/shard_map/ppermute | solution.py:478
  72.4 4.8 %collective-permute-start.23 = (bf16[352,128]{1,0:T(8,128)(2,1)S(1)}, bf16[352,128]{1,0:T(8,128)(2,1)S(1)}, u32[]{:S(2)}, u32[]{:S(2)}) collective-permute-start(bf16[352,128]{1,0:T(8,128)(2,1)S(1)} %get-tuple-element.63), channel_id=1, source_target_pairs={{16,8},{18,10},{20,12},{22,14},{17,9},{19,11},{21,13},{23,15}} | collective-permute-start | bytes 270344 | tf_op jit(solution)/shard_map/ppermute | solution.py:491
  73.1 11.7 %collective-permute-start.31 = (bf16[192,384]{1,0:T(8,128)(2,1)S(1)}, bf16[192,384]{1,0:T(8,128)(2,1)S(1)}, u32[]{:S(2)}, u32[]{:S(2)}) collective-permute-start(bf16[192,384]{1,0:T(8,128)(2,1)S(1)} %shard_map.58.refs_0_), channel_id=1, source_target_pairs={{0,2},{1,3},{2,0},{3,1},{4,6},{5,7},{6,4},{7,5},{8,10},{9,11},{10,... | collective-permute-start | bytes 442376 | tf_op jit(solution)/shard_map/ppermute | solution.py:478
  74.0 11.2 %collective-permute-start.32 = (bf16[192,384]{1,0:T(8,128)(2,1)S(1)}, bf16[192,384]{1,0:T(8,128)(2,1)S(1)}, u32[]{:S(2)}, u32[]{:S(2)}) collective-permute-start(bf16[192,384]{1,0:T(8,128)(2,1)S(1)} %shard_map.58.refs_0_), channel_id=1, source_target_pairs={{0,4},{1,5},{2,6},{3,7},{4,0},{5,1},{6,2},{7,3},{8,12},{9,13},{10,... | collective-permute-start | bytes 442376 | tf_op jit(solution)/shard_map/ppermute | solution.py:478
  75.7 7.7 %collective-permute-start.24 = (bf16[352,128]{1,0:T(8,128)(2,1)S(1)}, bf16[352,128]{1,0:T(8,128)(2,1)S(1)}, u32[]{:S(2)}, u32[]{:S(2)}) collective-permute-start(bf16[352,128]{1,0:T(8,128)(2,1)S(1)} %get-tuple-element.63), channel_id=1, source_target_pairs={{16,0},{18,2},{20,4},{22,6},{17,1},{19,3},{21,5},{23,7}} | collective-permute-start | bytes 270344 | tf_op jit(solution)/shard_map/ppermute | solution.py:491
  77.1 14.2 %collective-permute-start.26 = (bf16[768,384]{1,0:T(8,128)(2,1)S(1)}, bf16[768,384]{1,0:T(8,128)(2,1)S(1)}, u32[]{:S(2)}, u32[]{:S(2)}) collective-permute-start(bf16[768,384]{1,0:T(8,128)(2,1)S(1)} %shard_map.62.refs_2_), channel_id=1, source_target_pairs={{1,0},{0,1},{3,2},{2,3},{5,4},{4,5},{7,6},{6,7},{9,8},{8,9},{11,10... | collective-permute-start | bytes 1769480 | tf_op jit(solution)/shard_map/ppermute | solution.py:467
  77.2 11.2 %collective-permute-start.33 = (bf16[192,384]{1,0:T(8,128)(2,1)S(1)}, bf16[192,384]{1,0:T(8,128)(2,1)S(1)}, u32[]{:S(2)}, u32[]{:S(2)}) collective-permute-start(bf16[192,384]{1,0:T(8,128)(2,1)S(1)} %shard_map.58.refs_0_), channel_id=1, source_target_pairs={{0,6},{1,7},{2,4},{3,5},{4,2},{5,3},{6,0},{7,1},{8,14},{9,15},{10,... | collective-permute-start | bytes 442376 | tf_op jit(solution)/shard_map/ppermute | solution.py:478
  83.4 5.3 %collective-permute-start.27 = (bf16[352,128]{1,0:T(8,128)(2,1)S(1)}, bf16[352,128]{1,0:T(8,128)(2,1)S(1)}, u32[]{:S(2)}, u32[]{:S(2)}) collective-permute-start(bf16[352,128]{1,0:T(8,128)(2,1)S(1)} %shard_map.60.refs_0_), channel_id=1, source_target_pairs={{0,2},{1,3},{2,0},{3,1},{4,6},{5,7},{6,4},{7,5},{8,10},{9,11},{10,... | collective-permute-start | bytes 270344 | tf_op jit(solution)/shard_map/ppermute | solution.py:478
  84.8 5.0 %collective-permute-start.28 = (bf16[352,128]{1,0:T(8,128)(2,1)S(1)}, bf16[352,128]{1,0:T(8,128)(2,1)S(1)}, u32[]{:S(2)}, u32[]{:S(2)}) collective-permute-start(bf16[352,128]{1,0:T(8,128)(2,1)S(1)} %shard_map.60.refs_0_), channel_id=1, source_target_pairs={{0,4},{1,5},{2,6},{3,7},{4,0},{5,1},{6,2},{7,3},{8,12},{9,13},{10,... | collective-permute-start | bytes 270344 | tf_op jit(solution)/shard_map/ppermute | solution.py:478
  85.2 5.4 %collective-permute-start.29 = (bf16[352,128]{1,0:T(8,128)(2,1)S(1)}, bf16[352,128]{1,0:T(8,128)(2,1)S(1)}, u32[]{:S(2)}, u32[]{:S(2)}) collective-permute-start(bf16[352,128]{1,0:T(8,128)(2,1)S(1)} %shard_map.60.refs_0_), channel_id=1, source_target_pairs={{0,6},{1,7},{2,4},{3,5},{4,2},{5,3},{6,0},{7,1},{8,14},{9,15},{10,... | collective-permute-start | bytes 270344 | tf_op jit(solution)/shard_map/ppermute | solution.py:478
  90.7 5.0 %collective-permute-start.34 = (bf16[768,384]{1,0:T(8,128)(2,1)S(1)}, bf16[768,384]{1,0:T(8,128)(2,1)S(1)}, u32[]{:S(2)}, u32[]{:S(2)}) collective-permute-start(bf16[768,384]{1,0:T(8,128)(2,1)S(1)} %shard_map.66.refs_1_), channel_id=1, source_target_pairs={{1,0},{0,1},{3,2},{2,3},{5,4},{4,5},{7,6},{6,7},{9,8},{8,9},{11,10... | collective-permute-start | bytes 1769480 | tf_op jit(solution)/shard_map/ppermute | solution.py:467
  90.7 2.5 %collective-permute-start.30 = (bf16[1408,128]{1,0:T(8,128)(2,1)S(1)}, bf16[1408,128]{1,0:T(8,128)(2,1)S(1)}, u32[]{:S(2)}, u32[]{:S(2)}) collective-permute-start(bf16[1408,128]{1,0:T(8,128)(2,1)S(1)} %shard_map.64.refs_3_), channel_id=1, source_target_pairs={{1,0},{0,1},{3,2},{2,3},{5,4},{4,5},{7,6},{6,7},{9,8},{8,9},{11,10... | collective-permute-start | bytes 1081352 | tf_op jit(solution)/shard_map/ppermute | solution.py:467
  (5 other events, 31.4 us)

commit v2 on v0

--- a/solution.py
+++ b/solution.py
@@ -569,7 +569,7 @@
     c_t, c01_t = call(
         turn_comp_kernel, [c_all, c_t, c01], [VMEM] * 3, [turned_bf, square_bf], [], 0, {1: 0}
     )
-    s_second, s_diag = after(s_second, c_share), after(s_diag, c_far)
+    s_second, s_diag = after(s_second, c_share), after(s_diag, c_t)
     s_pieces = [p for v in (base_bf, s_first, s_second, s_diag) for p in over_panels(v)]
     agg, agg_bf, s3, s23 = call(
         functools.partial(group_cov_kernel, n),
@@ -602,21 +602,26 @@
     out_cov = jax.ShapeDtypeStruct((1, nb, w), F32)
     out_comp = jax.ShapeDtypeStruct((1, nb, w), BF)
     sum_scratch = pltpu.VMEM((nb, w), F32)
+    c_far = after(c_far, agg_bf)
     s_got = across(agg_bf, 0)
     for bit in range(levels):
         to_last = bit + 2 == levels
         if bit + 1 == levels:
-            c_parts = over_panels(joined(in_group(c_far)))
+            c_blocks = in_group(c_far)
+            if bit:
+                c_blocks[0] = after(c_blocks[0], cov)
+            c_panel = joined(c_blocks)
+            if bit:
+                c_panel = after(c_panel, *s_blocks[1:])
+            c_parts = over_panels(c_panel)
             (prop,) = call(
                 functools.partial(last_comp_kernel, n, bit),
-                [mine, *c_parts],
+                [after(mine, s_got), *c_parts],
                 [VMEM] * (1 + n),
                 [out_comp],
                 [],
                 one,
             )
-            if bit:
-                s_got = joined(in_group(after(s_far, prop, cov)))
             s_parts = over_panels(s_got)
             (cov,) = call(
                 functools.partial(last_cov_kernel, n, bit),
@@ -636,7 +641,7 @@
                 [],
                 one // 4,
             )
-            c_blocks = in_group(after(c_far, agg_bf))
+            c_blocks = in_group(after(c_far, c_send))
             c_parts = over_panels(joined(c_blocks))
         else:
             c_blocks = in_group(c_far)
@@ -649,7 +654,7 @@
                 [],
                 n * one,
             )
-        c_far = after(across(c_send, bit + 1), mine)
+        c_far = across(c_send, bit + 1)
         new_mine, new_mine_t = call(
             functools.partial(mine_comp_kernel, n, bit),
             [after(mine, c_send), mine_t, *c_parts],
@@ -658,7 +663,7 @@
             [],
             n * one,
         )
-        s_parts = over_panels(after(s_got, mine, cov, *c_blocks[1:]))
+        s_parts = over_panels(after(s_got, mine, cov, c_far, c_blocks[2], c_blocks[3]))
         outs = call(
             functools.partial(pair_cov_kernel, n, to_last),
             [agg, agg_cols, agg_t, *s_parts],
@@ -671,7 +676,7 @@
         s_far = across(s_send, bit + 1)
         (cov,) = call(
             functools.partial(mine_cov_kernel, n, bit),
-            [cov, mine, mine_t, right],
+            [after(cov, s_far), mine, mine_t, right],
             [VMEM] * 4,
             [panel_f32],
             [],
@@ -680,8 +685,9 @@
         if not to_last:
             agg, agg_bf = outs[2:]
             agg_c, agg_t, agg_cols = new_agg_c, new_agg_t, new_cols
-        if not to_last:
-            s_got = joined(in_group(s_far))
+        s_blocks = in_group(s_far)
+        s_got = joined(s_blocks)
+        c_far = after(c_far, s_send)
         mine, mine_t = new_mine, new_mine_t
     return cov, prop
 

time: 101 us -> 97.5 us (0.965)
  waiting for transfers between devices: 38.5 us -> 37 us
  starting transfers between devices: 34.7 us -> 33.4 us
    ppermute x15, waiting for transfers between devices: 30 us -> 25.5 us  [swap(): return lax.ppermute(value, ('tm', 'panel'), pairs)]
    ppermute x6, waiting for transfers between devices: 6.07 us -> 10.3 us  [across(): got.append(lax.ppermute(x, 'tm', pairs))]
    ppermute x14, waiting for transfers between devices: 2.41 us -> 1.12 us  [over_panels(): lax.ppermute(x, 'panel', [((i + r) % n, i) for i in range(n)])]
    ppermute x15, starting transfers between devices: 24.1 us -> 22.9 us  [swap(): return lax.ppermute(value, ('tm', 'panel'), pairs)]
  transfers between devices with their start and end apart: 35 -> 35, of which waited for: 14 -> 9; matrix products, arithmetic and copies ran while one was open for 0% -> 0% of each run, Pallas kernels for 22% -> 23%
where the time goes in v2:
time: 97.5 us; the launch traced here: 97.2 us
  waiting for transfers between devices  37 us (38%)
  starting transfers between devices  33.4 us (34%)
  Pallas kernels  24.4 us (25%)
  other arithmetic  1.55 us (2%)
    ppermute x15, waiting for transfers between devices, swap(): return lax.ppermute(value, ('tm', 'panel'), pairs)  25.5 us
    pallas_call x18, Pallas kernels, call(): pl.pallas_call(kernel, in_specs=in_specs, out_specs=[VMEM] * len(outs), o...  24.4 us
    ppermute x15, starting transfers between devices, swap(): return lax.ppermute(value, ('tm', 'panel'), pairs)  22.9 us
    ppermute x6, waiting for transfers between devices, across(): got.append(lax.ppermute(x, 'tm', pairs))  10.3 us
    ppermute x6, starting transfers between devices, across(): got.append(lax.ppermute(x, 'tm', pairs))  6.66 us
    ppermute x14, starting transfers between devices, over_panels(): lax.ppermute(x, 'panel', [((i + r) % n, i) for i in range(n)])  3.84 us
  transfers between devices with their start and end apart: 35, of which 9 were waited for; matrix products, arithmetic and copies ran while one was open for 0% of the time, Pallas kernels for 23%

profile of v2, /device:TPU:0, one launch (start us, length us, event | category | flops | bytes accessed | tf_op | source)
XLA Modules:
  0.0 97.2 jit_solution(1748556574342857733)
XLA Ops:
  0.6 1.5 %convert_bitcast_fusion.refs_4_.refs_0_ = bf16[768,384]{1,0:T(8,128)(2,1)S(1)} fusion(f32[1,768,384]{2,1,0:T(8,128)} %param.4), kind=kLoop, calls=%fused_computation | loop fusion | flops 294912 | bytes 1769472 | tf_op jit(solution)/shard_map/convert_element_type | solution.py:532
  2.1 3.0 %collective-permute-start.2 = (bf16[768,384]{1,0:T(8,128)(2,1)S(1)}, bf16[768,384]{1,0:T(8,128)(2,1)S(1)}, u32[]{:S(2)}, u32[]{:S(2)}) collective-permute-start(bf16[768,384]{1,0:T(8,128)(2,1)S(1)} %convert_bitcast_fusion.refs_4_.refs_0_), channel_id=1, source_target_pairs={{0,4},{1,3},{2,6},{3,1},{4,0},{5,7},{6,2},{7,5},{8,12},{9,11},{10,... | collective-permute-start | bytes 1769480 | tf_op jit(solution)/shard_map/ppermute | solution.py:478
  5.2 1.5 %collective-permute-start.4 = (bf16[768,384]{1,0:T(8,128)(2,1)S(1)}, bf16[768,384]{1,0:T(8,128)(2,1)S(1)}, u32[]{:S(2)}, u32[]{:S(2)}) collective-permute-start(bf16[768,384]{1,0:T(8,128)(2,1)S(1)} %convert_bitcast_fusion.refs_4_.refs_0_), channel_id=1, source_target_pairs={{0,2},{1,5},{2,0},{3,7},{4,6},{5,1},{6,4},{7,3},{8,10},{9,13},{10,... | collective-permute-start | bytes 1769480 | tf_op jit(solution)/shard_map/ppermute | solution.py:478
  7.3 11.5 %collective-permute-done.2.refs_2_ = bf16[768,384]{1,0:T(8,128)(2,1)S(1)} collective-permute-done((bf16[768,384]{1,0:T(8,128)(2,1)S(1)}, bf16[768,384]{1,0:T(8,128)(2,1)S(1)}, u32[]{:S(2)}, u32[]{:S(2)}) %collective-permute-start.2) | collective-permute-done | bytes 589856 | tf_op jit(solution)/shard_map/ppermute | solution.py:478
  19.3 1.5 %collective-permute-start.6 = (bf16[768,384]{1,0:T(8,128)(2,1)S(1)}, bf16[768,384]{1,0:T(8,128)(2,1)S(1)}, u32[]{:S(2)}, u32[]{:S(2)}) collective-permute-start(bf16[768,384]{1,0:T(8,128)(2,1)S(1)} %collective-permute-done.2.refs_2_), channel_id=1, source_target_pairs={{0,2},{1,5},{2,0},{3,7},{4,6},{5,1},{6,4},{7,3},{8,10},{9,13},{10,... | collective-permute-start | bytes 1769480 | tf_op jit(solution)/shard_map/ppermute | solution.py:478
  20.8 1.7 %shard_map.50 = (f32[768,384]{1,0:T(8,128)S(1)}, bf16[1408,128]{1,0:T(8,128)(2,1)S(1)}) custom-call(f32[768,384]{1,0:T(8,128)S(1)} %bitcast.4, f32[768,768]{1,0:T(8,128)S(1)} %copy-done.1, bf16[768,384]{1,0:T(8,128)(2,1)S(1)} %convert_element_type.10.refs_2_, bf16[768,384]{1,0:T(8,128)(2,1)S(1)} %collective-permute-done.refs_3_, ...), custom_call_target="tpu_custom_call" | custom-call | flops 905969664 | bytes 7438336 | tf_op jit(solution)/shard_map/pallas_call | solution.py:167
  22.6 1.8 %collective-permute-start.7 = (bf16[1408,128]{1,0:T(8,128)(2,1)S(1)}, bf16[1408,128]{1,0:T(8,128)(2,1)S(1)}, u32[]{:S(2)}, u32[]{:S(2)}) collective-permute-start(bf16[1408,128]{1,0:T(8,128)(2,1)S(1)} %get-tuple-element.43.refs_5_), channel_id=1, source_target_pairs={{0,4},{1,3},{2,6},{3,1},{4,0},{5,7},{6,2},{7,5},{8,12},{9,11},{10,... | collective-permute-start | bytes 1081352 | tf_op jit(solution)/shard_map/ppermute | solution.py:478
  24.3 1.9 %shard_map.51 = (bf16[4,2,768,384]{3,2,1,0:T(8,128)(2,1)S(1)}, bf16[4,768,768]{2,1,0:T(8,128)(2,1)S(1)}, bf16[768,768]{1,0:T(8,128)(2,1)S(1)}) custom-call(bf16[768,384]{1,0:T(8,128)(2,1)S(1)} %convert_bitcast_fusion.refs_4_.refs_0_, bf16[768,384]{1,0:T(8,128)(2,1)S(1)} %collective-permute-done.1.refs_5_.refs_1_, ...), custom_call_target="tpu_custom_call" | custom-call | flops 905969664 | bytes 14155776 | tf_op jit(solution)/shard_map/pallas_call | solution.py:167
  26.2 6.6 %collective-permute-done.7.refs_7_ = bf16[1408,128]{1,0:T(8,128)(2,1)S(1)} collective-permute-done((bf16[1408,128]{1,0:T(8,128)(2,1)S(1)}, bf16[1408,128]{1,0:T(8,128)(2,1)S(1)}, u32[]{:S(2)}, u32[]{:S(2)}) %collective-permute-start.7) | collective-permute-done | bytes 360480 | tf_op jit(solution)/shard_map/ppermute | solution.py:478
  33.0 1.6 %collective-permute-start.11 = (bf16[1408,128]{1,0:T(8,128)(2,1)S(1)}, bf16[1408,128]{1,0:T(8,128)(2,1)S(1)}, u32[]{:S(2)}, u32[]{:S(2)}) collective-permute-start(bf16[1408,128]{1,0:T(8,128)(2,1)S(1)} %get-tuple-element.43.refs_5_), channel_id=1, source_target_pairs={{0,2},{1,5},{2,0},{3,7},{4,6},{5,1},{6,4},{7,3},{8,10},{9,13},{10,... | collective-permute-start | bytes 1081352 | tf_op jit(solution)/shard_map/ppermute | solution.py:478
  35.8 2.3 %shard_map.52 = (bf16[4,2,768,384]{3,2,1,0:T(8,128)(2,1)S(1)}, bf16[2,768,384]{2,1,0:T(8,128)(2,1)S(1)}, bf16[768,768]{1,0:T(8,128)(2,1)S(1)}, bf16[768,384]{1,0:T(8,128)(2,1)S(1)}, bf16[192,384]{1,0:T(8,128)(2,1)S(1)}) custom-call(bf16[4,2,768,384]{3,2,1,0:T(8,128)(2,1)S(1)} %get-tuple-element.41.refs_0_, ...), custom_call_target="tpu_custom_call", output_to_operand_aliasing={{0}: (0, {})} | custom-call | flops 1811939328 | bytes 14893056 | tf_op jit(solution)/shard_map/pallas_call | solution.py:167
  38.2 2.2 %collective-permute-done.11.refs_9_ = bf16[1408,128]{1,0:T(8,128)(2,1)S(1)} collective-permute-done((bf16[1408,128]{1,0:T(8,128)(2,1)S(1)}, bf16[1408,128]{1,0:T(8,128)(2,1)S(1)}, u32[]{:S(2)}, u32[]{:S(2)}) %collective-permute-start.11) | collective-permute-done | bytes 360480 | tf_op jit(solution)/shard_map/ppermute | solution.py:478
  41.6 2.7 %collective-permute-done.13.refs_11_ = bf16[1408,128]{1,0:T(8,128)(2,1)S(1)} collective-permute-done((bf16[1408,128]{1,0:T(8,128)(2,1)S(1)}, bf16[1408,128]{1,0:T(8,128)(2,1)S(1)}, u32[]{:S(2)}, u32[]{:S(2)}) %collective-permute-start.13) | collective-permute-done | bytes 360480 | tf_op jit(solution)/shard_map/ppermute | solution.py:478
  44.5 1.5 %collective-permute-start.16 = (bf16[192,384]{1,0:T(8,128)(2,1)S(1)}, bf16[192,384]{1,0:T(8,128)(2,1)S(1)}, u32[]{:S(2)}, u32[]{:S(2)}) collective-permute-start(bf16[192,384]{1,0:T(8,128)(2,1)S(1)} %get-tuple-element.50), channel_id=1, source_target_pairs={{8,0},{10,2},{12,4},{14,6},{24,16},{26,18},{28,20},{30,22},{9,1},{... | collective-permute-start | bytes 442376 | tf_op jit(solution)/shard_map/ppermute | solution.py:491
  46.0 5.9 %shard_map.54 = (f32[768,384]{1,0:T(8,128)S(1)}, bf16[1408,128]{1,0:T(8,128)(2,1)S(1)}, bf16[768,768]{1,0:T(8,128)(2,1)S(1)}, bf16[768,768]{1,0:T(8,128)(2,1)S(1)}) custom-call(f32[768,384]{1,0:T(8,128)S(1)} %get-tuple-element.40.refs_0_.base, bf16[4,2,768,384]{3,2,1,0:T(8,128)(2,1)S(1)} %get-tuple-element.45.c.refs_1_, ...), custom_call_target="tpu_custom_call" | custom-call | flops 3623878656 | bytes 19759104 | tf_op jit(solution)/shard_map/pallas_call | solution.py:167
  51.9 1.3 %collective-permute-start.15 = (bf16[1408,128]{1,0:T(8,128)(2,1)S(1)}, bf16[1408,128]{1,0:T(8,128)(2,1)S(1)}, u32[]{:S(2)}, u32[]{:S(2)}) collective-permute-start(bf16[1408,128]{1,0:T(8,128)(2,1)S(1)} %get-tuple-element.58), channel_id=1, source_target_pairs={{8,0},{10,2},{12,4},{14,6},{24,16},{26,18},{28,20},{30,22},{9,1},{... | collective-permute-start | bytes 1081352 | tf_op jit(solution)/shard_map/ppermute | solution.py:491
  55.6 1.3 %collective-permute-start.19 = (bf16[192,384]{1,0:T(8,128)(2,1)S(1)}, bf16[192,384]{1,0:T(8,128)(2,1)S(1)}, u32[]{:S(2)}, u32[]{:S(2)}) collective-permute-start(bf16[192,384]{1,0:T(8,128)(2,1)S(1)} %shard_map.57), channel_id=1, source_target_pairs={{16,0},{18,2},{20,4},{22,6},{17,1},{19,3},{21,5},{23,7}} | collective-permute-start | bytes 442376 | tf_op jit(solution)/shard_map/ppermute | solution.py:491
  56.9 3.0 %collective-permute-start.20 = (bf16[192,384]{1,0:T(8,128)(2,1)S(1)}, bf16[192,384]{1,0:T(8,128)(2,1)S(1)}, u32[]{:S(2)}, u32[]{:S(2)}) collective-permute-start(bf16[192,384]{1,0:T(8,128)(2,1)S(1)} %collective-permute-done.16.refs_0_), channel_id=1, source_target_pairs={{0,4},{1,5},{2,6},{3,7},{4,0},{5,1},{6,2},{7,3},{8,12},{9,13},{10,... | collective-permute-start | bytes 442376 | tf_op jit(solution)/shard_map/ppermute | solution.py:478
  60.4 2.3 %shard_map.56 = (bf16[2,768,384]{2,1,0:T(8,128)(2,1)}, bf16[768,768]{1,0:T(8,128)(2,1)S(1)}, bf16[2,768,384]{2,1,0:T(8,128)(2,1)S(1)}, bf16[768,768]{1,0:T(8,128)(2,1)S(1)}) custom-call(bf16[4,2,768,384]{3,2,1,0:T(8,128)(2,1)S(1)} %get-tuple-element.45.c.refs_1_, bf16[2,768,384]{2,1,0:T(8,128)(2,1)S(1)} %get-tuple-element.47.c01.refs_3_, ...), custom_call_target="tpu_custom_call" | custom-call | flops 1811939328 | bytes 11796480 | tf_op jit(solution)/shard_map/pallas_call | solution.py:167
  62.8 5.4 %collective-permute-done.19.refs_1_ = bf16[192,384]{1,0:T(8,128)(2,1)S(1)} collective-permute-done((bf16[192,384]{1,0:T(8,128)(2,1)S(1)}, bf16[192,384]{1,0:T(8,128)(2,1)S(1)}, u32[]{:S(2)}, u32[]{:S(2)}) %collective-permute-start.19) | collective-permute-done | bytes 147488 | tf_op jit(solution)/shard_map/ppermute | solution.py:491
  68.3 1.8 %collective-permute-start.25 = (bf16[192,384]{1,0:T(8,128)(2,1)S(1)}, bf16[192,384]{1,0:T(8,128)(2,1)S(1)}, u32[]{:S(2)}, u32[]{:S(2)}) collective-permute-start(bf16[192,384]{1,0:T(8,128)(2,1)S(1)} %collective-permute-done.16.refs_0_), channel_id=1, source_target_pairs={{0,2},{1,3},{2,0},{3,1},{4,6},{5,7},{6,4},{7,5},{8,10},{9,11},{10,... | collective-permute-start | bytes 442376 | tf_op jit(solution)/shard_map/ppermute | solution.py:478
  70.2 1.6 %shard_map.59 = (bf16[352,128]{1,0:T(8,128)(2,1)S(1)}, bf16[768,768]{1,0:T(8,128)(2,1)S(1)}) custom-call(f32[768,384]{1,0:T(8,128)S(1)} %get-tuple-element.53.agg, bf16[768,384]{1,0:T(8,128)(2,1)S(1)} %get-tuple-element.56.agg_cols, bf16[768,768]{1,0:T(8,128)(2,1)S(1)} %get-tuple-element.60.agg_t, bf16[1408,128]{1,0:T(8,128)(2,1)S(1)} %collective-permute-done.15.refs_0_, ...), custom_call_target="tpu_custom_call" | custom-call | flops 905969664 | bytes 4939776 | tf_op jit(solution)/shard_map/pallas_call | solution.py:167
  72.5 1.7 %collective-permute-start.31 = (bf16[192,384]{1,0:T(8,128)(2,1)S(1)}, bf16[192,384]{1,0:T(8,128)(2,1)S(1)}, u32[]{:S(2)}, u32[]{:S(2)}) collective-permute-start(bf16[192,384]{1,0:T(8,128)(2,1)S(1)} %shard_map.58.refs_0_), channel_id=1, source_target_pairs={{0,2},{1,3},{2,0},{3,1},{4,6},{5,7},{6,4},{7,5},{8,10},{9,11},{10,... | collective-permute-start | bytes 442376 | tf_op jit(solution)/shard_map/ppermute | solution.py:478
  74.1 1.4 %collective-permute-start.32 = (bf16[192,384]{1,0:T(8,128)(2,1)S(1)}, bf16[192,384]{1,0:T(8,128)(2,1)S(1)}, u32[]{:S(2)}, u32[]{:S(2)}) collective-permute-start(bf16[192,384]{1,0:T(8,128)(2,1)S(1)} %shard_map.58.refs_0_), channel_id=1, source_target_pairs={{0,4},{1,5},{2,6},{3,7},{4,0},{5,1},{6,2},{7,3},{8,12},{9,13},{10,... | collective-permute-start | bytes 442376 | tf_op jit(solution)/shard_map/ppermute | solution.py:478
  78.1 4.9 %collective-permute-done.24.refs_1_ = bf16[352,128]{1,0:T(8,128)(2,1)S(1)} collective-permute-done((bf16[352,128]{1,0:T(8,128)(2,1)S(1)}, bf16[352,128]{1,0:T(8,128)(2,1)S(1)}, u32[]{:S(2)}, u32[]{:S(2)}) %collective-permute-start.24) | collective-permute-done | bytes 90144 | tf_op jit(solution)/shard_map/ppermute | solution.py:491
  83.0 1.7 %collective-permute-start.27 = (bf16[352,128]{1,0:T(8,128)(2,1)S(1)}, bf16[352,128]{1,0:T(8,128)(2,1)S(1)}, u32[]{:S(2)}, u32[]{:S(2)}) collective-permute-start(bf16[352,128]{1,0:T(8,128)(2,1)S(1)} %shard_map.60.refs_0_), channel_id=1, source_target_pairs={{0,2},{1,3},{2,0},{3,1},{4,6},{5,7},{6,4},{7,5},{8,10},{9,11},{10,... | collective-permute-start | bytes 270344 | tf_op jit(solution)/shard_map/ppermute | solution.py:478
  85.0 1.6 %collective-permute-start.29 = (bf16[352,128]{1,0:T(8,128)(2,1)S(1)}, bf16[352,128]{1,0:T(8,128)(2,1)S(1)}, u32[]{:S(2)}, u32[]{:S(2)}) collective-permute-start(bf16[352,128]{1,0:T(8,128)(2,1)S(1)} %shard_map.60.refs_0_), channel_id=1, source_target_pairs={{0,6},{1,7},{2,4},{3,5},{4,2},{5,3},{6,0},{7,1},{8,14},{9,15},{10,... | collective-permute-start | bytes 270344 | tf_op jit(solution)/shard_map/ppermute | solution.py:478
  86.6 1.4 %shard_map.61.refs_0_ = f32[768,384]{1,0:T(8,128)S(1)} custom-call(f32[768,384]{1,0:T(8,128)S(1)} %shard_map.55.cov, bf16[2,768,384]{2,1,0:T(8,128)(2,1)S(1)} %get-tuple-element.69.mine.refs_0_, bf16[768,768]{1,0:T(8,128)(2,1)S(1)} %get-tuple-element.67.mine_t.refs_1_, bf16[768,768]{1,0:T(8,128)(2,1)S(1)} %get-tuple-element.68.right), custom_call_target="tpu_custom_call" | custom-call | flops 905969664 | bytes 5898240 | tf_op jit(solution)/shard_map/pallas_call | solution.py:167
  88.1 2.5 %collective-permute-done.28.refs_2_ = bf16[352,128]{1,0:T(8,128)(2,1)S(1)} collective-permute-done((bf16[352,128]{1,0:T(8,128)(2,1)S(1)}, bf16[352,128]{1,0:T(8,128)(2,1)S(1)}, u32[]{:S(2)}, u32[]{:S(2)}) %collective-permute-start.28) | collective-permute-done | bytes 90144 | tf_op jit(solution)/shard_map/ppermute | solution.py:478
  91.1 1.8 %shard_map.63 = (bf16[2,768,384]{2,1,0:T(8,128)(2,1)S(1)}, bf16[768,768]{1,0:T(8,128)(2,1)S(1)}) custom-call(bf16[2,768,384]{2,1,0:T(8,128)(2,1)S(1)} %get-tuple-element.69.mine.refs_0_, bf16[768,768]{1,0:T(8,128)(2,1)S(1)} %get-tuple-element.67.mine_t.refs_1_, bf16[768,384]{1,0:T(8,128)(2,1)S(1)} %shard_map.62.refs_2_, ...), custom_call_target="tpu_custom_call" | custom-call | flops 905969664 | bytes 5898240 | tf_op jit(solution)/shard_map/pallas_call | solution.py:167
  93.0 2.5 %shard_map.65 = f32[1,768,384]{2,1,0:T(8,128)} custom-call(f32[768,384]{1,0:T(8,128)S(1)} %shard_map.61.refs_0_, bf16[2,768,384]{2,1,0:T(8,128)(2,1)S(1)} %get-tuple-element.72.refs_1_.refs_0_, bf16[768,768]{1,0:T(8,128)(2,1)S(1)} %get-tuple-element.71.refs_2_, bf16[1408,128]{1,0:T(8,128)(2,1)S(1)} %shard_map.64.refs_3_, ...), custom_call_target="tpu_custom_call" | custom-call | flops 905969664 | bytes 5439488 | tf_op jit(solution)/shard_map/pallas_call | solution.py:167
  95.6 1.7 %shard_map.67 = bf16[1,768,384]{2,1,0:T(8,128)(2,1)} custom-call(bf16[2,768,384]{2,1,0:T(8,128)(2,1)S(1)} %get-tuple-element.72.refs_1_.refs_0_, bf16[768,384]{1,0:T(8,128)(2,1)S(1)} %shard_map.66.refs_1_, bf16[768,384]{1,0:T(8,128)(2,1)S(1)} %collective-permute-done.34.refs_2_), custom_call_target="tpu_custom_call" | custom-call | flops 452984832 | bytes 2949120 | tf_op jit(solution)/shard_map/pallas_call | solution.py:167
  (62 shorter events, 11.2 us)
Async XLA Ops:
  2.1 16.7 %collective-permute-start.2 = (bf16[768,384]{1,0:T(8,128)(2,1)S(1)}, bf16[768,384]{1,0:T(8,128)(2,1)S(1)}, u32[]{:S(2)}, u32[]{:S(2)}) collective-permute-start(bf16[768,384]{1,0:T(8,128)(2,1)S(1)} %convert_bitcast_fusion.refs_4_.refs_0_), channel_id=1, source_target_pairs={{0,4},{1,3},{2,6},{3,1},{4,0},{5,7},{6,2},{7,5},{8,12},{9,11},{10,... | collective-permute-start | bytes 1769480 | tf_op jit(solution)/shard_map/ppermute | solution.py:478
  5.2 13.7 %collective-permute-start.4 = (bf16[768,384]{1,0:T(8,128)(2,1)S(1)}, bf16[768,384]{1,0:T(8,128)(2,1)S(1)}, u32[]{:S(2)}, u32[]{:S(2)}) collective-permute-start(bf16[768,384]{1,0:T(8,128)(2,1)S(1)} %convert_bitcast_fusion.refs_4_.refs_0_), channel_id=1, source_target_pairs={{0,2},{1,5},{2,0},{3,7},{4,6},{5,1},{6,4},{7,3},{8,10},{9,13},{10,... | collective-permute-start | bytes 1769480 | tf_op jit(solution)/shard_map/ppermute | solution.py:478
  6.7 14.1 %collective-permute-start = (bf16[768,384]{1,0:T(8,128)(2,1)S(1)}, bf16[768,384]{1,0:T(8,128)(2,1)S(1)}, u32[]{:S(2)}, u32[]{:S(2)}) collective-permute-start(bf16[768,384]{1,0:T(8,128)(2,1)S(1)} %convert_element_type.10.refs_2_), channel_id=1, source_target_pairs={{1,0},{0,1},{3,2},{2,3},{5,4},{4,5},{7,6},{6,7},{9,8},{8,9},{11,10... | collective-permute-start | bytes 1769480 | tf_op jit(solution)/shard_map/ppermute | solution.py:467
  6.8 14.0 %collective-permute-start.1 = (bf16[768,384]{1,0:T(8,128)(2,1)S(1)}, bf16[768,384]{1,0:T(8,128)(2,1)S(1)}, u32[]{:S(2)}, u32[]{:S(2)}) collective-permute-start(bf16[768,384]{1,0:T(8,128)(2,1)S(1)} %convert_bitcast_fusion.refs_4_.refs_0_), channel_id=1, source_target_pairs={{1,0},{0,1},{3,2},{2,3},{5,4},{4,5},{7,6},{6,7},{9,8},{8,9},{11,10... | collective-permute-start | bytes 1769480 | tf_op jit(solution)/shard_map/ppermute | solution.py:467
  18.8 5.5 %collective-permute-start.3 = (bf16[768,384]{1,0:T(8,128)(2,1)S(1)}, bf16[768,384]{1,0:T(8,128)(2,1)S(1)}, u32[]{:S(2)}, u32[]{:S(2)}) collective-permute-start(bf16[768,384]{1,0:T(8,128)(2,1)S(1)} %collective-permute-done.2.refs_2_), channel_id=1, source_target_pairs={{1,0},{0,1},{3,2},{2,3},{5,4},{4,5},{7,6},{6,7},{9,8},{8,9},{11,10... | collective-permute-start | bytes 1769480 | tf_op jit(solution)/shard_map/ppermute | solution.py:467
  18.8 5.5 %collective-permute-start.5 = (bf16[768,384]{1,0:T(8,128)(2,1)S(1)}, bf16[768,384]{1,0:T(8,128)(2,1)S(1)}, u32[]{:S(2)}, u32[]{:S(2)}) collective-permute-start(bf16[768,384]{1,0:T(8,128)(2,1)S(1)} %collective-permute-done.4.refs_4_), channel_id=1, source_target_pairs={{1,0},{0,1},{3,2},{2,3},{5,4},{4,5},{7,6},{6,7},{9,8},{8,9},{11,10... | collective-permute-start | bytes 1769480 | tf_op jit(solution)/shard_map/ppermute | solution.py:467
  19.3 13.5 %collective-permute-start.6 = (bf16[768,384]{1,0:T(8,128)(2,1)S(1)}, bf16[768,384]{1,0:T(8,128)(2,1)S(1)}, u32[]{:S(2)}, u32[]{:S(2)}) collective-permute-start(bf16[768,384]{1,0:T(8,128)(2,1)S(1)} %collective-permute-done.2.refs_2_), channel_id=1, source_target_pairs={{0,2},{1,5},{2,0},{3,7},{4,6},{5,1},{6,4},{7,3},{8,10},{9,13},{10,... | collective-permute-start | bytes 1769480 | tf_op jit(solution)/shard_map/ppermute | solution.py:478
  22.6 10.3 %collective-permute-start.7 = (bf16[1408,128]{1,0:T(8,128)(2,1)S(1)}, bf16[1408,128]{1,0:T(8,128)(2,1)S(1)}, u32[]{:S(2)}, u32[]{:S(2)}) collective-permute-start(bf16[1408,128]{1,0:T(8,128)(2,1)S(1)} %get-tuple-element.43.refs_5_), channel_id=1, source_target_pairs={{0,4},{1,3},{2,6},{3,1},{4,0},{5,7},{6,2},{7,5},{8,12},{9,11},{10,... | collective-permute-start | bytes 1081352 | tf_op jit(solution)/shard_map/ppermute | solution.py:478
  32.9 3.0 %collective-permute-start.8 = (bf16[768,384]{1,0:T(8,128)(2,1)S(1)}, bf16[768,384]{1,0:T(8,128)(2,1)S(1)}, u32[]{:S(2)}, u32[]{:S(2)}) collective-permute-start(bf16[768,384]{1,0:T(8,128)(2,1)S(1)} %collective-permute-done.6.refs_2_), channel_id=1, source_target_pairs={{1,0},{0,1},{3,2},{2,3},{5,4},{4,5},{7,6},{6,7},{9,8},{8,9},{11,10... | collective-permute-start | bytes 1769480 | tf_op jit(solution)/shard_map/ppermute | solution.py:467
  33.0 7.4 %collective-permute-start.11 = (bf16[1408,128]{1,0:T(8,128)(2,1)S(1)}, bf16[1408,128]{1,0:T(8,128)(2,1)S(1)}, u32[]{:S(2)}, u32[]{:S(2)}) collective-permute-start(bf16[1408,128]{1,0:T(8,128)(2,1)S(1)} %get-tuple-element.43.refs_5_), channel_id=1, source_target_pairs={{0,2},{1,5},{2,0},{3,7},{4,6},{5,1},{6,4},{7,3},{8,10},{9,13},{10,... | collective-permute-start | bytes 1081352 | tf_op jit(solution)/shard_map/ppermute | solution.py:478
  34.6 9.7 %collective-permute-start.13 = (bf16[1408,128]{1,0:T(8,128)(2,1)S(1)}, bf16[1408,128]{1,0:T(8,128)(2,1)S(1)}, u32[]{:S(2)}, u32[]{:S(2)}) collective-permute-start(bf16[1408,128]{1,0:T(8,128)(2,1)S(1)} %collective-permute-done.7.refs_7_), channel_id=1, source_target_pairs={{0,2},{1,5},{2,0},{3,7},{4,6},{5,1},{6,4},{7,3},{8,10},{9,13},{10,... | collective-permute-start | bytes 1081352 | tf_op jit(solution)/shard_map/ppermute | solution.py:478
  35.0 10.9 %collective-permute-start.9 = (bf16[1408,128]{1,0:T(8,128)(2,1)S(1)}, bf16[1408,128]{1,0:T(8,128)(2,1)S(1)}, u32[]{:S(2)}, u32[]{:S(2)}) collective-permute-start(bf16[1408,128]{1,0:T(8,128)(2,1)S(1)} %get-tuple-element.43.refs_5_), channel_id=1, source_target_pairs={{1,0},{0,1},{3,2},{2,3},{5,4},{4,5},{7,6},{6,7},{9,8},{8,9},{11,10... | collective-permute-start | bytes 1081352 | tf_op jit(solution)/shard_map/ppermute | solution.py:467
  35.8 10.1 %collective-permute-start.10 = (bf16[1408,128]{1,0:T(8,128)(2,1)S(1)}, bf16[1408,128]{1,0:T(8,128)(2,1)S(1)}, u32[]{:S(2)}, u32[]{:S(2)}) collective-permute-start(bf16[1408,128]{1,0:T(8,128)(2,1)S(1)} %collective-permute-done.7.refs_7_), channel_id=1, source_target_pairs={{1,0},{0,1},{3,2},{2,3},{5,4},{4,5},{7,6},{6,7},{9,8},{8,9},{11,10... | collective-permute-start | bytes 1081352 | tf_op jit(solution)/shard_map/ppermute | solution.py:467
  40.4 5.6 %collective-permute-start.12 = (bf16[1408,128]{1,0:T(8,128)(2,1)S(1)}, bf16[1408,128]{1,0:T(8,128)(2,1)S(1)}, u32[]{:S(2)}, u32[]{:S(2)}) collective-permute-start(bf16[1408,128]{1,0:T(8,128)(2,1)S(1)} %collective-permute-done.11.refs_9_), channel_id=1, source_target_pairs={{1,0},{0,1},{3,2},{2,3},{5,4},{4,5},{7,6},{6,7},{9,8},{8,9},{11,10... | collective-permute-start | bytes 1081352 | tf_op jit(solution)/shard_map/ppermute | solution.py:467
  44.5 8.7 %collective-permute-start.16 = (bf16[192,384]{1,0:T(8,128)(2,1)S(1)}, bf16[192,384]{1,0:T(8,128)(2,1)S(1)}, u32[]{:S(2)}, u32[]{:S(2)}) collective-permute-start(bf16[192,384]{1,0:T(8,128)(2,1)S(1)} %get-tuple-element.50), channel_id=1, source_target_pairs={{8,0},{10,2},{12,4},{14,6},{24,16},{26,18},{28,20},{30,22},{9,1},{... | collective-permute-start | bytes 442376 | tf_op jit(solution)/shard_map/ppermute | solution.py:491
  51.9 16.4 %collective-permute-start.15 = (bf16[1408,128]{1,0:T(8,128)(2,1)S(1)}, bf16[1408,128]{1,0:T(8,128)(2,1)S(1)}, u32[]{:S(2)}, u32[]{:S(2)}) collective-permute-start(bf16[1408,128]{1,0:T(8,128)(2,1)S(1)} %get-tuple-element.58), channel_id=1, source_target_pairs={{8,0},{10,2},{12,4},{14,6},{24,16},{26,18},{28,20},{30,22},{9,1},{... | collective-permute-start | bytes 1081352 | tf_op jit(solution)/shard_map/ppermute | solution.py:491
  54.9 7.8 %collective-permute-start.18 = (bf16[192,384]{1,0:T(8,128)(2,1)S(1)}, bf16[192,384]{1,0:T(8,128)(2,1)S(1)}, u32[]{:S(2)}, u32[]{:S(2)}) collective-permute-start(bf16[192,384]{1,0:T(8,128)(2,1)S(1)} %shard_map.57), channel_id=1, source_target_pairs={{16,8},{18,10},{20,12},{22,14},{17,9},{19,11},{21,13},{23,15}} | collective-permute-start | bytes 442376 | tf_op jit(solution)/shard_map/ppermute | solution.py:491
  55.6 12.6 %collective-permute-start.19 = (bf16[192,384]{1,0:T(8,128)(2,1)S(1)}, bf16[192,384]{1,0:T(8,128)(2,1)S(1)}, u32[]{:S(2)}, u32[]{:S(2)}) collective-permute-start(bf16[192,384]{1,0:T(8,128)(2,1)S(1)} %shard_map.57), channel_id=1, source_target_pairs={{16,0},{18,2},{20,4},{22,6},{17,1},{19,3},{21,5},{23,7}} | collective-permute-start | bytes 442376 | tf_op jit(solution)/shard_map/ppermute | solution.py:491
  56.9 11.3 %collective-permute-start.20 = (bf16[192,384]{1,0:T(8,128)(2,1)S(1)}, bf16[192,384]{1,0:T(8,128)(2,1)S(1)}, u32[]{:S(2)}, u32[]{:S(2)}) collective-permute-start(bf16[192,384]{1,0:T(8,128)(2,1)S(1)} %collective-permute-done.16.refs_0_), channel_id=1, source_target_pairs={{0,4},{1,5},{2,6},{3,7},{4,0},{5,1},{6,2},{7,3},{8,12},{9,13},{10,... | collective-permute-start | bytes 442376 | tf_op jit(solution)/shard_map/ppermute | solution.py:478
  60.0 8.3 %collective-permute-start.21 = (bf16[192,384]{1,0:T(8,128)(2,1)S(1)}, bf16[192,384]{1,0:T(8,128)(2,1)S(1)}, u32[]{:S(2)}, u32[]{:S(2)}) collective-permute-start(bf16[192,384]{1,0:T(8,128)(2,1)S(1)} %collective-permute-done.16.refs_0_), channel_id=1, source_target_pairs={{0,6},{1,7},{2,4},{3,5},{4,2},{5,3},{6,0},{7,1},{8,14},{9,15},{10,... | collective-permute-start | bytes 442376 | tf_op jit(solution)/shard_map/ppermute | solution.py:478
  68.3 8.5 %collective-permute-start.25 = (bf16[192,384]{1,0:T(8,128)(2,1)S(1)}, bf16[192,384]{1,0:T(8,128)(2,1)S(1)}, u32[]{:S(2)}, u32[]{:S(2)}) collective-permute-start(bf16[192,384]{1,0:T(8,128)(2,1)S(1)} %collective-permute-done.16.refs_0_), channel_id=1, source_target_pairs={{0,2},{1,3},{2,0},{3,1},{4,6},{5,7},{6,4},{7,5},{8,10},{9,11},{10,... | collective-permute-start | bytes 442376 | tf_op jit(solution)/shard_map/ppermute | solution.py:478
  71.8 5.2 %collective-permute-start.23 = (bf16[352,128]{1,0:T(8,128)(2,1)S(1)}, bf16[352,128]{1,0:T(8,128)(2,1)S(1)}, u32[]{:S(2)}, u32[]{:S(2)}) collective-permute-start(bf16[352,128]{1,0:T(8,128)(2,1)S(1)} %get-tuple-element.65), channel_id=1, source_target_pairs={{16,8},{18,10},{20,12},{22,14},{17,9},{19,11},{21,13},{23,15}} | collective-permute-start | bytes 270344 | tf_op jit(solution)/shard_map/ppermute | solution.py:491
  72.5 12.2 %collective-permute-start.31 = (bf16[192,384]{1,0:T(8,128)(2,1)S(1)}, bf16[192,384]{1,0:T(8,128)(2,1)S(1)}, u32[]{:S(2)}, u32[]{:S(2)}) collective-permute-start(bf16[192,384]{1,0:T(8,128)(2,1)S(1)} %shard_map.58.refs_0_), channel_id=1, source_target_pairs={{0,2},{1,3},{2,0},{3,1},{4,6},{5,7},{6,4},{7,5},{8,10},{9,11},{10,... | collective-permute-start | bytes 442376 | tf_op jit(solution)/shard_map/ppermute | solution.py:478
  74.1 10.8 %collective-permute-start.32 = (bf16[192,384]{1,0:T(8,128)(2,1)S(1)}, bf16[192,384]{1,0:T(8,128)(2,1)S(1)}, u32[]{:S(2)}, u32[]{:S(2)}) collective-permute-start(bf16[192,384]{1,0:T(8,128)(2,1)S(1)} %shard_map.58.refs_0_), channel_id=1, source_target_pairs={{0,4},{1,5},{2,6},{3,7},{4,0},{5,1},{6,2},{7,3},{8,12},{9,13},{10,... | collective-permute-start | bytes 442376 | tf_op jit(solution)/shard_map/ppermute | solution.py:478
  75.6 7.4 %collective-permute-start.24 = (bf16[352,128]{1,0:T(8,128)(2,1)S(1)}, bf16[352,128]{1,0:T(8,128)(2,1)S(1)}, u32[]{:S(2)}, u32[]{:S(2)}) collective-permute-start(bf16[352,128]{1,0:T(8,128)(2,1)S(1)} %get-tuple-element.65), channel_id=1, source_target_pairs={{16,0},{18,2},{20,4},{22,6},{17,1},{19,3},{21,5},{23,7}} | collective-permute-start | bytes 270344 | tf_op jit(solution)/shard_map/ppermute | solution.py:491
  76.9 14.2 %collective-permute-start.26 = (bf16[768,384]{1,0:T(8,128)(2,1)S(1)}, bf16[768,384]{1,0:T(8,128)(2,1)S(1)}, u32[]{:S(2)}, u32[]{:S(2)}) collective-permute-start(bf16[768,384]{1,0:T(8,128)(2,1)S(1)} %shard_map.62.refs_2_), channel_id=1, source_target_pairs={{1,0},{0,1},{3,2},{2,3},{5,4},{4,5},{7,6},{6,7},{9,8},{8,9},{11,10... | collective-permute-start | bytes 1769480 | tf_op jit(solution)/shard_map/ppermute | solution.py:467
  77.0 10.9 %collective-permute-start.33 = (bf16[192,384]{1,0:T(8,128)(2,1)S(1)}, bf16[192,384]{1,0:T(8,128)(2,1)S(1)}, u32[]{:S(2)}, u32[]{:S(2)}) collective-permute-start(bf16[192,384]{1,0:T(8,128)(2,1)S(1)} %shard_map.58.refs_0_), channel_id=1, source_target_pairs={{0,6},{1,7},{2,4},{3,5},{4,2},{5,3},{6,0},{7,1},{8,14},{9,15},{10,... | collective-permute-start | bytes 442376 | tf_op jit(solution)/shard_map/ppermute | solution.py:478
  83.0 5.0 %collective-permute-start.27 = (bf16[352,128]{1,0:T(8,128)(2,1)S(1)}, bf16[352,128]{1,0:T(8,128)(2,1)S(1)}, u32[]{:S(2)}, u32[]{:S(2)}) collective-permute-start(bf16[352,128]{1,0:T(8,128)(2,1)S(1)} %shard_map.60.refs_0_), channel_id=1, source_target_pairs={{0,2},{1,3},{2,0},{3,1},{4,6},{5,7},{6,4},{7,5},{8,10},{9,11},{10,... | collective-permute-start | bytes 270344 | tf_op jit(solution)/shard_map/ppermute | solution.py:478
  84.7 5.8 %collective-permute-start.28 = (bf16[352,128]{1,0:T(8,128)(2,1)S(1)}, bf16[352,128]{1,0:T(8,128)(2,1)S(1)}, u32[]{:S(2)}, u32[]{:S(2)}) collective-permute-start(bf16[352,128]{1,0:T(8,128)(2,1)S(1)} %shard_map.60.refs_0_), channel_id=1, source_target_pairs={{0,4},{1,5},{2,6},{3,7},{4,0},{5,1},{6,2},{7,3},{8,12},{9,13},{10,... | collective-permute-start | bytes 270344 | tf_op jit(solution)/shard_map/ppermute | solution.py:478
  85.0 5.6 %collective-permute-start.29 = (bf16[352,128]{1,0:T(8,128)(2,1)S(1)}, bf16[352,128]{1,0:T(8,128)(2,1)S(1)}, u32[]{:S(2)}, u32[]{:S(2)}) collective-permute-start(bf16[352,128]{1,0:T(8,128)(2,1)S(1)} %shard_map.60.refs_0_), channel_id=1, source_target_pairs={{0,6},{1,7},{2,4},{3,5},{4,2},{5,3},{6,0},{7,1},{8,14},{9,15},{10,... | collective-permute-start | bytes 270344 | tf_op jit(solution)/shard_map/ppermute | solution.py:478
  90.5 5.0 %collective-permute-start.34 = (bf16[768,384]{1,0:T(8,128)(2,1)S(1)}, bf16[768,384]{1,0:T(8,128)(2,1)S(1)}, u32[]{:S(2)}, u32[]{:S(2)}) collective-permute-start(bf16[768,384]{1,0:T(8,128)(2,1)S(1)} %shard_map.66.refs_1_), channel_id=1, source_target_pairs={{1,0},{0,1},{3,2},{2,3},{5,4},{4,5},{7,6},{6,7},{9,8},{8,9},{11,10... | collective-permute-start | bytes 1769480 | tf_op jit(solution)/shard_map/ppermute | solution.py:467
  90.6 2.5 %collective-permute-start.30 = (bf16[1408,128]{1,0:T(8,128)(2,1)S(1)}, bf16[1408,128]{1,0:T(8,128)(2,1)S(1)}, u32[]{:S(2)}, u32[]{:S(2)}) collective-permute-start(bf16[1408,128]{1,0:T(8,128)(2,1)S(1)} %shard_map.64.refs_3_), channel_id=1, source_target_pairs={{1,0},{0,1},{3,2},{2,3},{5,4},{4,5},{7,6},{6,7},{9,8},{8,9},{11,10... | collective-permute-start | bytes 1081352 | tf_op jit(solution)/shard_map/ppermute | solution.py:467
  (5 other events, 31.3 us)

commit v3 on v2

--- a/solution.py
+++ b/solution.py
@@ -356,7 +356,7 @@
 def join_kernel(*refs):
     *quarters, out = refs
     hi, lo, q = where_am_i()
-    for k, piece in enumerate(quarters):
+    for k, piece in enumerate(quarters[::-1]):
         out[quarter_rows(jnp.bitwise_xor(lo, k), out.shape[0]), :] = piece[...]
 
 
@@ -366,7 +366,7 @@
     d = len(got)
     for k, piece in enumerate(got):
 
-        @pl.when(lax.rem(hi, d) == d - 1 - k)
+        @pl.when(lax.rem(hi, d) == k)
         def _():
             out[...] = piece[...]
 
@@ -491,7 +491,7 @@
         got.append(lax.ppermute(x, "tm", pairs))
     if d == 1:
         return got[0]
-    return call(select_kernel, got, [VMEM] * d, [jax.ShapeDtypeStruct(x.shape, x.dtype)], [], 0)[0]
+    return call(select_kernel, got[::-1], [VMEM] * d, [jax.ShapeDtypeStruct(x.shape, x.dtype)], [], 0)[0]
 
 
 def in_group(x):
@@ -501,7 +501,7 @@
 def joined(quarters):
     rows, lanes = quarters[0].shape
     whole_panel = jax.ShapeDtypeStruct((rows * GROUP, lanes), BF)
-    return call(join_kernel, quarters, [VMEM] * GROUP, [whole_panel], [], 0)[0]
+    return call(join_kernel, quarters[::-1], [VMEM] * GROUP, [whole_panel], [], 0)[0]
 
 
 def after(x, *others):

time: 97.5 us -> 95.6 us (0.981)
  starting transfers between devices: 33.4 us -> 32.3 us
    ppermute x6, waiting for transfers between devices: 10.3 us -> 5.66 us  [across(): got.append(lax.ppermute(x, 'tm', pairs))]
    ppermute x15, waiting for transfers between devices: 25.5 us -> 29 us  [swap(): return lax.ppermute(value, ('tm', 'panel'), pairs)]
  transfers between devices with their start and end apart: 35 -> 35, of which waited for: 9 -> 13; matrix products, arithmetic and copies ran while one was open for 0% -> 0% of each run, Pallas kernels for 23% -> 24%
where the time goes in v3:
time: 95.6 us; the launch traced here: 95.3 us
  waiting for transfers between devices  36.1 us (38%)
  starting transfers between devices  32.3 us (34%)
  Pallas kernels  24.4 us (26%)
  other arithmetic  1.55 us (2%)
    ppermute x15, waiting for transfers between devices, swap(): return lax.ppermute(value, ('tm', 'panel'), pairs)  29 us
    pallas_call x18, Pallas kernels, call(): pl.pallas_call(kernel, in_specs=in_specs, out_specs=[VMEM] * len(outs), o...  24.4 us
    ppermute x15, starting transfers between devices, swap(): return lax.ppermute(value, ('tm', 'panel'), pairs)  21.9 us
    ppermute x6, starting transfers between devices, across(): got.append(lax.ppermute(x, 'tm', pairs))  6.66 us
    ppermute x6, waiting for transfers between devices, across(): got.append(lax.ppermute(x, 'tm', pairs))  5.66 us
    ppermute x14, starting transfers between devices, over_panels(): lax.ppermute(x, 'panel', [((i + r) % n, i) for i in range(n)])  3.78 us
  transfers between devices with their start and end apart: 35, of which 13 were waited for; matrix products, arithmetic and copies ran while one was open for 0% of the time, Pallas kernels for 24%

profile of v3, /device:TPU:0, one launch (start us, length us, event | category | flops | bytes accessed | tf_op | source)
XLA Modules:
  0.0 95.3 jit_solution(18227092885957765642)
XLA Ops:
  0.6 1.5 %convert_bitcast_fusion.refs_4_.refs_0_ = bf16[768,384]{1,0:T(8,128)(2,1)S(1)} fusion(f32[1,768,384]{2,1,0:T(8,128)} %param.4), kind=kLoop, calls=%fused_computation | loop fusion | flops 294912 | bytes 1769472 | tf_op jit(solution)/shard_map/convert_element_type | solution.py:532
  2.1 3.0 %collective-permute-start.2 = (bf16[768,384]{1,0:T(8,128)(2,1)S(1)}, bf16[768,384]{1,0:T(8,128)(2,1)S(1)}, u32[]{:S(2)}, u32[]{:S(2)}) collective-permute-start(bf16[768,384]{1,0:T(8,128)(2,1)S(1)} %convert_bitcast_fusion.refs_4_.refs_0_), channel_id=1, source_target_pairs={{0,4},{1,3},{2,6},{3,1},{4,0},{5,7},{6,2},{7,5},{8,12},{9,11},{10,... | collective-permute-start | bytes 1769480 | tf_op jit(solution)/shard_map/ppermute | solution.py:478
  5.2 1.5 %collective-permute-start.4 = (bf16[768,384]{1,0:T(8,128)(2,1)S(1)}, bf16[768,384]{1,0:T(8,128)(2,1)S(1)}, u32[]{:S(2)}, u32[]{:S(2)}) collective-permute-start(bf16[768,384]{1,0:T(8,128)(2,1)S(1)} %convert_bitcast_fusion.refs_4_.refs_0_), channel_id=1, source_target_pairs={{0,2},{1,5},{2,0},{3,7},{4,6},{5,1},{6,4},{7,3},{8,10},{9,13},{10,... | collective-permute-start | bytes 1769480 | tf_op jit(solution)/shard_map/ppermute | solution.py:478
  7.3 11.5 %collective-permute-done.2.refs_2_ = bf16[768,384]{1,0:T(8,128)(2,1)S(1)} collective-permute-done((bf16[768,384]{1,0:T(8,128)(2,1)S(1)}, bf16[768,384]{1,0:T(8,128)(2,1)S(1)}, u32[]{:S(2)}, u32[]{:S(2)}) %collective-permute-start.2) | collective-permute-done | bytes 589856 | tf_op jit(solution)/shard_map/ppermute | solution.py:478
  19.3 1.5 %collective-permute-start.6 = (bf16[768,384]{1,0:T(8,128)(2,1)S(1)}, bf16[768,384]{1,0:T(8,128)(2,1)S(1)}, u32[]{:S(2)}, u32[]{:S(2)}) collective-permute-start(bf16[768,384]{1,0:T(8,128)(2,1)S(1)} %collective-permute-done.2.refs_2_), channel_id=1, source_target_pairs={{0,2},{1,5},{2,0},{3,7},{4,6},{5,1},{6,4},{7,3},{8,10},{9,13},{10,... | collective-permute-start | bytes 1769480 | tf_op jit(solution)/shard_map/ppermute | solution.py:478
  20.8 1.7 %shard_map.50 = (f32[768,384]{1,0:T(8,128)S(1)}, bf16[1408,128]{1,0:T(8,128)(2,1)S(1)}) custom-call(f32[768,384]{1,0:T(8,128)S(1)} %bitcast.4, f32[768,768]{1,0:T(8,128)S(1)} %copy-done.1, bf16[768,384]{1,0:T(8,128)(2,1)S(1)} %convert_element_type.10.refs_2_, bf16[768,384]{1,0:T(8,128)(2,1)S(1)} %collective-permute-done.refs_3_, ...), custom_call_target="tpu_custom_call" | custom-call | flops 905969664 | bytes 7438336 | tf_op jit(solution)/shard_map/pallas_call | solution.py:167
  22.6 1.8 %collective-permute-start.7 = (bf16[1408,128]{1,0:T(8,128)(2,1)S(1)}, bf16[1408,128]{1,0:T(8,128)(2,1)S(1)}, u32[]{:S(2)}, u32[]{:S(2)}) collective-permute-start(bf16[1408,128]{1,0:T(8,128)(2,1)S(1)} %get-tuple-element.43.refs_5_), channel_id=1, source_target_pairs={{0,4},{1,3},{2,6},{3,1},{4,0},{5,7},{6,2},{7,5},{8,12},{9,11},{10,... | collective-permute-start | bytes 1081352 | tf_op jit(solution)/shard_map/ppermute | solution.py:478
  24.3 1.9 %shard_map.51 = (bf16[4,2,768,384]{3,2,1,0:T(8,128)(2,1)S(1)}, bf16[4,768,768]{2,1,0:T(8,128)(2,1)S(1)}, bf16[768,768]{1,0:T(8,128)(2,1)S(1)}) custom-call(bf16[768,384]{1,0:T(8,128)(2,1)S(1)} %convert_bitcast_fusion.refs_4_.refs_0_, bf16[768,384]{1,0:T(8,128)(2,1)S(1)} %collective-permute-done.1.refs_5_.refs_1_, ...), custom_call_target="tpu_custom_call" | custom-call | flops 905969664 | bytes 14155776 | tf_op jit(solution)/shard_map/pallas_call | solution.py:167
  26.2 6.6 %collective-permute-done.7.refs_7_ = bf16[1408,128]{1,0:T(8,128)(2,1)S(1)} collective-permute-done((bf16[1408,128]{1,0:T(8,128)(2,1)S(1)}, bf16[1408,128]{1,0:T(8,128)(2,1)S(1)}, u32[]{:S(2)}, u32[]{:S(2)}) %collective-permute-start.7) | collective-permute-done | bytes 360480 | tf_op jit(solution)/shard_map/ppermute | solution.py:478
  33.0 1.6 %collective-permute-start.11 = (bf16[1408,128]{1,0:T(8,128)(2,1)S(1)}, bf16[1408,128]{1,0:T(8,128)(2,1)S(1)}, u32[]{:S(2)}, u32[]{:S(2)}) collective-permute-start(bf16[1408,128]{1,0:T(8,128)(2,1)S(1)} %get-tuple-element.43.refs_5_), channel_id=1, source_target_pairs={{0,2},{1,5},{2,0},{3,7},{4,6},{5,1},{6,4},{7,3},{8,10},{9,13},{10,... | collective-permute-start | bytes 1081352 | tf_op jit(solution)/shard_map/ppermute | solution.py:478
  35.8 2.3 %shard_map.52 = (bf16[4,2,768,384]{3,2,1,0:T(8,128)(2,1)S(1)}, bf16[2,768,384]{2,1,0:T(8,128)(2,1)S(1)}, bf16[768,768]{1,0:T(8,128)(2,1)S(1)}, bf16[768,384]{1,0:T(8,128)(2,1)S(1)}, bf16[192,384]{1,0:T(8,128)(2,1)S(1)}) custom-call(bf16[4,2,768,384]{3,2,1,0:T(8,128)(2,1)S(1)} %get-tuple-element.41.refs_0_, ...), custom_call_target="tpu_custom_call", output_to_operand_aliasing={{0}: (0, {})} | custom-call | flops 1811939328 | bytes 14893056 | tf_op jit(solution)/shard_map/pallas_call | solution.py:167
  38.2 2.2 %collective-permute-done.11.refs_9_ = bf16[1408,128]{1,0:T(8,128)(2,1)S(1)} collective-permute-done((bf16[1408,128]{1,0:T(8,128)(2,1)S(1)}, bf16[1408,128]{1,0:T(8,128)(2,1)S(1)}, u32[]{:S(2)}, u32[]{:S(2)}) %collective-permute-start.11) | collective-permute-done | bytes 360480 | tf_op jit(solution)/shard_map/ppermute | solution.py:478
  41.6 2.7 %collective-permute-done.13.refs_11_ = bf16[1408,128]{1,0:T(8,128)(2,1)S(1)} collective-permute-done((bf16[1408,128]{1,0:T(8,128)(2,1)S(1)}, bf16[1408,128]{1,0:T(8,128)(2,1)S(1)}, u32[]{:S(2)}, u32[]{:S(2)}) %collective-permute-start.13) | collective-permute-done | bytes 360480 | tf_op jit(solution)/shard_map/ppermute | solution.py:478
  44.5 1.5 %collective-permute-start.16 = (bf16[192,384]{1,0:T(8,128)(2,1)S(1)}, bf16[192,384]{1,0:T(8,128)(2,1)S(1)}, u32[]{:S(2)}, u32[]{:S(2)}) collective-permute-start(bf16[192,384]{1,0:T(8,128)(2,1)S(1)} %get-tuple-element.50), channel_id=1, source_target_pairs={{8,0},{10,2},{12,4},{14,6},{24,16},{26,18},{28,20},{30,22},{9,1},{... | collective-permute-start | bytes 442376 | tf_op jit(solution)/shard_map/ppermute | solution.py:491
  46.0 5.9 %shard_map.54 = (f32[768,384]{1,0:T(8,128)S(1)}, bf16[1408,128]{1,0:T(8,128)(2,1)S(1)}, bf16[768,768]{1,0:T(8,128)(2,1)S(1)}, bf16[768,768]{1,0:T(8,128)(2,1)S(1)}) custom-call(f32[768,384]{1,0:T(8,128)S(1)} %get-tuple-element.40.refs_0_.base, bf16[4,2,768,384]{3,2,1,0:T(8,128)(2,1)S(1)} %get-tuple-element.45.c.refs_1_, ...), custom_call_target="tpu_custom_call" | custom-call | flops 3623878656 | bytes 19759104 | tf_op jit(solution)/shard_map/pallas_call | solution.py:167
  51.9 1.3 %collective-permute-start.15 = (bf16[1408,128]{1,0:T(8,128)(2,1)S(1)}, bf16[1408,128]{1,0:T(8,128)(2,1)S(1)}, u32[]{:S(2)}, u32[]{:S(2)}) collective-permute-start(bf16[1408,128]{1,0:T(8,128)(2,1)S(1)} %get-tuple-element.58), channel_id=1, source_target_pairs={{8,0},{10,2},{12,4},{14,6},{24,16},{26,18},{28,20},{30,22},{9,1},{... | collective-permute-start | bytes 1081352 | tf_op jit(solution)/shard_map/ppermute | solution.py:491
  54.9 1.3 %collective-permute-start.18 = (bf16[192,384]{1,0:T(8,128)(2,1)S(1)}, bf16[192,384]{1,0:T(8,128)(2,1)S(1)}, u32[]{:S(2)}, u32[]{:S(2)}) collective-permute-start(bf16[192,384]{1,0:T(8,128)(2,1)S(1)} %shard_map.57), channel_id=1, source_target_pairs={{16,0},{18,2},{20,4},{22,6},{17,1},{19,3},{21,5},{23,7}} | collective-permute-start | bytes 442376 | tf_op jit(solution)/shard_map/ppermute | solution.py:491
  56.9 3.0 %collective-permute-start.20 = (bf16[192,384]{1,0:T(8,128)(2,1)S(1)}, bf16[192,384]{1,0:T(8,128)(2,1)S(1)}, u32[]{:S(2)}, u32[]{:S(2)}) collective-permute-start(bf16[192,384]{1,0:T(8,128)(2,1)S(1)} %collective-permute-done.16.refs_0_.refs_3_), channel_id=1, source_target_pairs={{0,4},{1,5},{2,6},{3,7},{4,0},{5,1},{6,2},{7,3},{8,12},{9,13},{10,... | collective-permute-start | bytes 442376 | tf_op jit(solution)/shard_map/ppermute | solution.py:478
  60.4 2.3 %shard_map.56 = (bf16[2,768,384]{2,1,0:T(8,128)(2,1)}, bf16[768,768]{1,0:T(8,128)(2,1)S(1)}, bf16[2,768,384]{2,1,0:T(8,128)(2,1)S(1)}, bf16[768,768]{1,0:T(8,128)(2,1)S(1)}) custom-call(bf16[4,2,768,384]{3,2,1,0:T(8,128)(2,1)S(1)} %get-tuple-element.45.c.refs_1_, bf16[2,768,384]{2,1,0:T(8,128)(2,1)S(1)} %get-tuple-element.47.c01.refs_3_, ...), custom_call_target="tpu_custom_call" | custom-call | flops 1811939328 | bytes 11796480 | tf_op jit(solution)/shard_map/pallas_call | solution.py:167
  62.7 1.9 %collective-permute-done.18.refs_0_ = bf16[192,384]{1,0:T(8,128)(2,1)S(1)} collective-permute-done((bf16[192,384]{1,0:T(8,128)(2,1)S(1)}, bf16[192,384]{1,0:T(8,128)(2,1)S(1)}, u32[]{:S(2)}, u32[]{:S(2)}) %collective-permute-start.18) | collective-permute-done | bytes 147488 | tf_op jit(solution)/shard_map/ppermute | solution.py:491
  64.6 2.6 %collective-permute-done.20.refs_1_ = bf16[192,384]{1,0:T(8,128)(2,1)S(1)} collective-permute-done((bf16[192,384]{1,0:T(8,128)(2,1)S(1)}, bf16[192,384]{1,0:T(8,128)(2,1)S(1)}, u32[]{:S(2)}, u32[]{:S(2)}) %collective-permute-start.20) | collective-permute-done | bytes 147488 | tf_op jit(solution)/shard_map/ppermute | solution.py:478
  67.9 1.3 %collective-permute-start.25 = (bf16[192,384]{1,0:T(8,128)(2,1)S(1)}, bf16[192,384]{1,0:T(8,128)(2,1)S(1)}, u32[]{:S(2)}, u32[]{:S(2)}) collective-permute-start(bf16[192,384]{1,0:T(8,128)(2,1)S(1)} %collective-permute-done.16.refs_0_.refs_3_), channel_id=1, source_target_pairs={{0,2},{1,3},{2,0},{3,1},{4,6},{5,7},{6,4},{7,5},{8,10},{9,11},{10,... | collective-permute-start | bytes 442376 | tf_op jit(solution)/shard_map/ppermute | solution.py:478
  69.5 1.6 %shard_map.59 = (bf16[352,128]{1,0:T(8,128)(2,1)S(1)}, bf16[768,768]{1,0:T(8,128)(2,1)S(1)}) custom-call(f32[768,384]{1,0:T(8,128)S(1)} %get-tuple-element.53.agg, bf16[768,384]{1,0:T(8,128)(2,1)S(1)} %get-tuple-element.56.agg_cols, bf16[768,768]{1,0:T(8,128)(2,1)S(1)} %get-tuple-element.60.agg_t, bf16[1408,128]{1,0:T(8,128)(2,1)S(1)} %collective-permute-done.15.refs_0_, ...), custom_call_target="tpu_custom_call" | custom-call | flops 905969664 | bytes 4939776 | tf_op jit(solution)/shard_map/pallas_call | solution.py:167
  71.2 1.3 %collective-permute-start.23 = (bf16[352,128]{1,0:T(8,128)(2,1)S(1)}, bf16[352,128]{1,0:T(8,128)(2,1)S(1)}, u32[]{:S(2)}, u32[]{:S(2)}) collective-permute-start(bf16[352,128]{1,0:T(8,128)(2,1)S(1)} %get-tuple-element.65), channel_id=1, source_target_pairs={{16,0},{18,2},{20,4},{22,6},{17,1},{19,3},{21,5},{23,7}} | collective-permute-start | bytes 270344 | tf_op jit(solution)/shard_map/ppermute | solution.py:491
  72.5 2.5 %collective-permute-start.31 = (bf16[192,384]{1,0:T(8,128)(2,1)S(1)}, bf16[192,384]{1,0:T(8,128)(2,1)S(1)}, u32[]{:S(2)}, u32[]{:S(2)}) collective-permute-start(bf16[192,384]{1,0:T(8,128)(2,1)S(1)} %shard_map.58.refs_3_), channel_id=1, source_target_pairs={{0,6},{1,7},{2,4},{3,5},{4,2},{5,3},{6,0},{7,1},{8,14},{9,15},{10,... | collective-permute-start | bytes 442376 | tf_op jit(solution)/shard_map/ppermute | solution.py:478
  76.1 3.2 %collective-permute-done.23.refs_0_ = bf16[352,128]{1,0:T(8,128)(2,1)S(1)} collective-permute-done((bf16[352,128]{1,0:T(8,128)(2,1)S(1)}, bf16[352,128]{1,0:T(8,128)(2,1)S(1)}, u32[]{:S(2)}, u32[]{:S(2)}) %collective-permute-start.23) | collective-permute-done | bytes 90144 | tf_op jit(solution)/shard_map/ppermute | solution.py:491
  80.1 2.5 %collective-permute-start.27 = (bf16[352,128]{1,0:T(8,128)(2,1)S(1)}, bf16[352,128]{1,0:T(8,128)(2,1)S(1)}, u32[]{:S(2)}, u32[]{:S(2)}) collective-permute-start(bf16[352,128]{1,0:T(8,128)(2,1)S(1)} %shard_map.60.refs_3_), channel_id=1, source_target_pairs={{0,6},{1,7},{2,4},{3,5},{4,2},{5,3},{6,0},{7,1},{8,14},{9,15},{10,... | collective-permute-start | bytes 270344 | tf_op jit(solution)/shard_map/ppermute | solution.py:478
  83.8 1.4 %shard_map.61.refs_0_ = f32[768,384]{1,0:T(8,128)S(1)} custom-call(f32[768,384]{1,0:T(8,128)S(1)} %shard_map.55.cov, bf16[2,768,384]{2,1,0:T(8,128)(2,1)S(1)} %get-tuple-element.69.mine.refs_0_, bf16[768,768]{1,0:T(8,128)(2,1)S(1)} %get-tuple-element.67.mine_t.refs_1_, bf16[768,768]{1,0:T(8,128)(2,1)S(1)} %get-tuple-element.68.right), custom_call_target="tpu_custom_call" | custom-call | flops 905969664 | bytes 5898240 | tf_op jit(solution)/shard_map/pallas_call | solution.py:167
  86.1 2.4 %collective-permute-done.27.refs_0_ = bf16[352,128]{1,0:T(8,128)(2,1)S(1)} collective-permute-done((bf16[352,128]{1,0:T(8,128)(2,1)S(1)}, bf16[352,128]{1,0:T(8,128)(2,1)S(1)}, u32[]{:S(2)}, u32[]{:S(2)}) %collective-permute-start.27) | collective-permute-done | bytes 90144 | tf_op jit(solution)/shard_map/ppermute | solution.py:478
  89.2 1.8 %shard_map.63 = (bf16[2,768,384]{2,1,0:T(8,128)(2,1)S(1)}, bf16[768,768]{1,0:T(8,128)(2,1)S(1)}) custom-call(bf16[2,768,384]{2,1,0:T(8,128)(2,1)S(1)} %get-tuple-element.69.mine.refs_0_, bf16[768,768]{1,0:T(8,128)(2,1)S(1)} %get-tuple-element.67.mine_t.refs_1_, bf16[768,384]{1,0:T(8,128)(2,1)S(1)} %shard_map.62.refs_2_, ...), custom_call_target="tpu_custom_call" | custom-call | flops 905969664 | bytes 5898240 | tf_op jit(solution)/shard_map/pallas_call | solution.py:167
  91.1 2.5 %shard_map.65 = f32[1,768,384]{2,1,0:T(8,128)} custom-call(f32[768,384]{1,0:T(8,128)S(1)} %shard_map.61.refs_0_, bf16[2,768,384]{2,1,0:T(8,128)(2,1)S(1)} %get-tuple-element.72.refs_1_.refs_0_, bf16[768,768]{1,0:T(8,128)(2,1)S(1)} %get-tuple-element.71.refs_2_, bf16[1408,128]{1,0:T(8,128)(2,1)S(1)} %shard_map.64.refs_3_, ...), custom_call_target="tpu_custom_call" | custom-call | flops 905969664 | bytes 5439488 | tf_op jit(solution)/shard_map/pallas_call | solution.py:167
  93.6 1.7 %shard_map.67 = bf16[1,768,384]{2,1,0:T(8,128)(2,1)} custom-call(bf16[2,768,384]{2,1,0:T(8,128)(2,1)S(1)} %get-tuple-element.72.refs_1_.refs_0_, bf16[768,384]{1,0:T(8,128)(2,1)S(1)} %shard_map.66.refs_1_, bf16[768,384]{1,0:T(8,128)(2,1)S(1)} %collective-permute-done.34.refs_2_), custom_call_target="tpu_custom_call" | custom-call | flops 452984832 | bytes 2949120 | tf_op jit(solution)/shard_map/pallas_call | solution.py:167
  (62 shorter events, 12.6 us)
Async XLA Ops:
  2.1 16.7 %collective-permute-start.2 = (bf16[768,384]{1,0:T(8,128)(2,1)S(1)}, bf16[768,384]{1,0:T(8,128)(2,1)S(1)}, u32[]{:S(2)}, u32[]{:S(2)}) collective-permute-start(bf16[768,384]{1,0:T(8,128)(2,1)S(1)} %convert_bitcast_fusion.refs_4_.refs_0_), channel_id=1, source_target_pairs={{0,4},{1,3},{2,6},{3,1},{4,0},{5,7},{6,2},{7,5},{8,12},{9,11},{10,... | collective-permute-start | bytes 1769480 | tf_op jit(solution)/shard_map/ppermute | solution.py:478
  5.2 13.7 %collective-permute-start.4 = (bf16[768,384]{1,0:T(8,128)(2,1)S(1)}, bf16[768,384]{1,0:T(8,128)(2,1)S(1)}, u32[]{:S(2)}, u32[]{:S(2)}) collective-permute-start(bf16[768,384]{1,0:T(8,128)(2,1)S(1)} %convert_bitcast_fusion.refs_4_.refs_0_), channel_id=1, source_target_pairs={{0,2},{1,5},{2,0},{3,7},{4,6},{5,1},{6,4},{7,3},{8,10},{9,13},{10,... | collective-permute-start | bytes 1769480 | tf_op jit(solution)/shard_map/ppermute | solution.py:478
  6.7 14.1 %collective-permute-start = (bf16[768,384]{1,0:T(8,128)(2,1)S(1)}, bf16[768,384]{1,0:T(8,128)(2,1)S(1)}, u32[]{:S(2)}, u32[]{:S(2)}) collective-permute-start(bf16[768,384]{1,0:T(8,128)(2,1)S(1)} %convert_element_type.10.refs_2_), channel_id=1, source_target_pairs={{1,0},{0,1},{3,2},{2,3},{5,4},{4,5},{7,6},{6,7},{9,8},{8,9},{11,10... | collective-permute-start | bytes 1769480 | tf_op jit(solution)/shard_map/ppermute | solution.py:467
  6.8 14.0 %collective-permute-start.1 = (bf16[768,384]{1,0:T(8,128)(2,1)S(1)}, bf16[768,384]{1,0:T(8,128)(2,1)S(1)}, u32[]{:S(2)}, u32[]{:S(2)}) collective-permute-start(bf16[768,384]{1,0:T(8,128)(2,1)S(1)} %convert_bitcast_fusion.refs_4_.refs_0_), channel_id=1, source_target_pairs={{1,0},{0,1},{3,2},{2,3},{5,4},{4,5},{7,6},{6,7},{9,8},{8,9},{11,10... | collective-permute-start | bytes 1769480 | tf_op jit(solution)/shard_map/ppermute | solution.py:467
  18.8 5.5 %collective-permute-start.3 = (bf16[768,384]{1,0:T(8,128)(2,1)S(1)}, bf16[768,384]{1,0:T(8,128)(2,1)S(1)}, u32[]{:S(2)}, u32[]{:S(2)}) collective-permute-start(bf16[768,384]{1,0:T(8,128)(2,1)S(1)} %collective-permute-done.2.refs_2_), channel_id=1, source_target_pairs={{1,0},{0,1},{3,2},{2,3},{5,4},{4,5},{7,6},{6,7},{9,8},{8,9},{11,10... | collective-permute-start | bytes 1769480 | tf_op jit(solution)/shard_map/ppermute | solution.py:467
  18.8 5.5 %collective-permute-start.5 = (bf16[768,384]{1,0:T(8,128)(2,1)S(1)}, bf16[768,384]{1,0:T(8,128)(2,1)S(1)}, u32[]{:S(2)}, u32[]{:S(2)}) collective-permute-start(bf16[768,384]{1,0:T(8,128)(2,1)S(1)} %collective-permute-done.4.refs_4_), channel_id=1, source_target_pairs={{1,0},{0,1},{3,2},{2,3},{5,4},{4,5},{7,6},{6,7},{9,8},{8,9},{11,10... | collective-permute-start | bytes 1769480 | tf_op jit(solution)/shard_map/ppermute | solution.py:467
  19.3 13.5 %collective-permute-start.6 = (bf16[768,384]{1,0:T(8,128)(2,1)S(1)}, bf16[768,384]{1,0:T(8,128)(2,1)S(1)}, u32[]{:S(2)}, u32[]{:S(2)}) collective-permute-start(bf16[768,384]{1,0:T(8,128)(2,1)S(1)} %collective-permute-done.2.refs_2_), channel_id=1, source_target_pairs={{0,2},{1,5},{2,0},{3,7},{4,6},{5,1},{6,4},{7,3},{8,10},{9,13},{10,... | collective-permute-start | bytes 1769480 | tf_op jit(solution)/shard_map/ppermute | solution.py:478
  22.6 10.3 %collective-permute-start.7 = (bf16[1408,128]{1,0:T(8,128)(2,1)S(1)}, bf16[1408,128]{1,0:T(8,128)(2,1)S(1)}, u32[]{:S(2)}, u32[]{:S(2)}) collective-permute-start(bf16[1408,128]{1,0:T(8,128)(2,1)S(1)} %get-tuple-element.43.refs_5_), channel_id=1, source_target_pairs={{0,4},{1,3},{2,6},{3,1},{4,0},{5,7},{6,2},{7,5},{8,12},{9,11},{10,... | collective-permute-start | bytes 1081352 | tf_op jit(solution)/shard_map/ppermute | solution.py:478
  32.9 3.0 %collective-permute-start.8 = (bf16[768,384]{1,0:T(8,128)(2,1)S(1)}, bf16[768,384]{1,0:T(8,128)(2,1)S(1)}, u32[]{:S(2)}, u32[]{:S(2)}) collective-permute-start(bf16[768,384]{1,0:T(8,128)(2,1)S(1)} %collective-permute-done.6.refs_2_), channel_id=1, source_target_pairs={{1,0},{0,1},{3,2},{2,3},{5,4},{4,5},{7,6},{6,7},{9,8},{8,9},{11,10... | collective-permute-start | bytes 1769480 | tf_op jit(solution)/shard_map/ppermute | solution.py:467
  33.0 7.4 %collective-permute-start.11 = (bf16[1408,128]{1,0:T(8,128)(2,1)S(1)}, bf16[1408,128]{1,0:T(8,128)(2,1)S(1)}, u32[]{:S(2)}, u32[]{:S(2)}) collective-permute-start(bf16[1408,128]{1,0:T(8,128)(2,1)S(1)} %get-tuple-element.43.refs_5_), channel_id=1, source_target_pairs={{0,2},{1,5},{2,0},{3,7},{4,6},{5,1},{6,4},{7,3},{8,10},{9,13},{10,... | collective-permute-start | bytes 1081352 | tf_op jit(solution)/shard_map/ppermute | solution.py:478
  34.6 9.7 %collective-permute-start.13 = (bf16[1408,128]{1,0:T(8,128)(2,1)S(1)}, bf16[1408,128]{1,0:T(8,128)(2,1)S(1)}, u32[]{:S(2)}, u32[]{:S(2)}) collective-permute-start(bf16[1408,128]{1,0:T(8,128)(2,1)S(1)} %collective-permute-done.7.refs_7_), channel_id=1, source_target_pairs={{0,2},{1,5},{2,0},{3,7},{4,6},{5,1},{6,4},{7,3},{8,10},{9,13},{10,... | collective-permute-start | bytes 1081352 | tf_op jit(solution)/shard_map/ppermute | solution.py:478
  35.0 10.9 %collective-permute-start.9 = (bf16[1408,128]{1,0:T(8,128)(2,1)S(1)}, bf16[1408,128]{1,0:T(8,128)(2,1)S(1)}, u32[]{:S(2)}, u32[]{:S(2)}) collective-permute-start(bf16[1408,128]{1,0:T(8,128)(2,1)S(1)} %get-tuple-element.43.refs_5_), channel_id=1, source_target_pairs={{1,0},{0,1},{3,2},{2,3},{5,4},{4,5},{7,6},{6,7},{9,8},{8,9},{11,10... | collective-permute-start | bytes 1081352 | tf_op jit(solution)/shard_map/ppermute | solution.py:467
  35.8 10.1 %collective-permute-start.10 = (bf16[1408,128]{1,0:T(8,128)(2,1)S(1)}, bf16[1408,128]{1,0:T(8,128)(2,1)S(1)}, u32[]{:S(2)}, u32[]{:S(2)}) collective-permute-start(bf16[1408,128]{1,0:T(8,128)(2,1)S(1)} %collective-permute-done.7.refs_7_), channel_id=1, source_target_pairs={{1,0},{0,1},{3,2},{2,3},{5,4},{4,5},{7,6},{6,7},{9,8},{8,9},{11,10... | collective-permute-start | bytes 1081352 | tf_op jit(solution)/shard_map/ppermute | solution.py:467
  40.4 5.6 %collective-permute-start.12 = (bf16[1408,128]{1,0:T(8,128)(2,1)S(1)}, bf16[1408,128]{1,0:T(8,128)(2,1)S(1)}, u32[]{:S(2)}, u32[]{:S(2)}) collective-permute-start(bf16[1408,128]{1,0:T(8,128)(2,1)S(1)} %collective-permute-done.11.refs_9_), channel_id=1, source_target_pairs={{1,0},{0,1},{3,2},{2,3},{5,4},{4,5},{7,6},{6,7},{9,8},{8,9},{11,10... | collective-permute-start | bytes 1081352 | tf_op jit(solution)/shard_map/ppermute | solution.py:467
  44.5 8.7 %collective-permute-start.16 = (bf16[192,384]{1,0:T(8,128)(2,1)S(1)}, bf16[192,384]{1,0:T(8,128)(2,1)S(1)}, u32[]{:S(2)}, u32[]{:S(2)}) collective-permute-start(bf16[192,384]{1,0:T(8,128)(2,1)S(1)} %get-tuple-element.50), channel_id=1, source_target_pairs={{8,0},{10,2},{12,4},{14,6},{24,16},{26,18},{28,20},{30,22},{9,1},{... | collective-permute-start | bytes 442376 | tf_op jit(solution)/shard_map/ppermute | solution.py:491
  51.9 16.0 %collective-permute-start.15 = (bf16[1408,128]{1,0:T(8,128)(2,1)S(1)}, bf16[1408,128]{1,0:T(8,128)(2,1)S(1)}, u32[]{:S(2)}, u32[]{:S(2)}) collective-permute-start(bf16[1408,128]{1,0:T(8,128)(2,1)S(1)} %get-tuple-element.58), channel_id=1, source_target_pairs={{8,0},{10,2},{12,4},{14,6},{24,16},{26,18},{28,20},{30,22},{9,1},{... | collective-permute-start | bytes 1081352 | tf_op jit(solution)/shard_map/ppermute | solution.py:491
  54.9 9.7 %collective-permute-start.18 = (bf16[192,384]{1,0:T(8,128)(2,1)S(1)}, bf16[192,384]{1,0:T(8,128)(2,1)S(1)}, u32[]{:S(2)}, u32[]{:S(2)}) collective-permute-start(bf16[192,384]{1,0:T(8,128)(2,1)S(1)} %shard_map.57), channel_id=1, source_target_pairs={{16,0},{18,2},{20,4},{22,6},{17,1},{19,3},{21,5},{23,7}} | collective-permute-start | bytes 442376 | tf_op jit(solution)/shard_map/ppermute | solution.py:491
  56.2 8.4 %collective-permute-start.19 = (bf16[192,384]{1,0:T(8,128)(2,1)S(1)}, bf16[192,384]{1,0:T(8,128)(2,1)S(1)}, u32[]{:S(2)}, u32[]{:S(2)}) collective-permute-start(bf16[192,384]{1,0:T(8,128)(2,1)S(1)} %shard_map.57), channel_id=1, source_target_pairs={{16,8},{18,10},{20,12},{22,14},{17,9},{19,11},{21,13},{23,15}} | collective-permute-start | bytes 442376 | tf_op jit(solution)/shard_map/ppermute | solution.py:491
  56.9 10.3 %collective-permute-start.20 = (bf16[192,384]{1,0:T(8,128)(2,1)S(1)}, bf16[192,384]{1,0:T(8,128)(2,1)S(1)}, u32[]{:S(2)}, u32[]{:S(2)}) collective-permute-start(bf16[192,384]{1,0:T(8,128)(2,1)S(1)} %collective-permute-done.16.refs_0_.refs_3_), channel_id=1, source_target_pairs={{0,4},{1,5},{2,6},{3,7},{4,0},{5,1},{6,2},{7,3},{8,12},{9,13},{10,... | collective-permute-start | bytes 442376 | tf_op jit(solution)/shard_map/ppermute | solution.py:478
  60.0 7.3 %collective-permute-start.21 = (bf16[192,384]{1,0:T(8,128)(2,1)S(1)}, bf16[192,384]{1,0:T(8,128)(2,1)S(1)}, u32[]{:S(2)}, u32[]{:S(2)}) collective-permute-start(bf16[192,384]{1,0:T(8,128)(2,1)S(1)} %collective-permute-done.16.refs_0_.refs_3_), channel_id=1, source_target_pairs={{0,6},{1,7},{2,4},{3,5},{4,2},{5,3},{6,0},{7,1},{8,14},{9,15},{10,... | collective-permute-start | bytes 442376 | tf_op jit(solution)/shard_map/ppermute | solution.py:478
  67.9 8.1 %collective-permute-start.25 = (bf16[192,384]{1,0:T(8,128)(2,1)S(1)}, bf16[192,384]{1,0:T(8,128)(2,1)S(1)}, u32[]{:S(2)}, u32[]{:S(2)}) collective-permute-start(bf16[192,384]{1,0:T(8,128)(2,1)S(1)} %collective-permute-done.16.refs_0_.refs_3_), channel_id=1, source_target_pairs={{0,2},{1,3},{2,0},{3,1},{4,6},{5,7},{6,4},{7,5},{8,10},{9,11},{10,... | collective-permute-start | bytes 442376 | tf_op jit(solution)/shard_map/ppermute | solution.py:478
  71.2 8.1 %collective-permute-start.23 = (bf16[352,128]{1,0:T(8,128)(2,1)S(1)}, bf16[352,128]{1,0:T(8,128)(2,1)S(1)}, u32[]{:S(2)}, u32[]{:S(2)}) collective-permute-start(bf16[352,128]{1,0:T(8,128)(2,1)S(1)} %get-tuple-element.65), channel_id=1, source_target_pairs={{16,0},{18,2},{20,4},{22,6},{17,1},{19,3},{21,5},{23,7}} | collective-permute-start | bytes 270344 | tf_op jit(solution)/shard_map/ppermute | solution.py:491
  72.5 10.1 %collective-permute-start.31 = (bf16[192,384]{1,0:T(8,128)(2,1)S(1)}, bf16[192,384]{1,0:T(8,128)(2,1)S(1)}, u32[]{:S(2)}, u32[]{:S(2)}) collective-permute-start(bf16[192,384]{1,0:T(8,128)(2,1)S(1)} %shard_map.58.refs_3_), channel_id=1, source_target_pairs={{0,6},{1,7},{2,4},{3,5},{4,2},{5,3},{6,0},{7,1},{8,14},{9,15},{10,... | collective-permute-start | bytes 442376 | tf_op jit(solution)/shard_map/ppermute | solution.py:478
  75.0 7.9 %collective-permute-start.32 = (bf16[192,384]{1,0:T(8,128)(2,1)S(1)}, bf16[192,384]{1,0:T(8,128)(2,1)S(1)}, u32[]{:S(2)}, u32[]{:S(2)}) collective-permute-start(bf16[192,384]{1,0:T(8,128)(2,1)S(1)} %shard_map.58.refs_3_), channel_id=1, source_target_pairs={{0,4},{1,5},{2,6},{3,7},{4,0},{5,1},{6,2},{7,3},{8,12},{9,13},{10,... | collective-permute-start | bytes 442376 | tf_op jit(solution)/shard_map/ppermute | solution.py:478
  75.3 4.8 %collective-permute-start.24 = (bf16[352,128]{1,0:T(8,128)(2,1)S(1)}, bf16[352,128]{1,0:T(8,128)(2,1)S(1)}, u32[]{:S(2)}, u32[]{:S(2)}) collective-permute-start(bf16[352,128]{1,0:T(8,128)(2,1)S(1)} %get-tuple-element.65), channel_id=1, source_target_pairs={{16,8},{18,10},{20,12},{22,14},{17,9},{19,11},{21,13},{23,15}} | collective-permute-start | bytes 270344 | tf_op jit(solution)/shard_map/ppermute | solution.py:491
  76.0 13.2 %collective-permute-start.26 = (bf16[768,384]{1,0:T(8,128)(2,1)S(1)}, bf16[768,384]{1,0:T(8,128)(2,1)S(1)}, u32[]{:S(2)}, u32[]{:S(2)}) collective-permute-start(bf16[768,384]{1,0:T(8,128)(2,1)S(1)} %shard_map.62.refs_2_), channel_id=1, source_target_pairs={{1,0},{0,1},{3,2},{2,3},{5,4},{4,5},{7,6},{6,7},{9,8},{8,9},{11,10... | collective-permute-start | bytes 1769480 | tf_op jit(solution)/shard_map/ppermute | solution.py:467
  79.3 6.8 %collective-permute-start.33 = (bf16[192,384]{1,0:T(8,128)(2,1)S(1)}, bf16[192,384]{1,0:T(8,128)(2,1)S(1)}, u32[]{:S(2)}, u32[]{:S(2)}) collective-permute-start(bf16[192,384]{1,0:T(8,128)(2,1)S(1)} %shard_map.58.refs_3_), channel_id=1, source_target_pairs={{0,2},{1,3},{2,0},{3,1},{4,6},{5,7},{6,4},{7,5},{8,10},{9,11},{10,... | collective-permute-start | bytes 442376 | tf_op jit(solution)/shard_map/ppermute | solution.py:478
  80.1 8.5 %collective-permute-start.27 = (bf16[352,128]{1,0:T(8,128)(2,1)S(1)}, bf16[352,128]{1,0:T(8,128)(2,1)S(1)}, u32[]{:S(2)}, u32[]{:S(2)}) collective-permute-start(bf16[352,128]{1,0:T(8,128)(2,1)S(1)} %shard_map.60.refs_3_), channel_id=1, source_target_pairs={{0,6},{1,7},{2,4},{3,5},{4,2},{5,3},{6,0},{7,1},{8,14},{9,15},{10,... | collective-permute-start | bytes 270344 | tf_op jit(solution)/shard_map/ppermute | solution.py:478
  82.6 6.0 %collective-permute-start.28 = (bf16[352,128]{1,0:T(8,128)(2,1)S(1)}, bf16[352,128]{1,0:T(8,128)(2,1)S(1)}, u32[]{:S(2)}, u32[]{:S(2)}) collective-permute-start(bf16[352,128]{1,0:T(8,128)(2,1)S(1)} %shard_map.60.refs_3_), channel_id=1, source_target_pairs={{0,4},{1,5},{2,6},{3,7},{4,0},{5,1},{6,2},{7,3},{8,12},{9,13},{10,... | collective-permute-start | bytes 270344 | tf_op jit(solution)/shard_map/ppermute | solution.py:478
  82.9 5.7 %collective-permute-start.29 = (bf16[352,128]{1,0:T(8,128)(2,1)S(1)}, bf16[352,128]{1,0:T(8,128)(2,1)S(1)}, u32[]{:S(2)}, u32[]{:S(2)}) collective-permute-start(bf16[352,128]{1,0:T(8,128)(2,1)S(1)} %shard_map.60.refs_3_), channel_id=1, source_target_pairs={{0,2},{1,3},{2,0},{3,1},{4,6},{5,7},{6,4},{7,5},{8,10},{9,11},{10,... | collective-permute-start | bytes 270344 | tf_op jit(solution)/shard_map/ppermute | solution.py:478
  88.6 5.0 %collective-permute-start.34 = (bf16[768,384]{1,0:T(8,128)(2,1)S(1)}, bf16[768,384]{1,0:T(8,128)(2,1)S(1)}, u32[]{:S(2)}, u32[]{:S(2)}) collective-permute-start(bf16[768,384]{1,0:T(8,128)(2,1)S(1)} %shard_map.66.refs_1_), channel_id=1, source_target_pairs={{1,0},{0,1},{3,2},{2,3},{5,4},{4,5},{7,6},{6,7},{9,8},{8,9},{11,10... | collective-permute-start | bytes 1769480 | tf_op jit(solution)/shard_map/ppermute | solution.py:467
  88.6 2.5 %collective-permute-start.30 = (bf16[1408,128]{1,0:T(8,128)(2,1)S(1)}, bf16[1408,128]{1,0:T(8,128)(2,1)S(1)}, u32[]{:S(2)}, u32[]{:S(2)}) collective-permute-start(bf16[1408,128]{1,0:T(8,128)(2,1)S(1)} %shard_map.64.refs_3_), channel_id=1, source_target_pairs={{1,0},{0,1},{3,2},{2,3},{5,4},{4,5},{7,6},{6,7},{9,8},{8,9},{11,10... | collective-permute-start | bytes 1081352 | tf_op jit(solution)/shard_map/ppermute | solution.py:467
  (5 other events, 31.0 us)

commit v4 on v3

--- a/solution.py
+++ b/solution.py
@@ -356,7 +356,7 @@
 def join_kernel(*refs):
     *quarters, out = refs
     hi, lo, q = where_am_i()
-    for k, piece in enumerate(quarters[::-1]):
+    for k, piece in enumerate(quarters):
         out[quarter_rows(jnp.bitwise_xor(lo, k), out.shape[0]), :] = piece[...]
 
 
@@ -402,20 +402,6 @@
     def _():
         new_mine[...] = mine[...]
         new_mine_t[...] = mine_t[...]
-
-
-def last_comp_kernel(n, bit, *refs):
-    (mine,), parts, (out,) = split(refs, 1, n, 1)
-    hi, lo, q = where_am_i()
-    lower = is_lower(bit)
-
-    @pl.when(lower)
-    def _():
-        out[0] = times(parts, mine.at[q], q).astype(BF)
-
-    @pl.when(jnp.logical_not(lower))
-    def _():
-        out[0] = mine[q]
 
 
 def pair_cov_kernel(n, to_last, agg, agg_cols, agg_t, *refs):
@@ -445,20 +431,23 @@
         out[...] = cov[...]
 
 
-def last_cov_kernel(n, bit, *refs):
-    (cov, mine, mine_t), parts, (out,), (sent, right) = split(refs, 3, n, 1, 2)
+def last_kernel(n, bit, *refs):
+    (cov, mine, mine_t), c_parts, s_parts, (out, prop), scratch = split(refs, 3, n, n, 2, 2)
+    sent, right = scratch
     hi, lo, q = where_am_i()
     lower = is_lower(bit)
 
     @pl.when(lower)
     def _():
-        place_whole(parts, sent, q)
+        place_whole(s_parts, sent, q)
         unpack(sent, right, n)
         out[0] = cov[...] + sandwich(right[...], mine[q], mine_t[...])
+        prop[0] = times(c_parts, mine.at[q], q).astype(BF)
 
     @pl.when(jnp.logical_not(lower))
     def _():
         out[0] = cov[...]
+        prop[0] = mine[q]
 
 
 def over_panels(x):
@@ -501,7 +490,7 @@
 def joined(quarters):
     rows, lanes = quarters[0].shape
     whole_panel = jax.ShapeDtypeStruct((rows * GROUP, lanes), BF)
-    return call(join_kernel, quarters[::-1], [VMEM] * GROUP, [whole_panel], [], 0)[0]
+    return call(join_kernel, quarters, [VMEM] * GROUP, [whole_panel], [], 0)[0]
 
 
 def after(x, *others):
@@ -614,22 +603,14 @@
             if bit:
                 c_panel = after(c_panel, *s_blocks[1:])
             c_parts = over_panels(c_panel)
-            (prop,) = call(
-                functools.partial(last_comp_kernel, n, bit),
-                [after(mine, s_got), *c_parts],
-                [VMEM] * (1 + n),
-                [out_comp],
-                [],
-                one,
-            )
             s_parts = over_panels(s_got)
-            (cov,) = call(
-                functools.partial(last_cov_kernel, n, bit),
-                [cov, mine, mine_t, *s_parts],
-                [VMEM] * (3 + n),
-                [out_cov],
+            cov, prop = call(
+                functools.partial(last_kernel, n, bit),
+                [cov, mine, mine_t, *c_parts, *s_parts],
+                [VMEM] * (3 + 2 * n),
+                [out_cov, out_comp],
                 [packed_scratch, square_scratch],
-                2 * one,
+                3 * one,
             )
             break
         if to_last:

time: 95.6 us -> 96.6 us (1.010)
  starting transfers between devices: 32.3 us -> 33.6 us
    ppermute x6, waiting for transfers between devices: 5.66 us -> 4.26 us  [across(): got.append(lax.ppermute(x, 'tm', pairs))]
    ppermute x14, waiting for transfers between devices: 1.49 us -> 2.79 us  [over_panels(): lax.ppermute(x, 'panel', [((i + r) % n, i) for i in range(n)])]
    ppermute x15, starting transfers between devices: 21.9 us -> 23.2 us  [swap(): return lax.ppermute(value, ('tm', 'panel'), pairs)]
    pallas_call x18 -> x17, Pallas kernels: 24.4 us -> 23.9 us  [call(): pl.pallas_call(kernel, in_specs=in_specs, out_specs=[VMEM] * len(outs), o...]
  transfers between devices with their start and end apart: 35 -> 35, of which waited for: 13 -> 15; matrix products, arithmetic and copies ran while one was open for 0% -> 0% of each run, Pallas kernels for 24% -> 20%
where the time goes in v4:
time: 96.6 us; the launch traced here: 96.4 us
  waiting for transfers between devices  36.5 us (38%)
  starting transfers between devices  33.6 us (35%)
  Pallas kernels  23.9 us (25%)
  other arithmetic  1.55 us (2%)
    ppermute x15, waiting for transfers between devices, swap(): return lax.ppermute(value, ('tm', 'panel'), pairs)  29.4 us
    pallas_call x17, Pallas kernels, call(): pl.pallas_call(kernel, in_specs=in_specs, out_specs=[VMEM] * len(outs), o...  23.9 us
    ppermute x15, starting transfers between devices, swap(): return lax.ppermute(value, ('tm', 'panel'), pairs)  23.2 us
    ppermute x6, starting transfers between devices, across(): got.append(lax.ppermute(x, 'tm', pairs))  6.66 us
    ppermute x6, waiting for transfers between devices, across(): got.append(lax.ppermute(x, 'tm', pairs))  4.26 us
    ppermute x14, starting transfers between devices, over_panels(): lax.ppermute(x, 'panel', [((i + r) % n, i) for i in range(n)])  3.78 us
    ppermute x14, waiting for transfers between devices, over_panels(): lax.ppermute(x, 'panel', [((i + r) % n, i) for i in range(n)])  2.79 us
  transfers between devices with their start and end apart: 35, of which 15 were waited for; matrix products, arithmetic and copies ran while one was open for 0% of the time, Pallas kernels for 20%

profile of v4, /device:TPU:0, one launch (start us, length us, event | category | flops | bytes accessed | tf_op | source)
XLA Modules:
  0.0 96.4 jit_solution(11044373593589598874)
XLA Ops:
  0.6 1.5 %convert_bitcast_fusion.refs_4_.refs_0_ = bf16[768,384]{1,0:T(8,128)(2,1)S(1)} fusion(f32[1,768,384]{2,1,0:T(8,128)} %param.4), kind=kLoop, calls=%fused_computation | loop fusion | flops 294912 | bytes 1769472 | tf_op jit(solution)/shard_map/convert_element_type | solution.py:521
  2.1 3.0 %collective-permute-start.2 = (bf16[768,384]{1,0:T(8,128)(2,1)S(1)}, bf16[768,384]{1,0:T(8,128)(2,1)S(1)}, u32[]{:S(2)}, u32[]{:S(2)}) collective-permute-start(bf16[768,384]{1,0:T(8,128)(2,1)S(1)} %convert_bitcast_fusion.refs_4_.refs_0_), channel_id=1, source_target_pairs={{0,4},{1,3},{2,6},{3,1},{4,0},{5,7},{6,2},{7,5},{8,12},{9,11},{10,... | collective-permute-start | bytes 1769480 | tf_op jit(solution)/shard_map/ppermute | solution.py:467
  5.2 1.5 %collective-permute-start.4 = (bf16[768,384]{1,0:T(8,128)(2,1)S(1)}, bf16[768,384]{1,0:T(8,128)(2,1)S(1)}, u32[]{:S(2)}, u32[]{:S(2)}) collective-permute-start(bf16[768,384]{1,0:T(8,128)(2,1)S(1)} %convert_bitcast_fusion.refs_4_.refs_0_), channel_id=1, source_target_pairs={{0,2},{1,5},{2,0},{3,7},{4,6},{5,1},{6,4},{7,3},{8,10},{9,13},{10,... | collective-permute-start | bytes 1769480 | tf_op jit(solution)/shard_map/ppermute | solution.py:467
  7.3 11.5 %collective-permute-done.2.refs_2_ = bf16[768,384]{1,0:T(8,128)(2,1)S(1)} collective-permute-done((bf16[768,384]{1,0:T(8,128)(2,1)S(1)}, bf16[768,384]{1,0:T(8,128)(2,1)S(1)}, u32[]{:S(2)}, u32[]{:S(2)}) %collective-permute-start.2) | collective-permute-done | bytes 589856 | tf_op jit(solution)/shard_map/ppermute | solution.py:467
  19.3 1.5 %collective-permute-start.6 = (bf16[768,384]{1,0:T(8,128)(2,1)S(1)}, bf16[768,384]{1,0:T(8,128)(2,1)S(1)}, u32[]{:S(2)}, u32[]{:S(2)}) collective-permute-start(bf16[768,384]{1,0:T(8,128)(2,1)S(1)} %collective-permute-done.2.refs_2_), channel_id=1, source_target_pairs={{0,2},{1,5},{2,0},{3,7},{4,6},{5,1},{6,4},{7,3},{8,10},{9,13},{10,... | collective-permute-start | bytes 1769480 | tf_op jit(solution)/shard_map/ppermute | solution.py:467
  20.8 1.7 %shard_map.50 = (f32[768,384]{1,0:T(8,128)S(1)}, bf16[1408,128]{1,0:T(8,128)(2,1)S(1)}) custom-call(f32[768,384]{1,0:T(8,128)S(1)} %bitcast.4, f32[768,768]{1,0:T(8,128)S(1)} %copy-done.1, bf16[768,384]{1,0:T(8,128)(2,1)S(1)} %convert_element_type.10.refs_2_, bf16[768,384]{1,0:T(8,128)(2,1)S(1)} %collective-permute-done.refs_3_, ...), custom_call_target="tpu_custom_call" | custom-call | flops 905969664 | bytes 7438336 | tf_op jit(solution)/shard_map/pallas_call | solution.py:167
  22.6 1.8 %collective-permute-start.7 = (bf16[1408,128]{1,0:T(8,128)(2,1)S(1)}, bf16[1408,128]{1,0:T(8,128)(2,1)S(1)}, u32[]{:S(2)}, u32[]{:S(2)}) collective-permute-start(bf16[1408,128]{1,0:T(8,128)(2,1)S(1)} %get-tuple-element.42.refs_5_), channel_id=1, source_target_pairs={{0,4},{1,3},{2,6},{3,1},{4,0},{5,7},{6,2},{7,5},{8,12},{9,11},{10,... | collective-permute-start | bytes 1081352 | tf_op jit(solution)/shard_map/ppermute | solution.py:467
  24.3 1.9 %shard_map.51 = (bf16[4,2,768,384]{3,2,1,0:T(8,128)(2,1)S(1)}, bf16[4,768,768]{2,1,0:T(8,128)(2,1)S(1)}, bf16[768,768]{1,0:T(8,128)(2,1)S(1)}) custom-call(bf16[768,384]{1,0:T(8,128)(2,1)S(1)} %convert_bitcast_fusion.refs_4_.refs_0_, bf16[768,384]{1,0:T(8,128)(2,1)S(1)} %collective-permute-done.1.refs_5_.refs_1_, ...), custom_call_target="tpu_custom_call" | custom-call | flops 905969664 | bytes 14155776 | tf_op jit(solution)/shard_map/pallas_call | solution.py:167
  26.2 6.6 %collective-permute-done.7.refs_7_ = bf16[1408,128]{1,0:T(8,128)(2,1)S(1)} collective-permute-done((bf16[1408,128]{1,0:T(8,128)(2,1)S(1)}, bf16[1408,128]{1,0:T(8,128)(2,1)S(1)}, u32[]{:S(2)}, u32[]{:S(2)}) %collective-permute-start.7) | collective-permute-done | bytes 360480 | tf_op jit(solution)/shard_map/ppermute | solution.py:467
  33.0 1.6 %collective-permute-start.11 = (bf16[1408,128]{1,0:T(8,128)(2,1)S(1)}, bf16[1408,128]{1,0:T(8,128)(2,1)S(1)}, u32[]{:S(2)}, u32[]{:S(2)}) collective-permute-start(bf16[1408,128]{1,0:T(8,128)(2,1)S(1)} %get-tuple-element.42.refs_5_), channel_id=1, source_target_pairs={{0,2},{1,5},{2,0},{3,7},{4,6},{5,1},{6,4},{7,3},{8,10},{9,13},{10,... | collective-permute-start | bytes 1081352 | tf_op jit(solution)/shard_map/ppermute | solution.py:467
  35.8 2.3 %shard_map.52 = (bf16[4,2,768,384]{3,2,1,0:T(8,128)(2,1)S(1)}, bf16[2,768,384]{2,1,0:T(8,128)(2,1)S(1)}, bf16[768,768]{1,0:T(8,128)(2,1)S(1)}, bf16[768,384]{1,0:T(8,128)(2,1)S(1)}, bf16[192,384]{1,0:T(8,128)(2,1)S(1)}) custom-call(bf16[4,2,768,384]{3,2,1,0:T(8,128)(2,1)S(1)} %get-tuple-element.40.refs_0_, ...), custom_call_target="tpu_custom_call", output_to_operand_aliasing={{0}: (0, {})} | custom-call | flops 1811939328 | bytes 14893056 | tf_op jit(solution)/shard_map/pallas_call | solution.py:167
  38.2 2.2 %collective-permute-done.11.refs_9_ = bf16[1408,128]{1,0:T(8,128)(2,1)S(1)} collective-permute-done((bf16[1408,128]{1,0:T(8,128)(2,1)S(1)}, bf16[1408,128]{1,0:T(8,128)(2,1)S(1)}, u32[]{:S(2)}, u32[]{:S(2)}) %collective-permute-start.11) | collective-permute-done | bytes 360480 | tf_op jit(solution)/shard_map/ppermute | solution.py:467
  41.6 2.7 %collective-permute-done.13.refs_11_ = bf16[1408,128]{1,0:T(8,128)(2,1)S(1)} collective-permute-done((bf16[1408,128]{1,0:T(8,128)(2,1)S(1)}, bf16[1408,128]{1,0:T(8,128)(2,1)S(1)}, u32[]{:S(2)}, u32[]{:S(2)}) %collective-permute-start.13) | collective-permute-done | bytes 360480 | tf_op jit(solution)/shard_map/ppermute | solution.py:467
  44.5 1.5 %collective-permute-start.16 = (bf16[192,384]{1,0:T(8,128)(2,1)S(1)}, bf16[192,384]{1,0:T(8,128)(2,1)S(1)}, u32[]{:S(2)}, u32[]{:S(2)}) collective-permute-start(bf16[192,384]{1,0:T(8,128)(2,1)S(1)} %get-tuple-element.49), channel_id=1, source_target_pairs={{8,0},{10,2},{12,4},{14,6},{24,16},{26,18},{28,20},{30,22},{9,1},{... | collective-permute-start | bytes 442376 | tf_op jit(solution)/shard_map/ppermute | solution.py:480
  46.0 5.9 %shard_map.54 = (f32[768,384]{1,0:T(8,128)S(1)}, bf16[1408,128]{1,0:T(8,128)(2,1)S(1)}, bf16[768,768]{1,0:T(8,128)(2,1)S(1)}, bf16[768,768]{1,0:T(8,128)(2,1)S(1)}) custom-call(f32[768,384]{1,0:T(8,128)S(1)} %get-tuple-element.39.refs_0_.base, bf16[4,2,768,384]{3,2,1,0:T(8,128)(2,1)S(1)} %get-tuple-element.44.c.refs_1_, ...), custom_call_target="tpu_custom_call" | custom-call | flops 3623878656 | bytes 19759104 | tf_op jit(solution)/shard_map/pallas_call | solution.py:167
  56.9 3.0 %collective-permute-start.20 = (bf16[192,384]{1,0:T(8,128)(2,1)S(1)}, bf16[192,384]{1,0:T(8,128)(2,1)S(1)}, u32[]{:S(2)}, u32[]{:S(2)}) collective-permute-start(bf16[192,384]{1,0:T(8,128)(2,1)S(1)} %collective-permute-done.16.refs_0_), channel_id=1, source_target_pairs={{0,4},{1,5},{2,6},{3,7},{4,0},{5,1},{6,2},{7,3},{8,12},{9,13},{10,... | collective-permute-start | bytes 442376 | tf_op jit(solution)/shard_map/ppermute | solution.py:467
  60.4 2.3 %shard_map.56 = (bf16[2,768,384]{2,1,0:T(8,128)(2,1)}, bf16[768,768]{1,0:T(8,128)(2,1)S(1)}, bf16[2,768,384]{2,1,0:T(8,128)(2,1)S(1)}, bf16[768,768]{1,0:T(8,128)(2,1)S(1)}) custom-call(bf16[4,2,768,384]{3,2,1,0:T(8,128)(2,1)S(1)} %get-tuple-element.44.c.refs_1_, bf16[2,768,384]{2,1,0:T(8,128)(2,1)S(1)} %get-tuple-element.46.c01.refs_3_, ...), custom_call_target="tpu_custom_call" | custom-call | flops 1811939328 | bytes 11796480 | tf_op jit(solution)/shard_map/pallas_call | solution.py:167
  62.7 1.9 %collective-permute-done.18.refs_0_ = bf16[192,384]{1,0:T(8,128)(2,1)S(1)} collective-permute-done((bf16[192,384]{1,0:T(8,128)(2,1)S(1)}, bf16[192,384]{1,0:T(8,128)(2,1)S(1)}, u32[]{:S(2)}, u32[]{:S(2)}) %collective-permute-start.18) | collective-permute-done | bytes 147488 | tf_op jit(solution)/shard_map/ppermute | solution.py:480
  64.6 2.6 %collective-permute-done.20.refs_2_ = bf16[192,384]{1,0:T(8,128)(2,1)S(1)} collective-permute-done((bf16[192,384]{1,0:T(8,128)(2,1)S(1)}, bf16[192,384]{1,0:T(8,128)(2,1)S(1)}, u32[]{:S(2)}, u32[]{:S(2)}) %collective-permute-start.20) | collective-permute-done | bytes 147488 | tf_op jit(solution)/shard_map/ppermute | solution.py:467
  67.9 1.7 %collective-permute-done.22.refs_1_ = bf16[1408,128]{1,0:T(8,128)(2,1)S(1)} collective-permute-done((bf16[1408,128]{1,0:T(8,128)(2,1)S(1)}, bf16[1408,128]{1,0:T(8,128)(2,1)S(1)}, u32[]{:S(2)}, u32[]{:S(2)}) %collective-permute-start.22) | collective-permute-done | bytes 360480 | tf_op jit(solution)/shard_map/ppermute | solution.py:456
  69.5 1.6 %shard_map.59 = (bf16[352,128]{1,0:T(8,128)(2,1)S(1)}, bf16[768,768]{1,0:T(8,128)(2,1)S(1)}) custom-call(f32[768,384]{1,0:T(8,128)S(1)} %get-tuple-element.52.agg, bf16[768,384]{1,0:T(8,128)(2,1)S(1)} %get-tuple-element.55.agg_cols, bf16[768,768]{1,0:T(8,128)(2,1)S(1)} %get-tuple-element.59.agg_t, bf16[1408,128]{1,0:T(8,128)(2,1)S(1)} %collective-permute-done.15.refs_0_, ...), custom_call_target="tpu_custom_call" | custom-call | flops 905969664 | bytes 4939776 | tf_op jit(solution)/shard_map/pallas_call | solution.py:167
  71.2 1.3 %collective-permute-start.23 = (bf16[352,128]{1,0:T(8,128)(2,1)S(1)}, bf16[352,128]{1,0:T(8,128)(2,1)S(1)}, u32[]{:S(2)}, u32[]{:S(2)}) collective-permute-start(bf16[352,128]{1,0:T(8,128)(2,1)S(1)} %get-tuple-element.64), channel_id=1, source_target_pairs={{16,0},{18,2},{20,4},{22,6},{17,1},{19,3},{21,5},{23,7}} | collective-permute-start | bytes 270344 | tf_op jit(solution)/shard_map/ppermute | solution.py:480
  72.5 1.4 %collective-permute-start.25 = (bf16[192,384]{1,0:T(8,128)(2,1)S(1)}, bf16[192,384]{1,0:T(8,128)(2,1)S(1)}, u32[]{:S(2)}, u32[]{:S(2)}) collective-permute-start(bf16[192,384]{1,0:T(8,128)(2,1)S(1)} %collective-permute-done.16.refs_0_), channel_id=1, source_target_pairs={{0,2},{1,3},{2,0},{3,1},{4,6},{5,7},{6,4},{7,5},{8,10},{9,11},{10,... | collective-permute-start | bytes 442376 | tf_op jit(solution)/shard_map/ppermute | solution.py:467
  74.5 2.3 %collective-permute-start.28 = (bf16[192,384]{1,0:T(8,128)(2,1)S(1)}, bf16[192,384]{1,0:T(8,128)(2,1)S(1)}, u32[]{:S(2)}, u32[]{:S(2)}) collective-permute-start(bf16[192,384]{1,0:T(8,128)(2,1)S(1)} %shard_map.58.refs_0_), channel_id=1, source_target_pairs={{0,4},{1,5},{2,6},{3,7},{4,0},{5,1},{6,2},{7,3},{8,12},{9,13},{10,... | collective-permute-start | bytes 442376 | tf_op jit(solution)/shard_map/ppermute | solution.py:467
  77.5 1.8 %collective-permute-done.23.refs_0_ = bf16[352,128]{1,0:T(8,128)(2,1)S(1)} collective-permute-done((bf16[352,128]{1,0:T(8,128)(2,1)S(1)}, bf16[352,128]{1,0:T(8,128)(2,1)S(1)}, u32[]{:S(2)}, u32[]{:S(2)}) %collective-permute-start.23) | collective-permute-done | bytes 90144 | tf_op jit(solution)/shard_map/ppermute | solution.py:480
  79.3 1.8 %collective-permute-start.29 = (bf16[192,384]{1,0:T(8,128)(2,1)S(1)}, bf16[192,384]{1,0:T(8,128)(2,1)S(1)}, u32[]{:S(2)}, u32[]{:S(2)}) collective-permute-start(bf16[192,384]{1,0:T(8,128)(2,1)S(1)} %shard_map.58.refs_0_), channel_id=1, source_target_pairs={{0,6},{1,7},{2,4},{3,5},{4,2},{5,3},{6,0},{7,1},{8,14},{9,15},{10,... | collective-permute-start | bytes 442376 | tf_op jit(solution)/shard_map/ppermute | solution.py:467
  81.1 1.5 %collective-permute-start.30 = (bf16[352,128]{1,0:T(8,128)(2,1)S(1)}, bf16[352,128]{1,0:T(8,128)(2,1)S(1)}, u32[]{:S(2)}, u32[]{:S(2)}) collective-permute-start(bf16[352,128]{1,0:T(8,128)(2,1)S(1)} %shard_map.60.refs_0_), channel_id=1, source_target_pairs={{0,2},{1,3},{2,0},{3,1},{4,6},{5,7},{6,4},{7,5},{8,10},{9,11},{10,... | collective-permute-start | bytes 270344 | tf_op jit(solution)/shard_map/ppermute | solution.py:467
  82.9 1.9 %collective-permute-start.32 = (bf16[352,128]{1,0:T(8,128)(2,1)S(1)}, bf16[352,128]{1,0:T(8,128)(2,1)S(1)}, u32[]{:S(2)}, u32[]{:S(2)}) collective-permute-start(bf16[352,128]{1,0:T(8,128)(2,1)S(1)} %shard_map.60.refs_0_), channel_id=1, source_target_pairs={{0,6},{1,7},{2,4},{3,5},{4,2},{5,3},{6,0},{7,1},{8,14},{9,15},{10,... | collective-permute-start | bytes 270344 | tf_op jit(solution)/shard_map/ppermute | solution.py:467
  85.0 1.6 %shard_map.61.refs_0_ = f32[768,384]{1,0:T(8,128)S(1)} custom-call(f32[768,384]{1,0:T(8,128)S(1)} %shard_map.55.cov, bf16[2,768,384]{2,1,0:T(8,128)(2,1)S(1)} %get-tuple-element.68.mine.refs_0_, bf16[768,768]{1,0:T(8,128)(2,1)S(1)} %get-tuple-element.66.mine_t.refs_1_, bf16[768,768]{1,0:T(8,128)(2,1)S(1)} %get-tuple-element.67.right), custom_call_target="tpu_custom_call" | custom-call | flops 905969664 | bytes 5898240 | tf_op jit(solution)/shard_map/pallas_call | solution.py:167
  89.1 1.3 %collective-permute-done.32.refs_3_ = bf16[352,128]{1,0:T(8,128)(2,1)S(1)} collective-permute-done((bf16[352,128]{1,0:T(8,128)(2,1)S(1)}, bf16[352,128]{1,0:T(8,128)(2,1)S(1)}, u32[]{:S(2)}, u32[]{:S(2)}) %collective-permute-start.32) | collective-permute-done | bytes 90144 | tf_op jit(solution)/shard_map/ppermute | solution.py:467
  91.1 1.8 %shard_map.63 = (bf16[2,768,384]{2,1,0:T(8,128)(2,1)S(1)}, bf16[768,768]{1,0:T(8,128)(2,1)S(1)}) custom-call(bf16[2,768,384]{2,1,0:T(8,128)(2,1)S(1)} %get-tuple-element.68.mine.refs_0_, bf16[768,768]{1,0:T(8,128)(2,1)S(1)} %get-tuple-element.66.mine_t.refs_1_, bf16[768,384]{1,0:T(8,128)(2,1)S(1)} %shard_map.62.refs_2_, ...), custom_call_target="tpu_custom_call" | custom-call | flops 905969664 | bytes 5898240 | tf_op jit(solution)/shard_map/pallas_call | solution.py:167
  93.0 3.5 %shard_map.66 = (f32[1,768,384]{2,1,0:T(8,128)}, bf16[1,768,384]{2,1,0:T(8,128)(2,1)}) custom-call(f32[768,384]{1,0:T(8,128)S(1)} %shard_map.61.refs_0_, bf16[2,768,384]{2,1,0:T(8,128)(2,1)S(1)} %get-tuple-element.69.refs_1_, bf16[768,768]{1,0:T(8,128)(2,1)S(1)} %get-tuple-element.70.refs_2_, bf16[768,384]{1,0:T(8,128)(2,1)S(1)} %shard_map.64.refs_3_, ...), custom_call_target="tpu_custom_call" | custom-call | flops 1358954496 | bytes 7208960 | tf_op jit(solution)/shard_map/pallas_call | solution.py:167
  (61 shorter events, 15.1 us)
Async XLA Ops:
  2.1 16.7 %collective-permute-start.2 = (bf16[768,384]{1,0:T(8,128)(2,1)S(1)}, bf16[768,384]{1,0:T(8,128)(2,1)S(1)}, u32[]{:S(2)}, u32[]{:S(2)}) collective-permute-start(bf16[768,384]{1,0:T(8,128)(2,1)S(1)} %convert_bitcast_fusion.refs_4_.refs_0_), channel_id=1, source_target_pairs={{0,4},{1,3},{2,6},{3,1},{4,0},{5,7},{6,2},{7,5},{8,12},{9,11},{10,... | collective-permute-start | bytes 1769480 | tf_op jit(solution)/shard_map/ppermute | solution.py:467
  5.2 13.7 %collective-permute-start.4 = (bf16[768,384]{1,0:T(8,128)(2,1)S(1)}, bf16[768,384]{1,0:T(8,128)(2,1)S(1)}, u32[]{:S(2)}, u32[]{:S(2)}) collective-permute-start(bf16[768,384]{1,0:T(8,128)(2,1)S(1)} %convert_bitcast_fusion.refs_4_.refs_0_), channel_id=1, source_target_pairs={{0,2},{1,5},{2,0},{3,7},{4,6},{5,1},{6,4},{7,3},{8,10},{9,13},{10,... | collective-permute-start | bytes 1769480 | tf_op jit(solution)/shard_map/ppermute | solution.py:467
  6.7 14.1 %collective-permute-start = (bf16[768,384]{1,0:T(8,128)(2,1)S(1)}, bf16[768,384]{1,0:T(8,128)(2,1)S(1)}, u32[]{:S(2)}, u32[]{:S(2)}) collective-permute-start(bf16[768,384]{1,0:T(8,128)(2,1)S(1)} %convert_element_type.10.refs_2_), channel_id=1, source_target_pairs={{1,0},{0,1},{3,2},{2,3},{5,4},{4,5},{7,6},{6,7},{9,8},{8,9},{11,10... | collective-permute-start | bytes 1769480 | tf_op jit(solution)/shard_map/ppermute | solution.py:456
  6.8 14.0 %collective-permute-start.1 = (bf16[768,384]{1,0:T(8,128)(2,1)S(1)}, bf16[768,384]{1,0:T(8,128)(2,1)S(1)}, u32[]{:S(2)}, u32[]{:S(2)}) collective-permute-start(bf16[768,384]{1,0:T(8,128)(2,1)S(1)} %convert_bitcast_fusion.refs_4_.refs_0_), channel_id=1, source_target_pairs={{1,0},{0,1},{3,2},{2,3},{5,4},{4,5},{7,6},{6,7},{9,8},{8,9},{11,10... | collective-permute-start | bytes 1769480 | tf_op jit(solution)/shard_map/ppermute | solution.py:456
  18.8 5.5 %collective-permute-start.3 = (bf16[768,384]{1,0:T(8,128)(2,1)S(1)}, bf16[768,384]{1,0:T(8,128)(2,1)S(1)}, u32[]{:S(2)}, u32[]{:S(2)}) collective-permute-start(bf16[768,384]{1,0:T(8,128)(2,1)S(1)} %collective-permute-done.2.refs_2_), channel_id=1, source_target_pairs={{1,0},{0,1},{3,2},{2,3},{5,4},{4,5},{7,6},{6,7},{9,8},{8,9},{11,10... | collective-permute-start | bytes 1769480 | tf_op jit(solution)/shard_map/ppermute | solution.py:456
  18.8 5.5 %collective-permute-start.5 = (bf16[768,384]{1,0:T(8,128)(2,1)S(1)}, bf16[768,384]{1,0:T(8,128)(2,1)S(1)}, u32[]{:S(2)}, u32[]{:S(2)}) collective-permute-start(bf16[768,384]{1,0:T(8,128)(2,1)S(1)} %collective-permute-done.4.refs_4_), channel_id=1, source_target_pairs={{1,0},{0,1},{3,2},{2,3},{5,4},{4,5},{7,6},{6,7},{9,8},{8,9},{11,10... | collective-permute-start | bytes 1769480 | tf_op jit(solution)/shard_map/ppermute | solution.py:456
  19.3 13.5 %collective-permute-start.6 = (bf16[768,384]{1,0:T(8,128)(2,1)S(1)}, bf16[768,384]{1,0:T(8,128)(2,1)S(1)}, u32[]{:S(2)}, u32[]{:S(2)}) collective-permute-start(bf16[768,384]{1,0:T(8,128)(2,1)S(1)} %collective-permute-done.2.refs_2_), channel_id=1, source_target_pairs={{0,2},{1,5},{2,0},{3,7},{4,6},{5,1},{6,4},{7,3},{8,10},{9,13},{10,... | collective-permute-start | bytes 1769480 | tf_op jit(solution)/shard_map/ppermute | solution.py:467
  22.6 10.3 %collective-permute-start.7 = (bf16[1408,128]{1,0:T(8,128)(2,1)S(1)}, bf16[1408,128]{1,0:T(8,128)(2,1)S(1)}, u32[]{:S(2)}, u32[]{:S(2)}) collective-permute-start(bf16[1408,128]{1,0:T(8,128)(2,1)S(1)} %get-tuple-element.42.refs_5_), channel_id=1, source_target_pairs={{0,4},{1,3},{2,6},{3,1},{4,0},{5,7},{6,2},{7,5},{8,12},{9,11},{10,... | collective-permute-start | bytes 1081352 | tf_op jit(solution)/shard_map/ppermute | solution.py:467
  32.9 3.0 %collective-permute-start.8 = (bf16[768,384]{1,0:T(8,128)(2,1)S(1)}, bf16[768,384]{1,0:T(8,128)(2,1)S(1)}, u32[]{:S(2)}, u32[]{:S(2)}) collective-permute-start(bf16[768,384]{1,0:T(8,128)(2,1)S(1)} %collective-permute-done.6.refs_2_), channel_id=1, source_target_pairs={{1,0},{0,1},{3,2},{2,3},{5,4},{4,5},{7,6},{6,7},{9,8},{8,9},{11,10... | collective-permute-start | bytes 1769480 | tf_op jit(solution)/shard_map/ppermute | solution.py:456
  33.0 7.4 %collective-permute-start.11 = (bf16[1408,128]{1,0:T(8,128)(2,1)S(1)}, bf16[1408,128]{1,0:T(8,128)(2,1)S(1)}, u32[]{:S(2)}, u32[]{:S(2)}) collective-permute-start(bf16[1408,128]{1,0:T(8,128)(2,1)S(1)} %get-tuple-element.42.refs_5_), channel_id=1, source_target_pairs={{0,2},{1,5},{2,0},{3,7},{4,6},{5,1},{6,4},{7,3},{8,10},{9,13},{10,... | collective-permute-start | bytes 1081352 | tf_op jit(solution)/shard_map/ppermute | solution.py:467
  34.6 9.7 %collective-permute-start.13 = (bf16[1408,128]{1,0:T(8,128)(2,1)S(1)}, bf16[1408,128]{1,0:T(8,128)(2,1)S(1)}, u32[]{:S(2)}, u32[]{:S(2)}) collective-permute-start(bf16[1408,128]{1,0:T(8,128)(2,1)S(1)} %collective-permute-done.7.refs_7_), channel_id=1, source_target_pairs={{0,2},{1,5},{2,0},{3,7},{4,6},{5,1},{6,4},{7,3},{8,10},{9,13},{10,... | collective-permute-start | bytes 1081352 | tf_op jit(solution)/shard_map/ppermute | solution.py:467
  35.0 10.9 %collective-permute-start.9 = (bf16[1408,128]{1,0:T(8,128)(2,1)S(1)}, bf16[1408,128]{1,0:T(8,128)(2,1)S(1)}, u32[]{:S(2)}, u32[]{:S(2)}) collective-permute-start(bf16[1408,128]{1,0:T(8,128)(2,1)S(1)} %get-tuple-element.42.refs_5_), channel_id=1, source_target_pairs={{1,0},{0,1},{3,2},{2,3},{5,4},{4,5},{7,6},{6,7},{9,8},{8,9},{11,10... | collective-permute-start | bytes 1081352 | tf_op jit(solution)/shard_map/ppermute | solution.py:456
  35.8 10.1 %collective-permute-start.10 = (bf16[1408,128]{1,0:T(8,128)(2,1)S(1)}, bf16[1408,128]{1,0:T(8,128)(2,1)S(1)}, u32[]{:S(2)}, u32[]{:S(2)}) collective-permute-start(bf16[1408,128]{1,0:T(8,128)(2,1)S(1)} %collective-permute-done.7.refs_7_), channel_id=1, source_target_pairs={{1,0},{0,1},{3,2},{2,3},{5,4},{4,5},{7,6},{6,7},{9,8},{8,9},{11,10... | collective-permute-start | bytes 1081352 | tf_op jit(solution)/shard_map/ppermute | solution.py:456
  40.4 5.6 %collective-permute-start.12 = (bf16[1408,128]{1,0:T(8,128)(2,1)S(1)}, bf16[1408,128]{1,0:T(8,128)(2,1)S(1)}, u32[]{:S(2)}, u32[]{:S(2)}) collective-permute-start(bf16[1408,128]{1,0:T(8,128)(2,1)S(1)} %collective-permute-done.11.refs_9_), channel_id=1, source_target_pairs={{1,0},{0,1},{3,2},{2,3},{5,4},{4,5},{7,6},{6,7},{9,8},{8,9},{11,10... | collective-permute-start | bytes 1081352 | tf_op jit(solution)/shard_map/ppermute | solution.py:456
  44.5 8.7 %collective-permute-start.16 = (bf16[192,384]{1,0:T(8,128)(2,1)S(1)}, bf16[192,384]{1,0:T(8,128)(2,1)S(1)}, u32[]{:S(2)}, u32[]{:S(2)}) collective-permute-start(bf16[192,384]{1,0:T(8,128)(2,1)S(1)} %get-tuple-element.49), channel_id=1, source_target_pairs={{8,0},{10,2},{12,4},{14,6},{24,16},{26,18},{28,20},{30,22},{9,1},{... | collective-permute-start | bytes 442376 | tf_op jit(solution)/shard_map/ppermute | solution.py:480
  51.9 16.0 %collective-permute-start.15 = (bf16[1408,128]{1,0:T(8,128)(2,1)S(1)}, bf16[1408,128]{1,0:T(8,128)(2,1)S(1)}, u32[]{:S(2)}, u32[]{:S(2)}) collective-permute-start(bf16[1408,128]{1,0:T(8,128)(2,1)S(1)} %get-tuple-element.57), channel_id=1, source_target_pairs={{8,0},{10,2},{12,4},{14,6},{24,16},{26,18},{28,20},{30,22},{9,1},{... | collective-permute-start | bytes 1081352 | tf_op jit(solution)/shard_map/ppermute | solution.py:480
  54.9 9.7 %collective-permute-start.18 = (bf16[192,384]{1,0:T(8,128)(2,1)S(1)}, bf16[192,384]{1,0:T(8,128)(2,1)S(1)}, u32[]{:S(2)}, u32[]{:S(2)}) collective-permute-start(bf16[192,384]{1,0:T(8,128)(2,1)S(1)} %shard_map.57), channel_id=1, source_target_pairs={{16,0},{18,2},{20,4},{22,6},{17,1},{19,3},{21,5},{23,7}} | collective-permute-start | bytes 442376 | tf_op jit(solution)/shard_map/ppermute | solution.py:480
  56.2 8.4 %collective-permute-start.19 = (bf16[192,384]{1,0:T(8,128)(2,1)S(1)}, bf16[192,384]{1,0:T(8,128)(2,1)S(1)}, u32[]{:S(2)}, u32[]{:S(2)}) collective-permute-start(bf16[192,384]{1,0:T(8,128)(2,1)S(1)} %shard_map.57), channel_id=1, source_target_pairs={{16,8},{18,10},{20,12},{22,14},{17,9},{19,11},{21,13},{23,15}} | collective-permute-start | bytes 442376 | tf_op jit(solution)/shard_map/ppermute | solution.py:480
  56.9 10.3 %collective-permute-start.20 = (bf16[192,384]{1,0:T(8,128)(2,1)S(1)}, bf16[192,384]{1,0:T(8,128)(2,1)S(1)}, u32[]{:S(2)}, u32[]{:S(2)}) collective-permute-start(bf16[192,384]{1,0:T(8,128)(2,1)S(1)} %collective-permute-done.16.refs_0_), channel_id=1, source_target_pairs={{0,4},{1,5},{2,6},{3,7},{4,0},{5,1},{6,2},{7,3},{8,12},{9,13},{10,... | collective-permute-start | bytes 442376 | tf_op jit(solution)/shard_map/ppermute | solution.py:467
  60.0 7.3 %collective-permute-start.21 = (bf16[192,384]{1,0:T(8,128)(2,1)S(1)}, bf16[192,384]{1,0:T(8,128)(2,1)S(1)}, u32[]{:S(2)}, u32[]{:S(2)}) collective-permute-start(bf16[192,384]{1,0:T(8,128)(2,1)S(1)} %collective-permute-done.16.refs_0_), channel_id=1, source_target_pairs={{0,6},{1,7},{2,4},{3,5},{4,2},{5,3},{6,0},{7,1},{8,14},{9,15},{10,... | collective-permute-start | bytes 442376 | tf_op jit(solution)/shard_map/ppermute | solution.py:467
  71.2 8.1 %collective-permute-start.23 = (bf16[352,128]{1,0:T(8,128)(2,1)S(1)}, bf16[352,128]{1,0:T(8,128)(2,1)S(1)}, u32[]{:S(2)}, u32[]{:S(2)}) collective-permute-start(bf16[352,128]{1,0:T(8,128)(2,1)S(1)} %get-tuple-element.64), channel_id=1, source_target_pairs={{16,0},{18,2},{20,4},{22,6},{17,1},{19,3},{21,5},{23,7}} | collective-permute-start | bytes 270344 | tf_op jit(solution)/shard_map/ppermute | solution.py:480
  72.5 10.1 %collective-permute-start.25 = (bf16[192,384]{1,0:T(8,128)(2,1)S(1)}, bf16[192,384]{1,0:T(8,128)(2,1)S(1)}, u32[]{:S(2)}, u32[]{:S(2)}) collective-permute-start(bf16[192,384]{1,0:T(8,128)(2,1)S(1)} %collective-permute-done.16.refs_0_), channel_id=1, source_target_pairs={{0,2},{1,3},{2,0},{3,1},{4,6},{5,7},{6,4},{7,5},{8,10},{9,11},{10,... | collective-permute-start | bytes 442376 | tf_op jit(solution)/shard_map/ppermute | solution.py:467
  73.8 9.1 %collective-permute-start.27 = (bf16[192,384]{1,0:T(8,128)(2,1)S(1)}, bf16[192,384]{1,0:T(8,128)(2,1)S(1)}, u32[]{:S(2)}, u32[]{:S(2)}) collective-permute-start(bf16[192,384]{1,0:T(8,128)(2,1)S(1)} %shard_map.58.refs_0_), channel_id=1, source_target_pairs={{0,2},{1,3},{2,0},{3,1},{4,6},{5,7},{6,4},{7,5},{8,10},{9,11},{10,... | collective-permute-start | bytes 442376 | tf_op jit(solution)/shard_map/ppermute | solution.py:467
  74.5 10.3 %collective-permute-start.28 = (bf16[192,384]{1,0:T(8,128)(2,1)S(1)}, bf16[192,384]{1,0:T(8,128)(2,1)S(1)}, u32[]{:S(2)}, u32[]{:S(2)}) collective-permute-start(bf16[192,384]{1,0:T(8,128)(2,1)S(1)} %shard_map.58.refs_0_), channel_id=1, source_target_pairs={{0,4},{1,5},{2,6},{3,7},{4,0},{5,1},{6,2},{7,3},{8,12},{9,13},{10,... | collective-permute-start | bytes 442376 | tf_op jit(solution)/shard_map/ppermute | solution.py:467
  76.9 4.3 %collective-permute-start.24 = (bf16[352,128]{1,0:T(8,128)(2,1)S(1)}, bf16[352,128]{1,0:T(8,128)(2,1)S(1)}, u32[]{:S(2)}, u32[]{:S(2)}) collective-permute-start(bf16[352,128]{1,0:T(8,128)(2,1)S(1)} %get-tuple-element.64), channel_id=1, source_target_pairs={{16,8},{18,10},{20,12},{22,14},{17,9},{19,11},{21,13},{23,15}} | collective-permute-start | bytes 270344 | tf_op jit(solution)/shard_map/ppermute | solution.py:480
  79.3 8.0 %collective-permute-start.29 = (bf16[192,384]{1,0:T(8,128)(2,1)S(1)}, bf16[192,384]{1,0:T(8,128)(2,1)S(1)}, u32[]{:S(2)}, u32[]{:S(2)}) collective-permute-start(bf16[192,384]{1,0:T(8,128)(2,1)S(1)} %shard_map.58.refs_0_), channel_id=1, source_target_pairs={{0,6},{1,7},{2,4},{3,5},{4,2},{5,3},{6,0},{7,1},{8,14},{9,15},{10,... | collective-permute-start | bytes 442376 | tf_op jit(solution)/shard_map/ppermute | solution.py:467
  81.1 7.4 %collective-permute-start.30 = (bf16[352,128]{1,0:T(8,128)(2,1)S(1)}, bf16[352,128]{1,0:T(8,128)(2,1)S(1)}, u32[]{:S(2)}, u32[]{:S(2)}) collective-permute-start(bf16[352,128]{1,0:T(8,128)(2,1)S(1)} %shard_map.60.refs_0_), channel_id=1, source_target_pairs={{0,2},{1,3},{2,0},{3,1},{4,6},{5,7},{6,4},{7,5},{8,10},{9,11},{10,... | collective-permute-start | bytes 270344 | tf_op jit(solution)/shard_map/ppermute | solution.py:467
  82.6 6.5 %collective-permute-start.31 = (bf16[352,128]{1,0:T(8,128)(2,1)S(1)}, bf16[352,128]{1,0:T(8,128)(2,1)S(1)}, u32[]{:S(2)}, u32[]{:S(2)}) collective-permute-start(bf16[352,128]{1,0:T(8,128)(2,1)S(1)} %shard_map.60.refs_0_), channel_id=1, source_target_pairs={{0,4},{1,5},{2,6},{3,7},{4,0},{5,1},{6,2},{7,3},{8,12},{9,13},{10,... | collective-permute-start | bytes 270344 | tf_op jit(solution)/shard_map/ppermute | solution.py:467
  82.9 7.5 %collective-permute-start.32 = (bf16[352,128]{1,0:T(8,128)(2,1)S(1)}, bf16[352,128]{1,0:T(8,128)(2,1)S(1)}, u32[]{:S(2)}, u32[]{:S(2)}) collective-permute-start(bf16[352,128]{1,0:T(8,128)(2,1)S(1)} %shard_map.60.refs_0_), channel_id=1, source_target_pairs={{0,6},{1,7},{2,4},{3,5},{4,2},{5,3},{6,0},{7,1},{8,14},{9,15},{10,... | collective-permute-start | bytes 270344 | tf_op jit(solution)/shard_map/ppermute | solution.py:467
  84.9 6.1 %collective-permute-start.26 = (bf16[768,384]{1,0:T(8,128)(2,1)S(1)}, bf16[768,384]{1,0:T(8,128)(2,1)S(1)}, u32[]{:S(2)}, u32[]{:S(2)}) collective-permute-start(bf16[768,384]{1,0:T(8,128)(2,1)S(1)} %shard_map.62.refs_2_), channel_id=1, source_target_pairs={{1,0},{0,1},{3,2},{2,3},{5,4},{4,5},{7,6},{6,7},{9,8},{8,9},{11,10... | collective-permute-start | bytes 1769480 | tf_op jit(solution)/shard_map/ppermute | solution.py:456
  90.4 2.5 %collective-permute-start.33 = (bf16[768,384]{1,0:T(8,128)(2,1)S(1)}, bf16[768,384]{1,0:T(8,128)(2,1)S(1)}, u32[]{:S(2)}, u32[]{:S(2)}) collective-permute-start(bf16[768,384]{1,0:T(8,128)(2,1)S(1)} %shard_map.64.refs_3_), channel_id=1, source_target_pairs={{1,0},{0,1},{3,2},{2,3},{5,4},{4,5},{7,6},{6,7},{9,8},{8,9},{11,10... | collective-permute-start | bytes 1769480 | tf_op jit(solution)/shard_map/ppermute | solution.py:456
  90.5 2.5 %collective-permute-start.34 = (bf16[1408,128]{1,0:T(8,128)(2,1)S(1)}, bf16[1408,128]{1,0:T(8,128)(2,1)S(1)}, u32[]{:S(2)}, u32[]{:S(2)}) collective-permute-start(bf16[1408,128]{1,0:T(8,128)(2,1)S(1)} %shard_map.65.refs_5_), channel_id=1, source_target_pairs={{1,0},{0,1},{3,2},{2,3},{5,4},{4,5},{7,6},{6,7},{9,8},{8,9},{11,10... | collective-permute-start | bytes 1081352 | tf_op jit(solution)/shard_map/ppermute | solution.py:456
  (5 other events, 31.0 us)

commit v5 on v3

--- a/solution.py
+++ b/solution.py
@@ -663,7 +663,7 @@
             [],
             n * one,
         )
-        s_parts = over_panels(after(s_got, mine, cov, c_far, c_blocks[2], c_blocks[3]))
+        s_parts = over_panels(after(s_got, mine, cov, c_far, *c_blocks[1:]))
         outs = call(
             functools.partial(pair_cov_kernel, n, to_last),
             [agg, agg_cols, agg_t, *s_parts],

time: 95.6 us -> 97.3 us (1.018)
    ppermute x6, waiting for transfers between devices: 5.66 us -> 7.26 us  [across(): got.append(lax.ppermute(x, 'tm', pairs))]
    ppermute x15, starting transfers between devices: 21.9 us -> 23.2 us  [swap(): return lax.ppermute(value, ('tm', 'panel'), pairs)]
    ppermute x15, waiting for transfers between devices: 29 us -> 27.7 us  [swap(): return lax.ppermute(value, ('tm', 'panel'), pairs)]
  transfers between devices with their start and end apart: 35 -> 35, of which waited for: 13 -> 13; matrix products, arithmetic and copies ran while one was open for 0% -> 0% of each run, Pallas kernels for 24% -> 22%
where the time goes in v5:
time: 97.3 us; the launch traced here: 97 us
  waiting for transfers between devices  36.9 us (38%)
  starting transfers between devices  33.2 us (34%)
  Pallas kernels  24.4 us (25%)
  other arithmetic  1.55 us (2%)
    ppermute x15, waiting for transfers between devices, swap(): return lax.ppermute(value, ('tm', 'panel'), pairs)  27.7 us
    pallas_call x18, Pallas kernels, call(): pl.pallas_call(kernel, in_specs=in_specs, out_specs=[VMEM] * len(outs), o...  24.4 us
    ppermute x15, starting transfers between devices, swap(): return lax.ppermute(value, ('tm', 'panel'), pairs)  23.2 us
    ppermute x6, waiting for transfers between devices, across(): got.append(lax.ppermute(x, 'tm', pairs))  7.26 us
    ppermute x6, starting transfers between devices, across(): got.append(lax.ppermute(x, 'tm', pairs))  6.65 us
    ppermute x14, starting transfers between devices, over_panels(): lax.ppermute(x, 'panel', [((i + r) % n, i) for i in range(n)])  3.37 us
  transfers between devices with their start and end apart: 35, of which 13 were waited for; matrix products, arithmetic and copies ran while one was open for 0% of the time, Pallas kernels for 22%

profile of v5, /device:TPU:0, one launch (start us, length us, event | category | flops | bytes accessed | tf_op | source)
XLA Modules:
  0.0 97.0 jit_solution(18359373846839274494)
XLA Ops:
  0.6 1.5 %convert_bitcast_fusion.refs_4_.refs_0_ = bf16[768,384]{1,0:T(8,128)(2,1)S(1)} fusion(f32[1,768,384]{2,1,0:T(8,128)} %param.4), kind=kLoop, calls=%fused_computation | loop fusion | flops 294912 | bytes 1769472 | tf_op jit(solution)/shard_map/convert_element_type | solution.py:532
  2.1 3.0 %collective-permute-start.2 = (bf16[768,384]{1,0:T(8,128)(2,1)S(1)}, bf16[768,384]{1,0:T(8,128)(2,1)S(1)}, u32[]{:S(2)}, u32[]{:S(2)}) collective-permute-start(bf16[768,384]{1,0:T(8,128)(2,1)S(1)} %convert_bitcast_fusion.refs_4_.refs_0_), channel_id=1, source_target_pairs={{0,4},{1,3},{2,6},{3,1},{4,0},{5,7},{6,2},{7,5},{8,12},{9,11},{10,... | collective-permute-start | bytes 1769480 | tf_op jit(solution)/shard_map/ppermute | solution.py:478
  5.2 1.5 %collective-permute-start.4 = (bf16[768,384]{1,0:T(8,128)(2,1)S(1)}, bf16[768,384]{1,0:T(8,128)(2,1)S(1)}, u32[]{:S(2)}, u32[]{:S(2)}) collective-permute-start(bf16[768,384]{1,0:T(8,128)(2,1)S(1)} %convert_bitcast_fusion.refs_4_.refs_0_), channel_id=1, source_target_pairs={{0,2},{1,5},{2,0},{3,7},{4,6},{5,1},{6,4},{7,3},{8,10},{9,13},{10,... | collective-permute-start | bytes 1769480 | tf_op jit(solution)/shard_map/ppermute | solution.py:478
  7.3 11.5 %collective-permute-done.2.refs_2_ = bf16[768,384]{1,0:T(8,128)(2,1)S(1)} collective-permute-done((bf16[768,384]{1,0:T(8,128)(2,1)S(1)}, bf16[768,384]{1,0:T(8,128)(2,1)S(1)}, u32[]{:S(2)}, u32[]{:S(2)}) %collective-permute-start.2) | collective-permute-done | bytes 589856 | tf_op jit(solution)/shard_map/ppermute | solution.py:478
  19.3 1.5 %collective-permute-start.6 = (bf16[768,384]{1,0:T(8,128)(2,1)S(1)}, bf16[768,384]{1,0:T(8,128)(2,1)S(1)}, u32[]{:S(2)}, u32[]{:S(2)}) collective-permute-start(bf16[768,384]{1,0:T(8,128)(2,1)S(1)} %collective-permute-done.2.refs_2_), channel_id=1, source_target_pairs={{0,2},{1,5},{2,0},{3,7},{4,6},{5,1},{6,4},{7,3},{8,10},{9,13},{10,... | collective-permute-start | bytes 1769480 | tf_op jit(solution)/shard_map/ppermute | solution.py:478
  20.8 1.7 %shard_map.50 = (f32[768,384]{1,0:T(8,128)S(1)}, bf16[1408,128]{1,0:T(8,128)(2,1)S(1)}) custom-call(f32[768,384]{1,0:T(8,128)S(1)} %bitcast.4, f32[768,768]{1,0:T(8,128)S(1)} %copy-done.1, bf16[768,384]{1,0:T(8,128)(2,1)S(1)} %convert_element_type.10.refs_2_, bf16[768,384]{1,0:T(8,128)(2,1)S(1)} %collective-permute-done.refs_3_, ...), custom_call_target="tpu_custom_call" | custom-call | flops 905969664 | bytes 7438336 | tf_op jit(solution)/shard_map/pallas_call | solution.py:167
  22.6 1.8 %collective-permute-start.7 = (bf16[1408,128]{1,0:T(8,128)(2,1)S(1)}, bf16[1408,128]{1,0:T(8,128)(2,1)S(1)}, u32[]{:S(2)}, u32[]{:S(2)}) collective-permute-start(bf16[1408,128]{1,0:T(8,128)(2,1)S(1)} %get-tuple-element.43.refs_5_), channel_id=1, source_target_pairs={{0,4},{1,3},{2,6},{3,1},{4,0},{5,7},{6,2},{7,5},{8,12},{9,11},{10,... | collective-permute-start | bytes 1081352 | tf_op jit(solution)/shard_map/ppermute | solution.py:478
  24.3 1.9 %shard_map.51 = (bf16[4,2,768,384]{3,2,1,0:T(8,128)(2,1)S(1)}, bf16[4,768,768]{2,1,0:T(8,128)(2,1)S(1)}, bf16[768,768]{1,0:T(8,128)(2,1)S(1)}) custom-call(bf16[768,384]{1,0:T(8,128)(2,1)S(1)} %convert_bitcast_fusion.refs_4_.refs_0_, bf16[768,384]{1,0:T(8,128)(2,1)S(1)} %collective-permute-done.1.refs_5_.refs_1_, ...), custom_call_target="tpu_custom_call" | custom-call | flops 905969664 | bytes 14155776 | tf_op jit(solution)/shard_map/pallas_call | solution.py:167
  26.2 6.6 %collective-permute-done.7.refs_7_ = bf16[1408,128]{1,0:T(8,128)(2,1)S(1)} collective-permute-done((bf16[1408,128]{1,0:T(8,128)(2,1)S(1)}, bf16[1408,128]{1,0:T(8,128)(2,1)S(1)}, u32[]{:S(2)}, u32[]{:S(2)}) %collective-permute-start.7) | collective-permute-done | bytes 360480 | tf_op jit(solution)/shard_map/ppermute | solution.py:478
  33.0 1.6 %collective-permute-start.11 = (bf16[1408,128]{1,0:T(8,128)(2,1)S(1)}, bf16[1408,128]{1,0:T(8,128)(2,1)S(1)}, u32[]{:S(2)}, u32[]{:S(2)}) collective-permute-start(bf16[1408,128]{1,0:T(8,128)(2,1)S(1)} %get-tuple-element.43.refs_5_), channel_id=1, source_target_pairs={{0,2},{1,5},{2,0},{3,7},{4,6},{5,1},{6,4},{7,3},{8,10},{9,13},{10,... | collective-permute-start | bytes 1081352 | tf_op jit(solution)/shard_map/ppermute | solution.py:478
  35.8 2.3 %shard_map.52 = (bf16[4,2,768,384]{3,2,1,0:T(8,128)(2,1)S(1)}, bf16[2,768,384]{2,1,0:T(8,128)(2,1)S(1)}, bf16[768,768]{1,0:T(8,128)(2,1)S(1)}, bf16[768,384]{1,0:T(8,128)(2,1)S(1)}, bf16[192,384]{1,0:T(8,128)(2,1)S(1)}) custom-call(bf16[4,2,768,384]{3,2,1,0:T(8,128)(2,1)S(1)} %get-tuple-element.41.refs_0_, ...), custom_call_target="tpu_custom_call", output_to_operand_aliasing={{0}: (0, {})} | custom-call | flops 1811939328 | bytes 14893056 | tf_op jit(solution)/shard_map/pallas_call | solution.py:167
  38.2 2.2 %collective-permute-done.11.refs_9_ = bf16[1408,128]{1,0:T(8,128)(2,1)S(1)} collective-permute-done((bf16[1408,128]{1,0:T(8,128)(2,1)S(1)}, bf16[1408,128]{1,0:T(8,128)(2,1)S(1)}, u32[]{:S(2)}, u32[]{:S(2)}) %collective-permute-start.11) | collective-permute-done | bytes 360480 | tf_op jit(solution)/shard_map/ppermute | solution.py:478
  41.6 2.7 %collective-permute-done.13.refs_11_ = bf16[1408,128]{1,0:T(8,128)(2,1)S(1)} collective-permute-done((bf16[1408,128]{1,0:T(8,128)(2,1)S(1)}, bf16[1408,128]{1,0:T(8,128)(2,1)S(1)}, u32[]{:S(2)}, u32[]{:S(2)}) %collective-permute-start.13) | collective-permute-done | bytes 360480 | tf_op jit(solution)/shard_map/ppermute | solution.py:478
  44.5 1.5 %collective-permute-start.16 = (bf16[192,384]{1,0:T(8,128)(2,1)S(1)}, bf16[192,384]{1,0:T(8,128)(2,1)S(1)}, u32[]{:S(2)}, u32[]{:S(2)}) collective-permute-start(bf16[192,384]{1,0:T(8,128)(2,1)S(1)} %get-tuple-element.50), channel_id=1, source_target_pairs={{8,0},{10,2},{12,4},{14,6},{24,16},{26,18},{28,20},{30,22},{9,1},{... | collective-permute-start | bytes 442376 | tf_op jit(solution)/shard_map/ppermute | solution.py:491
  46.0 5.9 %shard_map.54 = (f32[768,384]{1,0:T(8,128)S(1)}, bf16[1408,128]{1,0:T(8,128)(2,1)S(1)}, bf16[768,768]{1,0:T(8,128)(2,1)S(1)}, bf16[768,768]{1,0:T(8,128)(2,1)S(1)}) custom-call(f32[768,384]{1,0:T(8,128)S(1)} %get-tuple-element.40.refs_0_.base, bf16[4,2,768,384]{3,2,1,0:T(8,128)(2,1)S(1)} %get-tuple-element.45.c.refs_1_, ...), custom_call_target="tpu_custom_call" | custom-call | flops 3623878656 | bytes 19759104 | tf_op jit(solution)/shard_map/pallas_call | solution.py:167
  54.4 1.3 %collective-permute-start.18 = (bf16[192,384]{1,0:T(8,128)(2,1)S(1)}, bf16[192,384]{1,0:T(8,128)(2,1)S(1)}, u32[]{:S(2)}, u32[]{:S(2)}) collective-permute-start(bf16[192,384]{1,0:T(8,128)(2,1)S(1)} %shard_map.57), channel_id=1, source_target_pairs={{16,0},{18,2},{20,4},{22,6},{17,1},{19,3},{21,5},{23,7}} | collective-permute-start | bytes 442376 | tf_op jit(solution)/shard_map/ppermute | solution.py:491
  56.5 2.7 %collective-permute-start.20 = (bf16[192,384]{1,0:T(8,128)(2,1)S(1)}, bf16[192,384]{1,0:T(8,128)(2,1)S(1)}, u32[]{:S(2)}, u32[]{:S(2)}) collective-permute-start(bf16[192,384]{1,0:T(8,128)(2,1)S(1)} %collective-permute-done.16.refs_0_.refs_3_), channel_id=1, source_target_pairs={{0,2},{1,3},{2,0},{3,1},{4,6},{5,7},{6,4},{7,5},{8,10},{9,11},{10,... | collective-permute-start | bytes 442376 | tf_op jit(solution)/shard_map/ppermute | solution.py:478
  60.2 3.6 %collective-permute-done.18.refs_0_ = bf16[192,384]{1,0:T(8,128)(2,1)S(1)} collective-permute-done((bf16[192,384]{1,0:T(8,128)(2,1)S(1)}, bf16[192,384]{1,0:T(8,128)(2,1)S(1)}, u32[]{:S(2)}, u32[]{:S(2)}) %collective-permute-start.18) | collective-permute-done | bytes 147488 | tf_op jit(solution)/shard_map/ppermute | solution.py:491
  63.9 2.4 %collective-permute-start.22 = (bf16[192,384]{1,0:T(8,128)(2,1)S(1)}, bf16[192,384]{1,0:T(8,128)(2,1)S(1)}, u32[]{:S(2)}, u32[]{:S(2)}) collective-permute-start(bf16[192,384]{1,0:T(8,128)(2,1)S(1)} %collective-permute-done.16.refs_0_.refs_3_), channel_id=1, source_target_pairs={{0,6},{1,7},{2,4},{3,5},{4,2},{5,3},{6,0},{7,1},{8,14},{9,15},{10,... | collective-permute-start | bytes 442376 | tf_op jit(solution)/shard_map/ppermute | solution.py:478
  66.3 2.3 %shard_map.56 = (bf16[2,768,384]{2,1,0:T(8,128)(2,1)}, bf16[768,768]{1,0:T(8,128)(2,1)S(1)}, bf16[2,768,384]{2,1,0:T(8,128)(2,1)S(1)}, bf16[768,768]{1,0:T(8,128)(2,1)S(1)}) custom-call(bf16[4,2,768,384]{3,2,1,0:T(8,128)(2,1)S(1)} %get-tuple-element.45.c.refs_1_, bf16[2,768,384]{2,1,0:T(8,128)(2,1)S(1)} %get-tuple-element.47.c01.refs_3_, ...), custom_call_target="tpu_custom_call" | custom-call | flops 1811939328 | bytes 11796480 | tf_op jit(solution)/shard_map/pallas_call | solution.py:167
  68.7 1.3 %collective-permute-done.22.refs_0_ = bf16[192,384]{1,0:T(8,128)(2,1)S(1)} collective-permute-done((bf16[192,384]{1,0:T(8,128)(2,1)S(1)}, bf16[192,384]{1,0:T(8,128)(2,1)S(1)}, u32[]{:S(2)}, u32[]{:S(2)}) %collective-permute-start.22) | collective-permute-done | bytes 147488 | tf_op jit(solution)/shard_map/ppermute | solution.py:478
  70.0 1.7 %collective-permute-done.23.refs_1_ = bf16[1408,128]{1,0:T(8,128)(2,1)S(1)} collective-permute-done((bf16[1408,128]{1,0:T(8,128)(2,1)S(1)}, bf16[1408,128]{1,0:T(8,128)(2,1)S(1)}, u32[]{:S(2)}, u32[]{:S(2)}) %collective-permute-start.23) | collective-permute-done | bytes 360480 | tf_op jit(solution)/shard_map/ppermute | solution.py:467
  71.7 1.6 %shard_map.59 = (bf16[352,128]{1,0:T(8,128)(2,1)S(1)}, bf16[768,768]{1,0:T(8,128)(2,1)S(1)}) custom-call(f32[768,384]{1,0:T(8,128)S(1)} %get-tuple-element.53.agg, bf16[768,384]{1,0:T(8,128)(2,1)S(1)} %get-tuple-element.56.agg_cols, bf16[768,768]{1,0:T(8,128)(2,1)S(1)} %get-tuple-element.60.agg_t, bf16[1408,128]{1,0:T(8,128)(2,1)S(1)} %collective-permute-done.15.refs_0_, ...), custom_call_target="tpu_custom_call" | custom-call | flops 905969664 | bytes 4939776 | tf_op jit(solution)/shard_map/pallas_call | solution.py:167
  73.3 1.3 %collective-permute-start.24 = (bf16[352,128]{1,0:T(8,128)(2,1)S(1)}, bf16[352,128]{1,0:T(8,128)(2,1)S(1)}, u32[]{:S(2)}, u32[]{:S(2)}) collective-permute-start(bf16[352,128]{1,0:T(8,128)(2,1)S(1)} %get-tuple-element.65), channel_id=1, source_target_pairs={{16,0},{18,2},{20,4},{22,6},{17,1},{19,3},{21,5},{23,7}} | collective-permute-start | bytes 270344 | tf_op jit(solution)/shard_map/ppermute | solution.py:491
  74.6 2.4 %collective-permute-start.31 = (bf16[192,384]{1,0:T(8,128)(2,1)S(1)}, bf16[192,384]{1,0:T(8,128)(2,1)S(1)}, u32[]{:S(2)}, u32[]{:S(2)}) collective-permute-start(bf16[192,384]{1,0:T(8,128)(2,1)S(1)} %shard_map.58.refs_3_), channel_id=1, source_target_pairs={{0,6},{1,7},{2,4},{3,5},{4,2},{5,3},{6,0},{7,1},{8,14},{9,15},{10,... | collective-permute-start | bytes 442376 | tf_op jit(solution)/shard_map/ppermute | solution.py:478
  78.0 2.8 %collective-permute-done.24.refs_0_ = bf16[352,128]{1,0:T(8,128)(2,1)S(1)} collective-permute-done((bf16[352,128]{1,0:T(8,128)(2,1)S(1)}, bf16[352,128]{1,0:T(8,128)(2,1)S(1)}, u32[]{:S(2)}, u32[]{:S(2)}) %collective-permute-start.24) | collective-permute-done | bytes 90144 | tf_op jit(solution)/shard_map/ppermute | solution.py:491
  81.9 2.5 %collective-permute-start.27 = (bf16[352,128]{1,0:T(8,128)(2,1)S(1)}, bf16[352,128]{1,0:T(8,128)(2,1)S(1)}, u32[]{:S(2)}, u32[]{:S(2)}) collective-permute-start(bf16[352,128]{1,0:T(8,128)(2,1)S(1)} %shard_map.60.refs_3_), channel_id=1, source_target_pairs={{0,6},{1,7},{2,4},{3,5},{4,2},{5,3},{6,0},{7,1},{8,14},{9,15},{10,... | collective-permute-start | bytes 270344 | tf_op jit(solution)/shard_map/ppermute | solution.py:478
  85.7 1.4 %shard_map.61.refs_0_ = f32[768,384]{1,0:T(8,128)S(1)} custom-call(f32[768,384]{1,0:T(8,128)S(1)} %shard_map.55.cov, bf16[2,768,384]{2,1,0:T(8,128)(2,1)S(1)} %get-tuple-element.69.mine.refs_0_, bf16[768,768]{1,0:T(8,128)(2,1)S(1)} %get-tuple-element.67.mine_t.refs_1_, bf16[768,768]{1,0:T(8,128)(2,1)S(1)} %get-tuple-element.68.right), custom_call_target="tpu_custom_call" | custom-call | flops 905969664 | bytes 5898240 | tf_op jit(solution)/shard_map/pallas_call | solution.py:167
  87.2 3.1 %collective-permute-done.27.refs_0_ = bf16[352,128]{1,0:T(8,128)(2,1)S(1)} collective-permute-done((bf16[352,128]{1,0:T(8,128)(2,1)S(1)}, bf16[352,128]{1,0:T(8,128)(2,1)S(1)}, u32[]{:S(2)}, u32[]{:S(2)}) %collective-permute-start.27) | collective-permute-done | bytes 90144 | tf_op jit(solution)/shard_map/ppermute | solution.py:478
  90.9 1.8 %shard_map.63 = (bf16[2,768,384]{2,1,0:T(8,128)(2,1)S(1)}, bf16[768,768]{1,0:T(8,128)(2,1)S(1)}) custom-call(bf16[2,768,384]{2,1,0:T(8,128)(2,1)S(1)} %get-tuple-element.69.mine.refs_0_, bf16[768,768]{1,0:T(8,128)(2,1)S(1)} %get-tuple-element.67.mine_t.refs_1_, bf16[768,384]{1,0:T(8,128)(2,1)S(1)} %shard_map.62.refs_2_, ...), custom_call_target="tpu_custom_call" | custom-call | flops 905969664 | bytes 5898240 | tf_op jit(solution)/shard_map/pallas_call | solution.py:167
  92.8 2.5 %shard_map.65 = f32[1,768,384]{2,1,0:T(8,128)} custom-call(f32[768,384]{1,0:T(8,128)S(1)} %shard_map.61.refs_0_, bf16[2,768,384]{2,1,0:T(8,128)(2,1)S(1)} %get-tuple-element.72.refs_1_.refs_0_, bf16[768,768]{1,0:T(8,128)(2,1)S(1)} %get-tuple-element.71.refs_2_, bf16[1408,128]{1,0:T(8,128)(2,1)S(1)} %shard_map.64.refs_3_, ...), custom_call_target="tpu_custom_call" | custom-call | flops 905969664 | bytes 5439488 | tf_op jit(solution)/shard_map/pallas_call | solution.py:167
  95.4 1.7 %shard_map.67 = bf16[1,768,384]{2,1,0:T(8,128)(2,1)} custom-call(bf16[2,768,384]{2,1,0:T(8,128)(2,1)S(1)} %get-tuple-element.72.refs_1_.refs_0_, bf16[768,384]{1,0:T(8,128)(2,1)S(1)} %shard_map.66.refs_1_, bf16[768,384]{1,0:T(8,128)(2,1)S(1)} %collective-permute-done.34.refs_2_), custom_call_target="tpu_custom_call" | custom-call | flops 452984832 | bytes 2949120 | tf_op jit(solution)/shard_map/pallas_call | solution.py:167
  (62 shorter events, 12.5 us)
Async XLA Ops:
  2.1 16.7 %collective-permute-start.2 = (bf16[768,384]{1,0:T(8,128)(2,1)S(1)}, bf16[768,384]{1,0:T(8,128)(2,1)S(1)}, u32[]{:S(2)}, u32[]{:S(2)}) collective-permute-start(bf16[768,384]{1,0:T(8,128)(2,1)S(1)} %convert_bitcast_fusion.refs_4_.refs_0_), channel_id=1, source_target_pairs={{0,4},{1,3},{2,6},{3,1},{4,0},{5,7},{6,2},{7,5},{8,12},{9,11},{10,... | collective-permute-start | bytes 1769480 | tf_op jit(solution)/shard_map/ppermute | solution.py:478
  5.2 13.7 %collective-permute-start.4 = (bf16[768,384]{1,0:T(8,128)(2,1)S(1)}, bf16[768,384]{1,0:T(8,128)(2,1)S(1)}, u32[]{:S(2)}, u32[]{:S(2)}) collective-permute-start(bf16[768,384]{1,0:T(8,128)(2,1)S(1)} %convert_bitcast_fusion.refs_4_.refs_0_), channel_id=1, source_target_pairs={{0,2},{1,5},{2,0},{3,7},{4,6},{5,1},{6,4},{7,3},{8,10},{9,13},{10,... | collective-permute-start | bytes 1769480 | tf_op jit(solution)/shard_map/ppermute | solution.py:478
  6.7 14.1 %collective-permute-start = (bf16[768,384]{1,0:T(8,128)(2,1)S(1)}, bf16[768,384]{1,0:T(8,128)(2,1)S(1)}, u32[]{:S(2)}, u32[]{:S(2)}) collective-permute-start(bf16[768,384]{1,0:T(8,128)(2,1)S(1)} %convert_element_type.10.refs_2_), channel_id=1, source_target_pairs={{1,0},{0,1},{3,2},{2,3},{5,4},{4,5},{7,6},{6,7},{9,8},{8,9},{11,10... | collective-permute-start | bytes 1769480 | tf_op jit(solution)/shard_map/ppermute | solution.py:467
  6.8 14.0 %collective-permute-start.1 = (bf16[768,384]{1,0:T(8,128)(2,1)S(1)}, bf16[768,384]{1,0:T(8,128)(2,1)S(1)}, u32[]{:S(2)}, u32[]{:S(2)}) collective-permute-start(bf16[768,384]{1,0:T(8,128)(2,1)S(1)} %convert_bitcast_fusion.refs_4_.refs_0_), channel_id=1, source_target_pairs={{1,0},{0,1},{3,2},{2,3},{5,4},{4,5},{7,6},{6,7},{9,8},{8,9},{11,10... | collective-permute-start | bytes 1769480 | tf_op jit(solution)/shard_map/ppermute | solution.py:467
  18.8 5.5 %collective-permute-start.3 = (bf16[768,384]{1,0:T(8,128)(2,1)S(1)}, bf16[768,384]{1,0:T(8,128)(2,1)S(1)}, u32[]{:S(2)}, u32[]{:S(2)}) collective-permute-start(bf16[768,384]{1,0:T(8,128)(2,1)S(1)} %collective-permute-done.2.refs_2_), channel_id=1, source_target_pairs={{1,0},{0,1},{3,2},{2,3},{5,4},{4,5},{7,6},{6,7},{9,8},{8,9},{11,10... | collective-permute-start | bytes 1769480 | tf_op jit(solution)/shard_map/ppermute | solution.py:467
  18.8 5.5 %collective-permute-start.5 = (bf16[768,384]{1,0:T(8,128)(2,1)S(1)}, bf16[768,384]{1,0:T(8,128)(2,1)S(1)}, u32[]{:S(2)}, u32[]{:S(2)}) collective-permute-start(bf16[768,384]{1,0:T(8,128)(2,1)S(1)} %collective-permute-done.4.refs_4_), channel_id=1, source_target_pairs={{1,0},{0,1},{3,2},{2,3},{5,4},{4,5},{7,6},{6,7},{9,8},{8,9},{11,10... | collective-permute-start | bytes 1769480 | tf_op jit(solution)/shard_map/ppermute | solution.py:467
  19.3 13.5 %collective-permute-start.6 = (bf16[768,384]{1,0:T(8,128)(2,1)S(1)}, bf16[768,384]{1,0:T(8,128)(2,1)S(1)}, u32[]{:S(2)}, u32[]{:S(2)}) collective-permute-start(bf16[768,384]{1,0:T(8,128)(2,1)S(1)} %collective-permute-done.2.refs_2_), channel_id=1, source_target_pairs={{0,2},{1,5},{2,0},{3,7},{4,6},{5,1},{6,4},{7,3},{8,10},{9,13},{10,... | collective-permute-start | bytes 1769480 | tf_op jit(solution)/shard_map/ppermute | solution.py:478
  22.6 10.3 %collective-permute-start.7 = (bf16[1408,128]{1,0:T(8,128)(2,1)S(1)}, bf16[1408,128]{1,0:T(8,128)(2,1)S(1)}, u32[]{:S(2)}, u32[]{:S(2)}) collective-permute-start(bf16[1408,128]{1,0:T(8,128)(2,1)S(1)} %get-tuple-element.43.refs_5_), channel_id=1, source_target_pairs={{0,4},{1,3},{2,6},{3,1},{4,0},{5,7},{6,2},{7,5},{8,12},{9,11},{10,... | collective-permute-start | bytes 1081352 | tf_op jit(solution)/shard_map/ppermute | solution.py:478
  32.9 3.0 %collective-permute-start.8 = (bf16[768,384]{1,0:T(8,128)(2,1)S(1)}, bf16[768,384]{1,0:T(8,128)(2,1)S(1)}, u32[]{:S(2)}, u32[]{:S(2)}) collective-permute-start(bf16[768,384]{1,0:T(8,128)(2,1)S(1)} %collective-permute-done.6.refs_2_), channel_id=1, source_target_pairs={{1,0},{0,1},{3,2},{2,3},{5,4},{4,5},{7,6},{6,7},{9,8},{8,9},{11,10... | collective-permute-start | bytes 1769480 | tf_op jit(solution)/shard_map/ppermute | solution.py:467
  33.0 7.4 %collective-permute-start.11 = (bf16[1408,128]{1,0:T(8,128)(2,1)S(1)}, bf16[1408,128]{1,0:T(8,128)(2,1)S(1)}, u32[]{:S(2)}, u32[]{:S(2)}) collective-permute-start(bf16[1408,128]{1,0:T(8,128)(2,1)S(1)} %get-tuple-element.43.refs_5_), channel_id=1, source_target_pairs={{0,2},{1,5},{2,0},{3,7},{4,6},{5,1},{6,4},{7,3},{8,10},{9,13},{10,... | collective-permute-start | bytes 1081352 | tf_op jit(solution)/shard_map/ppermute | solution.py:478
  34.6 9.7 %collective-permute-start.13 = (bf16[1408,128]{1,0:T(8,128)(2,1)S(1)}, bf16[1408,128]{1,0:T(8,128)(2,1)S(1)}, u32[]{:S(2)}, u32[]{:S(2)}) collective-permute-start(bf16[1408,128]{1,0:T(8,128)(2,1)S(1)} %collective-permute-done.7.refs_7_), channel_id=1, source_target_pairs={{0,2},{1,5},{2,0},{3,7},{4,6},{5,1},{6,4},{7,3},{8,10},{9,13},{10,... | collective-permute-start | bytes 1081352 | tf_op jit(solution)/shard_map/ppermute | solution.py:478
  35.0 10.9 %collective-permute-start.9 = (bf16[1408,128]{1,0:T(8,128)(2,1)S(1)}, bf16[1408,128]{1,0:T(8,128)(2,1)S(1)}, u32[]{:S(2)}, u32[]{:S(2)}) collective-permute-start(bf16[1408,128]{1,0:T(8,128)(2,1)S(1)} %get-tuple-element.43.refs_5_), channel_id=1, source_target_pairs={{1,0},{0,1},{3,2},{2,3},{5,4},{4,5},{7,6},{6,7},{9,8},{8,9},{11,10... | collective-permute-start | bytes 1081352 | tf_op jit(solution)/shard_map/ppermute | solution.py:467
  35.8 10.1 %collective-permute-start.10 = (bf16[1408,128]{1,0:T(8,128)(2,1)S(1)}, bf16[1408,128]{1,0:T(8,128)(2,1)S(1)}, u32[]{:S(2)}, u32[]{:S(2)}) collective-permute-start(bf16[1408,128]{1,0:T(8,128)(2,1)S(1)} %collective-permute-done.7.refs_7_), channel_id=1, source_target_pairs={{1,0},{0,1},{3,2},{2,3},{5,4},{4,5},{7,6},{6,7},{9,8},{8,9},{11,10... | collective-permute-start | bytes 1081352 | tf_op jit(solution)/shard_map/ppermute | solution.py:467
  40.4 5.6 %collective-permute-start.12 = (bf16[1408,128]{1,0:T(8,128)(2,1)S(1)}, bf16[1408,128]{1,0:T(8,128)(2,1)S(1)}, u32[]{:S(2)}, u32[]{:S(2)}) collective-permute-start(bf16[1408,128]{1,0:T(8,128)(2,1)S(1)} %collective-permute-done.11.refs_9_), channel_id=1, source_target_pairs={{1,0},{0,1},{3,2},{2,3},{5,4},{4,5},{7,6},{6,7},{9,8},{8,9},{11,10... | collective-permute-start | bytes 1081352 | tf_op jit(solution)/shard_map/ppermute | solution.py:467
  44.5 8.2 %collective-permute-start.16 = (bf16[192,384]{1,0:T(8,128)(2,1)S(1)}, bf16[192,384]{1,0:T(8,128)(2,1)S(1)}, u32[]{:S(2)}, u32[]{:S(2)}) collective-permute-start(bf16[192,384]{1,0:T(8,128)(2,1)S(1)} %get-tuple-element.50), channel_id=1, source_target_pairs={{8,0},{10,2},{12,4},{14,6},{24,16},{26,18},{28,20},{30,22},{9,1},{... | collective-permute-start | bytes 442376 | tf_op jit(solution)/shard_map/ppermute | solution.py:491
  52.7 17.3 %collective-permute-start.15 = (bf16[1408,128]{1,0:T(8,128)(2,1)S(1)}, bf16[1408,128]{1,0:T(8,128)(2,1)S(1)}, u32[]{:S(2)}, u32[]{:S(2)}) collective-permute-start(bf16[1408,128]{1,0:T(8,128)(2,1)S(1)} %get-tuple-element.58), channel_id=1, source_target_pairs={{8,0},{10,2},{12,4},{14,6},{24,16},{26,18},{28,20},{30,22},{9,1},{... | collective-permute-start | bytes 1081352 | tf_op jit(solution)/shard_map/ppermute | solution.py:491
  54.4 9.5 %collective-permute-start.18 = (bf16[192,384]{1,0:T(8,128)(2,1)S(1)}, bf16[192,384]{1,0:T(8,128)(2,1)S(1)}, u32[]{:S(2)}, u32[]{:S(2)}) collective-permute-start(bf16[192,384]{1,0:T(8,128)(2,1)S(1)} %shard_map.57), channel_id=1, source_target_pairs={{16,0},{18,2},{20,4},{22,6},{17,1},{19,3},{21,5},{23,7}} | collective-permute-start | bytes 442376 | tf_op jit(solution)/shard_map/ppermute | solution.py:491
  55.8 12.8 %collective-permute-start.19 = (bf16[192,384]{1,0:T(8,128)(2,1)S(1)}, bf16[192,384]{1,0:T(8,128)(2,1)S(1)}, u32[]{:S(2)}, u32[]{:S(2)}) collective-permute-start(bf16[192,384]{1,0:T(8,128)(2,1)S(1)} %shard_map.57), channel_id=1, source_target_pairs={{16,8},{18,10},{20,12},{22,14},{17,9},{19,11},{21,13},{23,15}} | collective-permute-start | bytes 442376 | tf_op jit(solution)/shard_map/ppermute | solution.py:491
  56.5 12.2 %collective-permute-start.20 = (bf16[192,384]{1,0:T(8,128)(2,1)S(1)}, bf16[192,384]{1,0:T(8,128)(2,1)S(1)}, u32[]{:S(2)}, u32[]{:S(2)}) collective-permute-start(bf16[192,384]{1,0:T(8,128)(2,1)S(1)} %collective-permute-done.16.refs_0_.refs_3_), channel_id=1, source_target_pairs={{0,2},{1,3},{2,0},{3,1},{4,6},{5,7},{6,4},{7,5},{8,10},{9,11},{10,... | collective-permute-start | bytes 442376 | tf_op jit(solution)/shard_map/ppermute | solution.py:478
  59.2 9.5 %collective-permute-start.21 = (bf16[192,384]{1,0:T(8,128)(2,1)S(1)}, bf16[192,384]{1,0:T(8,128)(2,1)S(1)}, u32[]{:S(2)}, u32[]{:S(2)}) collective-permute-start(bf16[192,384]{1,0:T(8,128)(2,1)S(1)} %collective-permute-done.16.refs_0_.refs_3_), channel_id=1, source_target_pairs={{0,4},{1,5},{2,6},{3,7},{4,0},{5,1},{6,2},{7,3},{8,12},{9,13},{10,... | collective-permute-start | bytes 442376 | tf_op jit(solution)/shard_map/ppermute | solution.py:478
  63.9 6.1 %collective-permute-start.22 = (bf16[192,384]{1,0:T(8,128)(2,1)S(1)}, bf16[192,384]{1,0:T(8,128)(2,1)S(1)}, u32[]{:S(2)}, u32[]{:S(2)}) collective-permute-start(bf16[192,384]{1,0:T(8,128)(2,1)S(1)} %collective-permute-done.16.refs_0_.refs_3_), channel_id=1, source_target_pairs={{0,6},{1,7},{2,4},{3,5},{4,2},{5,3},{6,0},{7,1},{8,14},{9,15},{10,... | collective-permute-start | bytes 442376 | tf_op jit(solution)/shard_map/ppermute | solution.py:478
  73.3 7.5 %collective-permute-start.24 = (bf16[352,128]{1,0:T(8,128)(2,1)S(1)}, bf16[352,128]{1,0:T(8,128)(2,1)S(1)}, u32[]{:S(2)}, u32[]{:S(2)}) collective-permute-start(bf16[352,128]{1,0:T(8,128)(2,1)S(1)} %get-tuple-element.65), channel_id=1, source_target_pairs={{16,0},{18,2},{20,4},{22,6},{17,1},{19,3},{21,5},{23,7}} | collective-permute-start | bytes 270344 | tf_op jit(solution)/shard_map/ppermute | solution.py:491
  74.6 9.8 %collective-permute-start.31 = (bf16[192,384]{1,0:T(8,128)(2,1)S(1)}, bf16[192,384]{1,0:T(8,128)(2,1)S(1)}, u32[]{:S(2)}, u32[]{:S(2)}) collective-permute-start(bf16[192,384]{1,0:T(8,128)(2,1)S(1)} %shard_map.58.refs_3_), channel_id=1, source_target_pairs={{0,6},{1,7},{2,4},{3,5},{4,2},{5,3},{6,0},{7,1},{8,14},{9,15},{10,... | collective-permute-start | bytes 442376 | tf_op jit(solution)/shard_map/ppermute | solution.py:478
  77.0 7.6 %collective-permute-start.32 = (bf16[192,384]{1,0:T(8,128)(2,1)S(1)}, bf16[192,384]{1,0:T(8,128)(2,1)S(1)}, u32[]{:S(2)}, u32[]{:S(2)}) collective-permute-start(bf16[192,384]{1,0:T(8,128)(2,1)S(1)} %shard_map.58.refs_3_), channel_id=1, source_target_pairs={{0,4},{1,5},{2,6},{3,7},{4,0},{5,1},{6,2},{7,3},{8,12},{9,13},{10,... | collective-permute-start | bytes 442376 | tf_op jit(solution)/shard_map/ppermute | solution.py:478
  77.2 4.7 %collective-permute-start.25 = (bf16[352,128]{1,0:T(8,128)(2,1)S(1)}, bf16[352,128]{1,0:T(8,128)(2,1)S(1)}, u32[]{:S(2)}, u32[]{:S(2)}) collective-permute-start(bf16[352,128]{1,0:T(8,128)(2,1)S(1)} %get-tuple-element.65), channel_id=1, source_target_pairs={{16,8},{18,10},{20,12},{22,14},{17,9},{19,11},{21,13},{23,15}} | collective-permute-start | bytes 270344 | tf_op jit(solution)/shard_map/ppermute | solution.py:491
  77.9 13.0 %collective-permute-start.26 = (bf16[768,384]{1,0:T(8,128)(2,1)S(1)}, bf16[768,384]{1,0:T(8,128)(2,1)S(1)}, u32[]{:S(2)}, u32[]{:S(2)}) collective-permute-start(bf16[768,384]{1,0:T(8,128)(2,1)S(1)} %shard_map.62.refs_2_), channel_id=1, source_target_pairs={{1,0},{0,1},{3,2},{2,3},{5,4},{4,5},{7,6},{6,7},{9,8},{8,9},{11,10... | collective-permute-start | bytes 1769480 | tf_op jit(solution)/shard_map/ppermute | solution.py:467
  80.8 6.3 %collective-permute-start.33 = (bf16[192,384]{1,0:T(8,128)(2,1)S(1)}, bf16[192,384]{1,0:T(8,128)(2,1)S(1)}, u32[]{:S(2)}, u32[]{:S(2)}) collective-permute-start(bf16[192,384]{1,0:T(8,128)(2,1)S(1)} %shard_map.58.refs_3_), channel_id=1, source_target_pairs={{0,2},{1,3},{2,0},{3,1},{4,6},{5,7},{6,4},{7,5},{8,10},{9,11},{10,... | collective-permute-start | bytes 442376 | tf_op jit(solution)/shard_map/ppermute | solution.py:478
  81.9 8.4 %collective-permute-start.27 = (bf16[352,128]{1,0:T(8,128)(2,1)S(1)}, bf16[352,128]{1,0:T(8,128)(2,1)S(1)}, u32[]{:S(2)}, u32[]{:S(2)}) collective-permute-start(bf16[352,128]{1,0:T(8,128)(2,1)S(1)} %shard_map.60.refs_3_), channel_id=1, source_target_pairs={{0,6},{1,7},{2,4},{3,5},{4,2},{5,3},{6,0},{7,1},{8,14},{9,15},{10,... | collective-permute-start | bytes 270344 | tf_op jit(solution)/shard_map/ppermute | solution.py:478
  84.4 5.9 %collective-permute-start.28 = (bf16[352,128]{1,0:T(8,128)(2,1)S(1)}, bf16[352,128]{1,0:T(8,128)(2,1)S(1)}, u32[]{:S(2)}, u32[]{:S(2)}) collective-permute-start(bf16[352,128]{1,0:T(8,128)(2,1)S(1)} %shard_map.60.refs_3_), channel_id=1, source_target_pairs={{0,4},{1,5},{2,6},{3,7},{4,0},{5,1},{6,2},{7,3},{8,12},{9,13},{10,... | collective-permute-start | bytes 270344 | tf_op jit(solution)/shard_map/ppermute | solution.py:478
  84.7 5.7 %collective-permute-start.29 = (bf16[352,128]{1,0:T(8,128)(2,1)S(1)}, bf16[352,128]{1,0:T(8,128)(2,1)S(1)}, u32[]{:S(2)}, u32[]{:S(2)}) collective-permute-start(bf16[352,128]{1,0:T(8,128)(2,1)S(1)} %shard_map.60.refs_3_), channel_id=1, source_target_pairs={{0,2},{1,3},{2,0},{3,1},{4,6},{5,7},{6,4},{7,5},{8,10},{9,11},{10,... | collective-permute-start | bytes 270344 | tf_op jit(solution)/shard_map/ppermute | solution.py:478
  90.3 5.0 %collective-permute-start.34 = (bf16[768,384]{1,0:T(8,128)(2,1)S(1)}, bf16[768,384]{1,0:T(8,128)(2,1)S(1)}, u32[]{:S(2)}, u32[]{:S(2)}) collective-permute-start(bf16[768,384]{1,0:T(8,128)(2,1)S(1)} %shard_map.66.refs_1_), channel_id=1, source_target_pairs={{1,0},{0,1},{3,2},{2,3},{5,4},{4,5},{7,6},{6,7},{9,8},{8,9},{11,10... | collective-permute-start | bytes 1769480 | tf_op jit(solution)/shard_map/ppermute | solution.py:467
  90.4 2.5 %collective-permute-start.30 = (bf16[1408,128]{1,0:T(8,128)(2,1)S(1)}, bf16[1408,128]{1,0:T(8,128)(2,1)S(1)}, u32[]{:S(2)}, u32[]{:S(2)}) collective-permute-start(bf16[1408,128]{1,0:T(8,128)(2,1)S(1)} %shard_map.64.refs_3_), channel_id=1, source_target_pairs={{1,0},{0,1},{3,2},{2,3},{5,4},{4,5},{7,6},{6,7},{9,8},{8,9},{11,10... | collective-permute-start | bytes 1081352 | tf_op jit(solution)/shard_map/ppermute | solution.py:467
  (5 other events, 31.0 us)
